TPU v7x, 256 devices: a whole 4x4x8 slice. The times are simulated.
256 devices in a mesh: row: 16 (over z, y_lo), col: 16 (over y_hi, x, core).
Axes of the slice: x: 4, y: 4 (y_hi: 2, y_lo: 2; y = y_hi * 2 + y_lo), z: 8, core: 2. Of those that a mesh axis runs over, the one named last changes fastest.
Arguments:
- factors: bfloat16 [768, 12, 5120], P('row', None, 'col'), may hold values from -0.21875 to 0.21875
- amplitudes: bfloat16 [16, 12, 12], replicated, may hold values from -6 to 6
- vir_energy: float32 [768], replicated, may hold values from 0.2 to 2
- pair_energy: float32 [16], replicated, may hold values from -1.5 to -0.5
Outputs:
- residual: float32 [16, 768, 768], P('col', 'row')
- update: float32 [16, 768, 768], P('col', 'row')
All inputs are finite; a program needn't handle non-finite values.
Results may differ from a plain program's by a relative error of at most 0.0024.
Values may be sent and summed in bfloat16 or wider, within the bound.
No kernel may reach another device: no remote copies, remote signals or barrier semaphores. Data moves between devices by JAX's collectives and lax.ppermute only.
A program may use at most 256 MiB of HBM per device.

v0:
```python
import jax
import jax.numpy as jnp
from jax import lax
from jax.sharding import PartitionSpec as P


def block_terms(left_side, shard_piece, row_count):
    piece_rows = shard_piece.shape[0]
    slab_size = shard_piece.shape[1]
    products = lax.dot_general(
        left_side,
        shard_piece.reshape(piece_rows * slab_size, -1),
        (((1,), (1,)), ((), ())),
        preferred_element_type=jnp.float32,
    )
    return products.astype(jnp.bfloat16).reshape(row_count, slab_size, piece_rows, slab_size)


def own_term(products, amplitudes):
    return jnp.einsum("acbd,pcd->pab", products, amplitudes, preferred_element_type=jnp.float32)


def mirror_term(products, amplitudes):
    return jnp.einsum("bdac,pcd->pab", products, amplitudes, preferred_element_type=jnp.float32)


def per_device(factors, amplitudes, vir_energy, pair_energy):
    row_count, slab_size, aux_count = factors.shape
    pair_count = amplitudes.shape[0]
    vir_total = vir_energy.shape[0]
    row_devices = lax.axis_size("row")
    here_row = lax.axis_index("row")
    here_col = lax.axis_index("col")
    left_side = factors.reshape(row_count * slab_size, aux_count)
    partial_rows = jnp.zeros((pair_count, row_count, vir_total), jnp.float32)
    outgoing = jnp.zeros((pair_count, row_count, row_devices, row_count), jnp.float32)
    gathered = lax.all_gather(factors, "row", axis=0, tiled=True)

    def visit_lower(other_row, state_tuple):
        partial_sum, sending = state_tuple
        current = lax.dynamic_slice_in_dim(gathered, other_row * row_count, row_count, 0)
        products = block_terms(left_side, current, row_count)
        own_block = own_term(products, amplitudes)
        partial_sum = lax.dynamic_update_slice_in_dim(
            partial_sum, own_block, other_row * row_count, 2
        )
        mirror = mirror_term(products, amplitudes) * jnp.where(
            other_row < here_row, 1.0, 0.0
        ).astype(jnp.float32)
        sending = lax.dynamic_update_slice_in_dim(sending, mirror[:, :, None, :], other_row, 2)
        return (partial_sum, sending)

    partial_rows, outgoing = lax.fori_loop(0, here_row + 1, visit_lower, (partial_rows, outgoing))
    received = lax.all_to_all(outgoing, "row", split_axis=2, concat_axis=2, tiled=True)
    row_sum = partial_rows + received.reshape(pair_count, row_count, vir_total)
    reduced = lax.psum_scatter(row_sum, "col", scatter_dimension=0, tiled=True)
    pair_share = reduced.shape[0]
    first_energy = lax.dynamic_slice_in_dim(vir_energy, here_row * row_count, row_count)
    pair_here = lax.dynamic_slice_in_dim(pair_energy, here_col * pair_share, pair_share)
    divisor = first_energy[None, :, None] + vir_energy[None, None, :] - pair_here[:, None, None]
    return (reduced, reduced / divisor)


def solution(mesh):
    return jax.shard_map(
        per_device,
        mesh=mesh,
        in_specs=(P("row", None, "col"), P(), P(), P()),
        out_specs=(P("col", "row", None), P("col", "row", None)),
        check_vma=False,
    )
```

profile of v0, /device:TPU:1, one launch (start us, length us, event | category | flops | bytes accessed | tf_op | source)
XLA Modules:
  0.0 852.8 jit_solution(11890622636218101873)
XLA Ops:
  7.2 0.7 all-gather.2.cloned.1.call-update
  7.9 1.1 copy.23
  9.3 1.0 copy.25
  10.3 159.5 %all-gather.2.cloned.1.call-done = bf16[768,12,320]{2,0,1:T(8,128)(2,1)} async-done(((bf16[48,12,320]{2,0,1:T(8,128)(2,1)}), bf16[768,12,320]{2,0,1:T(8,128)(2,1)}) %all-gather.2.cloned.1.call-update) | async-done | bytes 5898256 | tf_op jit(solution)/shard_map/all_gather | solution.py:37
  169.8 1.7 broadcast_in_dim.12.clone
  171.5 3.2 broadcast_in_dim.13
  174.7 29.7 %while.12 = (s32[]{:T(128)}, f32[16,48,768]{2,1,0:T(8,128)}, f32[16,48,16,48]{1,0,3,2:T(8,128)}, s32[]{:T(128)}, bf16[768,12,320]{2,0,1:T(8,128)(2,1)}, /*index=...) while((s32[]{:T(128)}, f32[16,48,768]{2,1,0:T(8,128)}, ...), condition=%wide.region_1.2_spmd, body=%wide.region_0.1_spmd.sunk | while | flops 233938944 | bytes 15157515 | solution.py:53
  174.7 1.1 constant_dynamic-slice_fusion.2
  176.1 0.6 fusion.24
  176.8 0.4 copy.41
  177.1 9.7 %reshape.82 = bf16[48,12,48,12]{3,2,1,0:T(8,128)(2,1)} reshape(bf16[576,576]{1,0:T(8,128)(2,1)S(1)} %copy.41) | data formatting | bytes 1327104 | tf_op jit(solution)/shard_map/while/body/reshape | solution.py:16
  187.0 6.4 convolution_bitcast_fusion.3
  193.7 3.6 dynamic_update_slice.10
  197.3 7.2 fusion.25
  204.5 8.6 %reshape.77 = f32[16,1,36864]{2,1,0:T(1,128)} reshape(f32[16,48,16,48]{3,2,1,0:T(8,128)} %bitcast.56) | data formatting | bytes 4718592
  213.1 529.4 %all_to_all.5 = f32[16,1,36864]{2,1,0:T(1,128)S(1)} all-to-all(f32[16,1,36864]{2,1,0:T(1,128)} %reshape.77), channel_id=1, replica_groups=mesh['row'=16,'col'=16] {'row'}, dimensions={0} | all-to-all | bytes 4718592 | tf_op jit(solution)/shard_map/all_to_all | solution.py:54
  742.5 0.5 broadcast.53
  743.0 8.4 reduce
  751.4 5.6 reshape.78
  757.0 6.6 copy.32
  763.6 3.4 add.46
  767.0 0.6 dynamic_slice.10
  767.7 75.9 %reduce-scatter.2.cloned.1.call-done = f32[1,48,768]{2,1,0:T(8,128)} async-done(((f32[16,48,768]{2,1,0:T(8,128)}), f32[1,48,768]{2,1,0:T(8,128)}) %reduce-scatter.2.cloned.1.call-update) | async-done | bytes 147472 | tf_op jit(solution)/shard_map/reduce_scatter | solution.py:56
  843.6 2.3 subtract_divide_fusion
  (15 shorter events, 1.1 us)
Async XLA Ops:
  7.2 162.7 %all-gather.2.cloned.1.call-start = ((), (), s32[]{:S(2)}) async-start(), calls=%async_computation.2 | async-start | bytes 7520256 | tf_op jit(solution)/shard_map/all_gather | solution.py:37
  7.9 835.7 %reduce-scatter.2.cloned.1.call-start = ((), (), s32[]{:S(2)}) async-start(), calls=%async_computation.3 | async-start | bytes 2506752 | tf_op jit(solution)/shard_map/reduce_scatter | solution.py:56
  757.0 6.6 copy-start
  763.6 3.4 copy-start.2
  763.6 4.0 copy-start.1
Sparse Core Ops, SparseCore 0:
  9.8 159.9 all-gather.1
  767.1 76.4 reduce-scatter.1
where the time goes:
time: 857 us; the launch traced here: 853 us
  blocking collectives  529 us (62%)
  waiting for transfers between devices  236 us (28%)
  local copies, waits for them, and re-layouts  44.6 us (5%)
  matrix products  14.3 us (2%)
  other arithmetic  14.1 us (2%)
  between operations  14.1 us (2%)
    all_to_all x1, blocking collectives, per_device(): lax.all_to_all(outgoing, 'row', split_axis=2, concat_axis=2, tiled=True)  529 us
    all_gather x1, waiting for transfers between devices, per_device(): gathered = lax.all_gather(factors, 'row', axis=0, tiled=True)  160 us
    reduce_scatter x1, waiting for transfers between devices, per_device(): reduced = lax.psum_scatter(row_sum, 'col', scatter_dimension=0, tiled=True)  75.9 us
  transfers between devices with their start and end apart: 2, of which 2 were waited for; matrix products, arithmetic and copies ran while one was open for 0% of the time, Pallas kernels for 0%

commit v1 on v0

v1 whole, which is shorter than its diff:
```python
import jax
import jax.numpy as jnp
import numpy as np
from jax import lax
from jax.experimental import pallas as pl
from jax.experimental.pallas import tpu as pltpu
from jax.sharding import PartitionSpec as P

ROWS = 48
SLAB = 12
PAIRS = 16
LANE = 128
WIDE = 256
TILES = 30
GROUP = 8
GROUPS = ROWS // GROUP
DEPTH = SLAB * SLAB * GROUP
OUT = 3 * LANE
BF16 = jnp.bfloat16
F32 = jnp.float32


def device_of(index):
    row, col = divmod(index, 16)
    return row // 2, row % 2, col // 8, (col // 2) % 4, col % 2


def index_of(z, y_lo, y_hi, x, core):
    return ((z % 8) * 2 + y_lo % 2) * 16 + (y_hi % 2) * 8 + (x % 4) * 2 + core % 2


def shift(array, dz=0, dy=0, dh=0, dx=0, dc=0):
    pairs = []
    for source in range(256):
        z, y, h, x, c = device_of(source)
        pairs.append((source, index_of(z + dz, y + dy, h + dh, x + dx, c + dc)))
    return lax.ppermute(array, ("row", "col"), pairs)


def full(count):
    return [pl.BlockSpec(memory_space=pltpu.VMEM)] * count


def params():
    return pltpu.CompilerParams(vmem_limit_bytes=40 * 1024 * 1024)


def pack_block(factors):
    main = factors[:, :, :WIDE].reshape(ROWS, 2 * SLAB, LANE).transpose(1, 0, 2)
    rest = factors[:, :, WIDE:].reshape(ROWS, 2, SLAB // 2, LANE // 2)
    rest = rest.transpose(2, 0, 1, 3).reshape(SLAB // 2, ROWS, LANE)
    return jnp.concatenate([main, rest], axis=0)


def star_kernel(center, m1, own, p1, m2, p2, weights, keep, send, left, products):
    low = lax.broadcasted_iota(jnp.int32, (ROWS, LANE), 1) < LANE // 2
    zero = jnp.zeros((ROWS, LANE), F32)
    for c in range(SLAB):
        rows = pl.ds(c * ROWS, ROWS)
        last = center[2 * SLAB + c % 6].astype(F32)
        moved = pltpu.roll(last, LANE // 2, 1)
        in_low, in_high = (last, moved) if c < 6 else (moved, last)
        for half in range(2):
            left[half, rows, 0:LANE] = center[2 * c]
            left[half, rows, LANE:2 * LANE] = center[2 * c + 1]
        left[0, rows, 2 * LANE:] = jnp.where(low, in_low, zero).astype(BF16)
        left[1, rows, 2 * LANE:] = jnp.where(low, zero, in_high).astype(BF16)
    for d in range(SLAB):
        columns = []
        for tile in (2 * d, 2 * d + 1, 2 * SLAB + d % 6):
            columns.append(jnp.concatenate(
                [m1[tile], own[tile], p1[tile], m2[tile], p2[tile], p1[tile, 32:, :]], axis=0))
        right = jnp.concatenate(columns, axis=1)
        block = lax.dot_general(left[d // 6], right, (((1,), (1,)), ((), ())), preferred_element_type=F32)
        block = block.reshape(SLAB, GROUPS, GROUP, WIDE)
        for g in range(GROUPS):
            part = block[:, g].reshape(SLAB * GROUP, WIDE)
            products[g, d * SLAB * GROUP:(d + 1) * SLAB * GROUP, :] = part.astype(BF16)
    first = lax.broadcasted_iota(jnp.int32, (PAIRS * GROUP, LANE), 1) < 5 * ROWS - LANE
    half_pairs = PAIRS // 2
    for g in range(GROUPS):
        terms = jnp.dot(weights[...], products[g], preferred_element_type=F32)
        plain, mirror = terms[:PAIRS * GROUP], terms[PAIRS * GROUP:]
        middle = jnp.where(first, plain[:, LANE:], mirror[:, LANE:])
        rows = pl.ds(g * GROUP, GROUP)
        for at, value in enumerate((plain[:, :LANE], middle, mirror[:, :LANE])):
            value = value.reshape(PAIRS, GROUP, LANE)
            lanes = pl.ds(at * LANE, LANE)
            keep[:, rows, lanes] = value[:half_pairs]
            send[:, rows, lanes] = value[half_pairs:]


def star(center, others, weights):
    half = jax.ShapeDtypeStruct((PAIRS // 2, ROWS, OUT), F32)
    return pl.pallas_call(
        star_kernel,
        out_shape=(half, half),
        in_specs=full(7),
        out_specs=tuple(full(2)),
        scratch_shapes=[
            pltpu.VMEM((2, SLAB * ROWS, 3 * LANE), BF16),
            pltpu.VMEM((GROUPS, DEPTH, WIDE), BF16),
        ],
        compiler_params=params(),
        cost_estimate=pl.CostEstimate(flops=3_500_000_000, bytes_accessed=4_000_000, transcendentals=0),
        name="star",
    )(center, *others, weights)


def core_kernel(keep, got, stay, one, two, three):
    stay[...] = keep[0:2] + got[0:2]
    one[...] = (keep[2:4] + got[2:4]).astype(BF16)
    two[...] = (keep[4:6] + got[4:6]).astype(BF16)
    three[...] = (keep[6:8] + got[6:8]).astype(BF16)


def add_cores(keep, got):
    part = jax.ShapeDtypeStruct((2, ROWS, OUT), BF16)
    return pl.pallas_call(
        core_kernel,
        out_shape=(jax.ShapeDtypeStruct((2, ROWS, OUT), F32), part, part, part),
        in_specs=full(2),
        out_specs=tuple(full(4)),
        compiler_params=params(),
        name="add_cores",
    )(keep, got)


def x_kernel(stay, one, two, three, keep, send):
    total = stay[...] + one[...].astype(F32) + two[...].astype(F32) + three[...].astype(F32)
    keep[...] = total[0]
    send[...] = total[1].astype(BF16)


def add_x(*parts):
    return pl.pallas_call(
        x_kernel,
        out_shape=(jax.ShapeDtypeStruct((ROWS, OUT), F32), jax.ShapeDtypeStruct((ROWS, OUT), BF16)),
        in_specs=full(4),
        out_specs=tuple(full(2)),
        compiler_params=params(),
        name="add_x",
    )(*parts)


def y_kernel(keep_a, got_a, keep_b, got_b, plain_a, plain_b, to_m1, own, to_p1):
    sum_a = keep_a[...] + got_a[...].astype(F32)
    sum_b = keep_b[...] + got_b[...].astype(F32)
    plain_a[...] = sum_a[:, :WIDE]
    plain_b[...] = sum_b[:, :WIDE]
    pad = jnp.zeros((LANE - 2 * ROWS, LANE), F32)
    mirror = jnp.concatenate([sum_a[:, WIDE:], sum_b[:, WIDE:], pad], axis=0).T
    tail = jnp.concatenate([sum_a[:, LANE:WIDE], sum_b[:, LANE:WIDE], pad], axis=0).T
    to_m1[...] = mirror[0:ROWS]
    own[...] = mirror[ROWS:2 * ROWS]
    to_p1[0:32, :] = mirror[2 * ROWS:]
    to_p1[32:, :] = tail[LANE - 16:]


def add_y(*parts):
    wide = jax.ShapeDtypeStruct((ROWS, WIDE), F32)
    slim = jax.ShapeDtypeStruct((ROWS, LANE), F32)
    return pl.pallas_call(
        y_kernel,
        out_shape=(wide, wide, slim, slim, slim),
        in_specs=full(4),
        out_specs=tuple(full(5)),
        compiler_params=params(),
        name="add_y",
    )(*parts)


def place_kernel(plain_a, plain_b, from_p1, own, from_m1, places, divisor, residual, update):
    source = jnp.concatenate(
        [plain_a[...], plain_b[...], from_p1[...], own[...], from_m1[...]], axis=1)
    high = source.astype(BF16)
    rest = source - high.astype(F32)
    middle = rest.astype(BF16)
    low = (rest - middle.astype(F32)).astype(BF16)
    stacked = jnp.concatenate([high, middle, low], axis=0)
    placed = jnp.dot(stacked, places[...], preferred_element_type=F32)
    value = placed[:ROWS] + (placed[ROWS:2 * ROWS] + placed[2 * ROWS:])
    residual[0] = value
    update[0] = value / divisor[...]


def place(*parts):
    out = jax.ShapeDtypeStruct((1, ROWS, 16 * ROWS), F32)
    return pl.pallas_call(
        place_kernel,
        out_shape=(out, out),
        in_specs=full(7),
        out_specs=tuple(full(2)),
        compiler_params=params(),
        name="place",
    )(*parts)


def place_table():
    blocks = [[(1, 0), (2, 0), (3, 0), (0, 0), (4, 0)],
              [(5, 1), (6, 1), (7, 1), (4, 1), (0, 1)],
              [(7, 0), (3, 1)], [(6, 0), (2, 1)], [(5, 0), (1, 1)]]
    widths = [WIDE, WIDE, LANE, LANE, LANE]
    dz, dy, at, counts = [], [], [], []
    for group, width in zip(blocks, widths):
        for lane in range(width):
            valid = lane < ROWS * len(group)
            block = group[lane // ROWS] if valid else (0, 0)
            dz.append(block[0])
            dy.append(block[1])
            at.append(lane % ROWS)
            counts.append(valid)
    return np.array(dz, np.int32), np.array(dy, np.int32), np.array(at, np.int32), np.array(counts)


def contraction_weights(amplitudes, y_hi, x, core):
    plain = jnp.swapaxes(amplitudes, 1, 2).reshape(PAIRS, SLAB * SLAB)
    mirror = amplitudes.reshape(PAIRS, SLAB * SLAB)
    both = jnp.concatenate([plain, mirror], axis=0)
    row = jnp.arange(2 * PAIRS * GROUP, dtype=jnp.int32)
    near = (row // GROUP) % PAIRS
    order = row // (GROUP * PAIRS)
    pair = ((near % 2) ^ y_hi) * 8 + ((near // 2 + x) % 4) * 2 + ((near // 8) ^ core)
    chosen = (order * PAIRS + pair)[:, None] == jnp.arange(2 * PAIRS, dtype=jnp.int32)[None, :]
    spread = np.arange(DEPTH)[None, :] // GROUP == np.arange(SLAB * SLAB)[:, None]
    rows = jnp.dot(chosen.astype(BF16), both, preferred_element_type=F32).astype(BF16)
    wide = jnp.dot(rows, jnp.asarray(spread, BF16), preferred_element_type=F32)
    same = (row % GROUP)[:, None] == jnp.arange(DEPTH, dtype=jnp.int32)[None, :] % GROUP
    return jnp.where(same, wide, 0.0).astype(BF16)


def per_device(factors, amplitudes, vir_energy, pair_energy):
    here_row = lax.axis_index("row")
    here_col = lax.axis_index("col")
    z, y_lo = here_row // 2, here_row % 2
    y_hi, x, core = here_col // 8, (here_col // 2) % 4, here_col % 2

    own = pack_block(factors)
    p1 = shift(own, dz=-1)
    m1 = shift(own, dz=1)

    weights = contraction_weights(amplitudes, y_hi, x, core)
    dz, dy, at, counts = place_table()
    target = (((z + dz) % 8) * 2 + (y_lo ^ dy)) * ROWS + at
    places = (target[:, None] == jnp.arange(16 * ROWS, dtype=jnp.int32)[None, :]) & counts[:, None]
    places = places.astype(BF16)
    first_energy = lax.dynamic_slice_in_dim(vir_energy, here_row * ROWS, ROWS)
    pair_here = lax.dynamic_slice_in_dim(pair_energy, here_col, 1)
    divisor = first_energy[:, None] + vir_energy[None, :] - pair_here[:, None]

    p2 = shift(p1, dz=-1)
    m2 = shift(m1, dz=1)
    cross = shift(p2, dy=1)
    others = (m1, own, p1, m2, p2)

    def reduced(center):
        keep, send = star(center, others, weights)
        stay, one, two, three = add_cores(keep, shift(send, dc=1))
        keep, send = add_x(stay, shift(one, dx=1), shift(two, dx=2), shift(three, dx=-1))
        return keep, shift(send, dh=1)

    keep_a, got_a = reduced(m2)
    keep_b, got_b = reduced(cross)
    plain_a, plain_b, to_m1, stays, to_p1 = add_y(keep_a, got_a, keep_b, got_b)
    return place(
        shift(plain_a, dz=-2), shift(plain_b, dz=2, dy=1), shift(to_m1, dz=-1), stays, shift(to_p1, dz=1),
        places, divisor)


def solution(mesh):
    return jax.shard_map(
        per_device,
        mesh=mesh,
        in_specs=(P("row", None, "col"), P(), P(), P()),
        out_specs=(P("col", "row", None), P("col", "row", None)),
        check_vma=False,
    )
```

time: 857 us -> 75.1 us (0.09)
  the two profiles are of different devices: /device:TPU:1 before, /device:TPU:6 now
where the time goes in v1:
time: 75.1 us; the launch traced here: 74.9 us
  starting transfers between devices  34.6 us (46%)
  waiting for transfers between devices  24.6 us (33%)
  Pallas kernels  7.54 us (10%)
  local copies, waits for them, and re-layouts  5.44 us (7%)
  other arithmetic  1.29 us (2%)
  between operations  0.91 us (1%)
    ppermute x19, starting transfers between devices, shift(): return lax.ppermute(array, ('row', 'col'), pairs)  34.6 us
    ppermute x19, waiting for transfers between devices, shift(): return lax.ppermute(array, ('row', 'col'), pairs)  24.6 us
    pallas_call x2, Pallas kernels, star(): pl.pallas_call(star_kernel, out_shape=(half, half), in_specs=full(7), out...  6.13 us
    unnamed x25, local copies, waits for them, and re-layouts  2.87 us
  transfers between devices with their start and end apart: 19, of which 10 were waited for; matrix products, arithmetic and copies ran while one was open for 4% of the time, Pallas kernels for 8%

profile of v1, /device:TPU:6, one launch (start us, length us, event | category | flops | bytes accessed | tf_op | source)
XLA Modules:
  0.0 74.9 jit_solution(2048747513896957647)
XLA Ops:
  0.6 1.0 %slice.7 = bf16[48,12,64]{2,0,1:T(8,128)(2,1)S(1)} slice(bf16[48,12,320]{2,0,1:T(8,128)(2,1)} %param.9), slice={[0:48], [0:12], [256:320]} | slice | bytes 147456 | tf_op jit(solution)/shard_map/slice | solution.py:50
  2.2 5.9 %collective-permute-start.2 = (bf16[30,48,128]{2,1,0:T(8,128)(2,1)S(1)}, bf16[30,48,128]{2,1,0:T(8,128)(2,1)S(1)}, u32[]{:S(2)}, u32[]{:S(2)}) collective-permute-start(bf16[30,48,128]{2,1,0:T(8,128)(2,1)S(1)} %pad_maximum_fusion.own), channel_id=1, source_target_pairs={{0,224},{1,225},{2,226},{3,227},{4,228},{5,229},{6,230},{7,231},{8... | collective-permute-start | bytes 1105928 | tf_op jit(solution)/shard_map/ppermute | solution.py:37
  8.1 7.8 %collective-permute-done.2.p1 = bf16[30,48,128]{2,1,0:T(8,128)(2,1)S(1)} collective-permute-done((bf16[30,48,128]{2,1,0:T(8,128)(2,1)S(1)}, bf16[30,48,128]{2,1,0:T(8,128)(2,1)S(1)}, u32[]{:S(2)}, u32[]{:S(2)}) %collective-permute-start.2) | collective-permute-done | bytes 368672 | tf_op jit(solution)/shard_map/ppermute | solution.py:37
  16.0 3.7 %collective-permute-start.3 = (bf16[30,48,128]{2,1,0:T(8,128)(2,1)S(1)}, bf16[30,48,128]{2,1,0:T(8,128)(2,1)S(1)}, u32[]{:S(2)}, u32[]{:S(2)}) collective-permute-start(bf16[30,48,128]{2,1,0:T(8,128)(2,1)S(1)} %collective-permute-done.2.p1), channel_id=1, source_target_pairs={{0,224},{1,225},{2,226},{3,227},{4,228},{5,229},{6,230},{7,231},{8... | collective-permute-start | bytes 1105928 | tf_op jit(solution)/shard_map/ppermute | solution.py:37
  20.2 6.4 %collective-permute-done.3.p2 = bf16[30,48,128]{2,1,0:T(8,128)(2,1)S(1)} collective-permute-done((bf16[30,48,128]{2,1,0:T(8,128)(2,1)S(1)}, bf16[30,48,128]{2,1,0:T(8,128)(2,1)S(1)}, u32[]{:S(2)}, u32[]{:S(2)}) %collective-permute-start.3) | collective-permute-done | bytes 368672 | tf_op jit(solution)/shard_map/ppermute | solution.py:37
  26.6 1.6 %collective-permute-start.9 = (bf16[30,48,128]{2,1,0:T(8,128)(2,1)S(1)}, bf16[30,48,128]{2,1,0:T(8,128)(2,1)S(1)}, u32[]{:S(2)}, u32[]{:S(2)}) collective-permute-start(bf16[30,48,128]{2,1,0:T(8,128)(2,1)S(1)} %collective-permute-done.3.p2), channel_id=1, source_target_pairs={{0,16},{1,17},{2,18},{3,19},{4,20},{5,21},{6,22},{7,23},{8,24},{9,... | collective-permute-start | bytes 1105928 | tf_op jit(solution)/shard_map/ppermute | solution.py:37
  28.8 1.3 %collective-permute-done.1.center.m2 = bf16[30,48,128]{2,1,0:T(8,128)(2,1)S(1)} collective-permute-done((bf16[30,48,128]{2,1,0:T(8,128)(2,1)S(1)}, bf16[30,48,128]{2,1,0:T(8,128)(2,1)S(1)}, u32[]{:S(2)}, u32[]{:S(2)}) %collective-permute-start.1) | collective-permute-done | bytes 368672 | tf_op jit(solution)/shard_map/ppermute | solution.py:37
  30.1 3.1 %star.2 = (f32[8,48,384]{2,1,0:T(8,128)S(1)}, f32[8,48,384]{2,1,0:T(8,128)S(1)}) custom-call(bf16[30,48,128]{2,1,0:T(8,128)(2,1)S(1)} %collective-permute-done.1.center.m2, bf16[30,48,128]{2,1,0:T(8,128)(2,1)S(1)} %collective-permute-done.m1, bf16[30,48,128]{2,1,0:T(8,128)(2,1)S(1)} %pad_maximum_fusion.own, ...), custom_call_target="tpu_custom_call" | custom-call | flops 3500000000 | bytes 4000000 | tf_op jit(solution)/shard_map/star/pallas_call | solution.py:95
  33.2 1.9 %collective-permute-done.9.center = bf16[30,48,128]{2,1,0:T(8,128)(2,1)S(1)} collective-permute-done((bf16[30,48,128]{2,1,0:T(8,128)(2,1)S(1)}, bf16[30,48,128]{2,1,0:T(8,128)(2,1)S(1)}, u32[]{:S(2)}, u32[]{:S(2)}) %collective-permute-start.9) | collective-permute-done | bytes 368672 | tf_op jit(solution)/shard_map/ppermute | solution.py:37
  35.9 1.0 %copy-done.1 = bf16[30,48,128]{2,1,0:T(8,128)(2,1)S(1)} copy-done((bf16[30,48,128]{2,1,0:T(8,128)(2,1)S(1)}, bf16[30,48,128]{2,1,0:T(8,128)(2,1)}, u32[]{:S(2)}) %copy-start.1) | copy-done | bytes 368664
  36.9 1.1 %copy-done.3 = bf16[256,1152]{1,0:T(8,128)(2,1)S(1)} copy-done((bf16[256,1152]{1,0:T(8,128)(2,1)S(1)}, bf16[256,1152]{1,0:T(8,128)(2,1)}, u32[]{:S(2)}) %copy-start.3) | copy-done | bytes 589848
  38.0 3.1 %star.3 = (f32[8,48,384]{2,1,0:T(8,128)S(1)}, f32[8,48,384]{2,1,0:T(8,128)S(1)}) custom-call(bf16[30,48,128]{2,1,0:T(8,128)(2,1)S(1)} %copy-done.1, bf16[30,48,128]{2,1,0:T(8,128)(2,1)S(1)} %collective-permute-done.m1, bf16[30,48,128]{2,1,0:T(8,128)(2,1)S(1)} %pad_maximum_fusion.own, bf16[30,48,128]{2,1,0:T(8,128)(2,1)S(1)} %collective-permute-done.2.p1, ...), custom_call_target="tpu_custom_call" | custom-call | flops 3500000000 | bytes 4000000 | tf_op jit(solution)/shard_map/star/pallas_call | solution.py:95
  41.8 2.4 %collective-permute-start.6 = (bf16[2,48,384]{2,1,0:T(8,128)(2,1)S(1)}, bf16[2,48,384]{2,1,0:T(8,128)(2,1)S(1)}, u32[]{:S(2)}, u32[]{:S(2)}) collective-permute-start(bf16[2,48,384]{2,1,0:T(8,128)(2,1)S(1)} %get-tuple-element.27), channel_id=1, source_target_pairs={{0,4},{1,5},{2,6},{3,7},{4,0},{5,1},{6,2},{7,3},{8,12},{9,13},{10,... | collective-permute-start | bytes 221192 | tf_op jit(solution)/shard_map/ppermute | solution.py:37
  44.3 3.3 %collective-permute-start.11 = (bf16[2,48,384]{2,1,0:T(8,128)(2,1)S(1)}, bf16[2,48,384]{2,1,0:T(8,128)(2,1)S(1)}, u32[]{:S(2)}, u32[]{:S(2)}) collective-permute-start(bf16[2,48,384]{2,1,0:T(8,128)(2,1)S(1)} %get-tuple-element.34), channel_id=1, source_target_pairs={{0,2},{1,3},{2,4},{3,5},{4,6},{5,7},{6,0},{7,1},{8,10},{9,11},{10,... | collective-permute-start | bytes 221192 | tf_op jit(solution)/shard_map/ppermute | solution.py:37
  47.8 1.3 %collective-permute-start.13 = (bf16[2,48,384]{2,1,0:T(8,128)(2,1)S(1)}, bf16[2,48,384]{2,1,0:T(8,128)(2,1)S(1)}, u32[]{:S(2)}, u32[]{:S(2)}) collective-permute-start(bf16[2,48,384]{2,1,0:T(8,128)(2,1)S(1)} %get-tuple-element.36), channel_id=1, source_target_pairs={{0,6},{1,7},{2,0},{3,1},{4,2},{5,3},{6,4},{7,5},{8,14},{9,15},{10,... | collective-permute-start | bytes 221192 | tf_op jit(solution)/shard_map/ppermute | solution.py:37
  49.9 3.3 %collective-permute-start.8 = (bf16[48,384]{1,0:T(8,128)(2,1)S(1)}, bf16[48,384]{1,0:T(8,128)(2,1)S(1)}, u32[]{:S(2)}, u32[]{:S(2)}) collective-permute-start(bf16[48,384]{1,0:T(8,128)(2,1)S(1)} %get-tuple-element.30), channel_id=1, source_target_pairs={{0,8},{1,9},{2,10},{3,11},{4,12},{5,13},{6,14},{7,15},{8,0},{9,1},... | collective-permute-start | bytes 110600 | tf_op jit(solution)/shard_map/ppermute | solution.py:37
  54.2 3.3 %collective-permute-start.14 = (bf16[48,384]{1,0:T(8,128)(2,1)S(1)}, bf16[48,384]{1,0:T(8,128)(2,1)S(1)}, u32[]{:S(2)}, u32[]{:S(2)}) collective-permute-start(bf16[48,384]{1,0:T(8,128)(2,1)S(1)} %get-tuple-element.38), channel_id=1, source_target_pairs={{0,8},{1,9},{2,10},{3,11},{4,12},{5,13},{6,14},{7,15},{8,0},{9,1},... | collective-permute-start | bytes 110600 | tf_op jit(solution)/shard_map/ppermute | solution.py:37
  58.7 1.1 %collective-permute-done.14.got_b = bf16[48,384]{1,0:T(8,128)(2,1)S(1)} collective-permute-done((bf16[48,384]{1,0:T(8,128)(2,1)S(1)}, bf16[48,384]{1,0:T(8,128)(2,1)S(1)}, u32[]{:S(2)}, u32[]{:S(2)}) %collective-permute-start.14) | collective-permute-done | bytes 36896 | tf_op jit(solution)/shard_map/ppermute | solution.py:37
  59.8 2.6 %collective-permute-start.15 = (f32[48,256]{1,0:T(8,128)S(1)}, f32[48,256]{1,0:T(8,128)S(1)}, u32[]{:S(2)}, u32[]{:S(2)}) collective-permute-start(f32[48,256]{1,0:T(8,128)S(1)} %get-tuple-element.39), channel_id=1, source_target_pairs={{0,192},{1,193},{2,194},{3,195},{4,196},{5,197},{6,198},{7,199},{8... | collective-permute-start | bytes 147464 | tf_op jit(solution)/shard_map/ppermute | solution.py:37
  62.4 1.5 %collective-permute-start.16 = (f32[48,256]{1,0:T(8,128)S(1)}, f32[48,256]{1,0:T(8,128)S(1)}, u32[]{:S(2)}, u32[]{:S(2)}) collective-permute-start(f32[48,256]{1,0:T(8,128)S(1)} %get-tuple-element.40), channel_id=1, source_target_pairs={{0,80},{1,81},{2,82},{3,83},{4,84},{5,85},{6,86},{7,87},{8,88},{9,... | collective-permute-start | bytes 147464 | tf_op jit(solution)/shard_map/ppermute | solution.py:37
  63.9 4.9 %collective-permute-start.17 = (f32[48,128]{1,0:T(8,128)S(1)}, f32[48,128]{1,0:T(8,128)S(1)}, u32[]{:S(2)}, u32[]{:S(2)}) collective-permute-start(f32[48,128]{1,0:T(8,128)S(1)} %get-tuple-element.41), channel_id=1, source_target_pairs={{0,224},{1,225},{2,226},{3,227},{4,228},{5,229},{6,230},{7,231},{8... | collective-permute-start | bytes 73736 | tf_op jit(solution)/shard_map/ppermute | solution.py:37
  69.5 0.8 %collective-permute-done.17.from_p1 = f32[48,128]{1,0:T(8,128)S(1)} collective-permute-done((f32[48,128]{1,0:T(8,128)S(1)}, f32[48,128]{1,0:T(8,128)S(1)}, u32[]{:S(2)}, u32[]{:S(2)}) %collective-permute-start.17) | collective-permute-done | bytes 24608 | tf_op jit(solution)/shard_map/ppermute | solution.py:37
  70.3 3.5 %collective-permute-done.18.from_m1 = f32[48,128]{1,0:T(8,128)S(1)} collective-permute-done((f32[48,128]{1,0:T(8,128)S(1)}, f32[48,128]{1,0:T(8,128)S(1)}, u32[]{:S(2)}, u32[]{:S(2)}) %collective-permute-start.18) | collective-permute-done | bytes 24608 | tf_op jit(solution)/shard_map/ppermute | solution.py:37
  73.8 1.1 %place.1 = (f32[1,48,768]{2,1,0:T(8,128)}, f32[1,48,768]{2,1,0:T(8,128)}) custom-call(f32[48,256]{1,0:T(8,128)S(1)} %collective-permute-done.15.plain_a, f32[48,256]{1,0:T(8,128)S(1)} %collective-permute-done.16.plain_b, f32[48,128]{1,0:T(8,128)S(1)} %collective-permute-done.17.from_p1, f32[48,128]{1,0:T(8,128)S(1)} %get-tuple-element.42.own, ...), custom_call_target="tpu_custom_call" | custom-call | tf_op jit(solution)/shard_map/place/pallas_call | solution.py:189
  (67 shorter events, 7.1 us)
Async XLA Ops:
  2.0 17.7 %copy-start.4 = (bf16[16,12,12]{2,0,1:T(8,128)(2,1)S(1)}, bf16[16,12,12]{2,0,1:T(8,128)(2,1)}, u32[]{:S(2)}) copy-start(bf16[16,12,12]{2,0,1:T(8,128)(2,1)} %param.10) | copy-start | bytes 13828
  2.0 26.2 %copy-start.11 = (bf16[144,1152]{1,0:T(8,128)(2,1)S(1)}, bf16[144,1152]{1,0:T(8,128)(2,1)}, u32[]{:S(2)}) copy-start(bf16[144,1152]{1,0:T(8,128)(2,1)} %constant.172.clone) | copy-start | bytes 995332
  2.2 13.8 %collective-permute-start.2 = (bf16[30,48,128]{2,1,0:T(8,128)(2,1)S(1)}, bf16[30,48,128]{2,1,0:T(8,128)(2,1)S(1)}, u32[]{:S(2)}, u32[]{:S(2)}) collective-permute-start(bf16[30,48,128]{2,1,0:T(8,128)(2,1)S(1)} %pad_maximum_fusion.own), channel_id=1, source_target_pairs={{0,224},{1,225},{2,226},{3,227},{4,228},{5,229},{6,230},{7,231},{8... | collective-permute-start | bytes 1105928 | tf_op jit(solution)/shard_map/ppermute | solution.py:37
  8.1 11.5 %collective-permute-start = (bf16[30,48,128]{2,1,0:T(8,128)(2,1)S(1)}, bf16[30,48,128]{2,1,0:T(8,128)(2,1)S(1)}, u32[]{:S(2)}, u32[]{:S(2)}) collective-permute-start(bf16[30,48,128]{2,1,0:T(8,128)(2,1)S(1)} %pad_maximum_fusion.own), channel_id=1, source_target_pairs={{0,32},{1,33},{2,34},{3,35},{4,36},{5,37},{6,38},{7,39},{8,40},{9,... | collective-permute-start | bytes 1105928 | tf_op jit(solution)/shard_map/ppermute | solution.py:37
  16.0 10.7 %collective-permute-start.3 = (bf16[30,48,128]{2,1,0:T(8,128)(2,1)S(1)}, bf16[30,48,128]{2,1,0:T(8,128)(2,1)S(1)}, u32[]{:S(2)}, u32[]{:S(2)}) collective-permute-start(bf16[30,48,128]{2,1,0:T(8,128)(2,1)S(1)} %collective-permute-done.2.p1), channel_id=1, source_target_pairs={{0,224},{1,225},{2,226},{3,227},{4,228},{5,229},{6,230},{7,231},{8... | collective-permute-start | bytes 1105928 | tf_op jit(solution)/shard_map/ppermute | solution.py:37
  19.7 10.4 %collective-permute-start.1 = (bf16[30,48,128]{2,1,0:T(8,128)(2,1)S(1)}, bf16[30,48,128]{2,1,0:T(8,128)(2,1)S(1)}, u32[]{:S(2)}, u32[]{:S(2)}) collective-permute-start(bf16[30,48,128]{2,1,0:T(8,128)(2,1)S(1)} %collective-permute-done.m1), channel_id=1, source_target_pairs={{0,32},{1,33},{2,34},{3,35},{4,36},{5,37},{6,38},{7,39},{8,40},{9,... | collective-permute-start | bytes 1105928 | tf_op jit(solution)/shard_map/ppermute | solution.py:37
  26.6 8.5 %collective-permute-start.9 = (bf16[30,48,128]{2,1,0:T(8,128)(2,1)S(1)}, bf16[30,48,128]{2,1,0:T(8,128)(2,1)S(1)}, u32[]{:S(2)}, u32[]{:S(2)}) collective-permute-start(bf16[30,48,128]{2,1,0:T(8,128)(2,1)S(1)} %collective-permute-done.3.p2), channel_id=1, source_target_pairs={{0,16},{1,17},{2,18},{3,19},{4,20},{5,21},{6,22},{7,23},{8,24},{9,... | collective-permute-start | bytes 1105928 | tf_op jit(solution)/shard_map/ppermute | solution.py:37
  33.1 8.0 %collective-permute-start.4 = (f32[8,48,384]{2,1,0:T(8,128)S(1)}, f32[8,48,384]{2,1,0:T(8,128)S(1)}, u32[]{:S(2)}, u32[]{:S(2)}) collective-permute-start(f32[8,48,384]{2,1,0:T(8,128)S(1)} %get-tuple-element.24), channel_id=1, source_target_pairs={{0,1},{1,0},{2,3},{3,2},{4,5},{5,4},{6,7},{7,6},{8,9},{9,8},{10,11... | collective-permute-start | bytes 1769480 | tf_op jit(solution)/shard_map/ppermute | solution.py:37
  41.1 3.2 %collective-permute-start.10 = (f32[8,48,384]{2,1,0:T(8,128)S(1)}, f32[8,48,384]{2,1,0:T(8,128)S(1)}, u32[]{:S(2)}, u32[]{:S(2)}) collective-permute-start(f32[8,48,384]{2,1,0:T(8,128)S(1)} %get-tuple-element.32), channel_id=1, source_target_pairs={{0,1},{1,0},{2,3},{3,2},{4,5},{5,4},{6,7},{7,6},{8,9},{9,8},{10,11... | collective-permute-start | bytes 1769480 | tf_op jit(solution)/shard_map/ppermute | solution.py:37
  41.3 16.2 %copy-start.9 = (pred[896]{0:T(1024)(128)(4,1)S(1)}, pred[896]{0:T(1024)(128)(4,1)}, u32[]{:S(2)}) copy-start(pred[896]{0:T(1024)(128)(4,1)} %constant.177) | copy-start | bytes 2692
  41.3 6.5 %collective-permute-start.5 = (bf16[2,48,384]{2,1,0:T(8,128)(2,1)S(1)}, bf16[2,48,384]{2,1,0:T(8,128)(2,1)S(1)}, u32[]{:S(2)}, u32[]{:S(2)}) collective-permute-start(bf16[2,48,384]{2,1,0:T(8,128)(2,1)S(1)} %get-tuple-element.26), channel_id=1, source_target_pairs={{0,2},{1,3},{2,4},{3,5},{4,6},{5,7},{6,0},{7,1},{8,10},{9,11},{10,... | collective-permute-start | bytes 221192 | tf_op jit(solution)/shard_map/ppermute | solution.py:37
  41.8 7.3 %collective-permute-start.6 = (bf16[2,48,384]{2,1,0:T(8,128)(2,1)S(1)}, bf16[2,48,384]{2,1,0:T(8,128)(2,1)S(1)}, u32[]{:S(2)}, u32[]{:S(2)}) collective-permute-start(bf16[2,48,384]{2,1,0:T(8,128)(2,1)S(1)} %get-tuple-element.27), channel_id=1, source_target_pairs={{0,4},{1,5},{2,6},{3,7},{4,0},{5,1},{6,2},{7,3},{8,12},{9,13},{10,... | collective-permute-start | bytes 221192 | tf_op jit(solution)/shard_map/ppermute | solution.py:37
  44.3 5.6 %collective-permute-start.7 = (bf16[2,48,384]{2,1,0:T(8,128)(2,1)S(1)}, bf16[2,48,384]{2,1,0:T(8,128)(2,1)S(1)}, u32[]{:S(2)}, u32[]{:S(2)}) collective-permute-start(bf16[2,48,384]{2,1,0:T(8,128)(2,1)S(1)} %get-tuple-element.28), channel_id=1, source_target_pairs={{0,6},{1,7},{2,0},{3,1},{4,2},{5,3},{6,4},{7,5},{8,14},{9,15},{10,... | collective-permute-start | bytes 221192 | tf_op jit(solution)/shard_map/ppermute | solution.py:37
  44.3 13.7 %copy-start.10 = (f32[16]{0:T(128)S(1)}, f32[16]{0:T(128)}, u32[]{:S(2)}) copy-start(f32[16]{0:T(128)} %param.12) | copy-start | bytes 196
  44.3 14.2 %copy-start.5 = (f32[768]{0:T(1024)S(1)}, f32[768]{0:T(1024)}, u32[]{:S(2)}) copy-start(f32[768]{0:T(1024)} %param.11) | copy-start | bytes 9220
  44.3 8.8 %collective-permute-start.11 = (bf16[2,48,384]{2,1,0:T(8,128)(2,1)S(1)}, bf16[2,48,384]{2,1,0:T(8,128)(2,1)S(1)}, u32[]{:S(2)}, u32[]{:S(2)}) collective-permute-start(bf16[2,48,384]{2,1,0:T(8,128)(2,1)S(1)} %get-tuple-element.34), channel_id=1, source_target_pairs={{0,2},{1,3},{2,4},{3,5},{4,6},{5,7},{6,0},{7,1},{8,10},{9,11},{10,... | collective-permute-start | bytes 221192 | tf_op jit(solution)/shard_map/ppermute | solution.py:37
  47.7 5.9 %collective-permute-start.12 = (bf16[2,48,384]{2,1,0:T(8,128)(2,1)S(1)}, bf16[2,48,384]{2,1,0:T(8,128)(2,1)S(1)}, u32[]{:S(2)}, u32[]{:S(2)}) collective-permute-start(bf16[2,48,384]{2,1,0:T(8,128)(2,1)S(1)} %get-tuple-element.35), channel_id=1, source_target_pairs={{0,4},{1,5},{2,6},{3,7},{4,0},{5,1},{6,2},{7,3},{8,12},{9,13},{10,... | collective-permute-start | bytes 221192 | tf_op jit(solution)/shard_map/ppermute | solution.py:37
  47.8 6.4 %collective-permute-start.13 = (bf16[2,48,384]{2,1,0:T(8,128)(2,1)S(1)}, bf16[2,48,384]{2,1,0:T(8,128)(2,1)S(1)}, u32[]{:S(2)}, u32[]{:S(2)}) collective-permute-start(bf16[2,48,384]{2,1,0:T(8,128)(2,1)S(1)} %get-tuple-element.36), channel_id=1, source_target_pairs={{0,6},{1,7},{2,0},{3,1},{4,2},{5,3},{6,4},{7,5},{8,14},{9,15},{10,... | collective-permute-start | bytes 221192 | tf_op jit(solution)/shard_map/ppermute | solution.py:37
  49.9 8.8 %collective-permute-start.8 = (bf16[48,384]{1,0:T(8,128)(2,1)S(1)}, bf16[48,384]{1,0:T(8,128)(2,1)S(1)}, u32[]{:S(2)}, u32[]{:S(2)}) collective-permute-start(bf16[48,384]{1,0:T(8,128)(2,1)S(1)} %get-tuple-element.30), channel_id=1, source_target_pairs={{0,8},{1,9},{2,10},{3,11},{4,12},{5,13},{6,14},{7,15},{8,0},{9,1},... | collective-permute-start | bytes 110600 | tf_op jit(solution)/shard_map/ppermute | solution.py:37
  54.2 5.5 %collective-permute-start.14 = (bf16[48,384]{1,0:T(8,128)(2,1)S(1)}, bf16[48,384]{1,0:T(8,128)(2,1)S(1)}, u32[]{:S(2)}, u32[]{:S(2)}) collective-permute-start(bf16[48,384]{1,0:T(8,128)(2,1)S(1)} %get-tuple-element.38), channel_id=1, source_target_pairs={{0,8},{1,9},{2,10},{3,11},{4,12},{5,13},{6,14},{7,15},{8,0},{9,1},... | collective-permute-start | bytes 110600 | tf_op jit(solution)/shard_map/ppermute | solution.py:37
  59.8 14.0 %collective-permute-start.15 = (f32[48,256]{1,0:T(8,128)S(1)}, f32[48,256]{1,0:T(8,128)S(1)}, u32[]{:S(2)}, u32[]{:S(2)}) collective-permute-start(f32[48,256]{1,0:T(8,128)S(1)} %get-tuple-element.39), channel_id=1, source_target_pairs={{0,192},{1,193},{2,194},{3,195},{4,196},{5,197},{6,198},{7,199},{8... | collective-permute-start | bytes 147464 | tf_op jit(solution)/shard_map/ppermute | solution.py:37
  62.4 11.4 %collective-permute-start.16 = (f32[48,256]{1,0:T(8,128)S(1)}, f32[48,256]{1,0:T(8,128)S(1)}, u32[]{:S(2)}, u32[]{:S(2)}) collective-permute-start(f32[48,256]{1,0:T(8,128)S(1)} %get-tuple-element.40), channel_id=1, source_target_pairs={{0,80},{1,81},{2,82},{3,83},{4,84},{5,85},{6,86},{7,87},{8,88},{9,... | collective-permute-start | bytes 147464 | tf_op jit(solution)/shard_map/ppermute | solution.py:37
  63.9 6.4 %collective-permute-start.17 = (f32[48,128]{1,0:T(8,128)S(1)}, f32[48,128]{1,0:T(8,128)S(1)}, u32[]{:S(2)}, u32[]{:S(2)}) collective-permute-start(f32[48,128]{1,0:T(8,128)S(1)} %get-tuple-element.41), channel_id=1, source_target_pairs={{0,224},{1,225},{2,226},{3,227},{4,228},{5,229},{6,230},{7,231},{8... | collective-permute-start | bytes 73736 | tf_op jit(solution)/shard_map/ppermute | solution.py:37
  68.8 5.0 %collective-permute-start.18 = (f32[48,128]{1,0:T(8,128)S(1)}, f32[48,128]{1,0:T(8,128)S(1)}, u32[]{:S(2)}, u32[]{:S(2)}) collective-permute-start(f32[48,128]{1,0:T(8,128)S(1)} %get-tuple-element.43), channel_id=1, source_target_pairs={{0,32},{1,33},{2,34},{3,35},{4,36},{5,37},{6,38},{7,39},{8,40},{9,... | collective-permute-start | bytes 73736 | tf_op jit(solution)/shard_map/ppermute | solution.py:37
  (8 other events, 32.2 us)

commit v2 on v1

v2 whole, which is shorter than its diff:
```python
import jax
import jax.numpy as jnp
import numpy as np
from jax import lax
from jax.experimental import pallas as pl
from jax.experimental.pallas import tpu as pltpu
from jax.sharding import PartitionSpec as P

ROWS = 48
SLAB = 12
PAIRS = 16
LANE = 128
WIDE = 256
CHUNK = 15
GROUP = 8
GROUPS = ROWS // GROUP
DEPTH = SLAB * SLAB * GROUP // 2
OUT = 3 * LANE
BF16 = jnp.bfloat16
F32 = jnp.float32


def device_of(index):
    row, col = divmod(index, 16)
    return row // 2, row % 2, col // 8, (col // 2) % 4, col % 2


def index_of(z, y_lo, y_hi, x, core):
    return ((z % 8) * 2 + y_lo % 2) * 16 + (y_hi % 2) * 8 + (x % 4) * 2 + core % 2


def shift(array, dz=0, dy=0, dh=0, dx=0, dc=0):
    pairs = []
    for source in range(256):
        z, y, h, x, c = device_of(source)
        pairs.append((source, index_of(z + dz, y + dy, h + dh, x + dx, c + dc)))
    return lax.ppermute(array, ("row", "col"), pairs)


def to_rows(array, flows):
    pairs = []
    for source in range(256):
        z, y, h, x, c = device_of(source)
        dz, dy = flows[c]
        pairs.append((source, index_of(z + dz, y + dy, h, x, c)))
    return lax.ppermute(array, ("row", "col"), pairs)


def full(count):
    return [pl.BlockSpec(memory_space=pltpu.VMEM)] * count


def params():
    return pltpu.CompilerParams(vmem_limit_bytes=24 * 1024 * 1024)


def core_here():
    return lax.rem(lax.axis_index("col"), 2)


def tiles_of(c):
    start, within = CHUNK * (c // 6), c % 6
    return start + 2 * within, start + 2 * within + 1, start + 12 + within % 3, within // 3


def pack_kernel(factors, packed):
    for c in range(SLAB):
        first, second, last, half = tiles_of(c)
        packed[first] = factors[c, :, 0:LANE]
        packed[second] = factors[c, :, LANE:WIDE]
        if half == 0:
            both = [factors[at, :, WIDE:].astype(F32) for at in (c, c + 3)]
            packed[last] = jnp.concatenate(both, axis=1).astype(BF16)


def pack_block(factors):
    return pl.pallas_call(
        pack_kernel,
        out_shape=jax.ShapeDtypeStruct((2 * CHUNK, ROWS, LANE), BF16),
        in_specs=full(1),
        out_specs=full(1)[0],
        compiler_params=params(),
        name="pack",
    )(jnp.transpose(factors, (1, 0, 2)))


def build_left(center, left):
    low = lax.broadcasted_iota(jnp.int32, (ROWS, LANE), 1) < LANE // 2
    zero = jnp.zeros((ROWS, LANE), F32)
    for c in range(SLAB):
        rows = pl.ds(c * ROWS, ROWS)
        main, second, tile, at = tiles_of(c)
        last = center[tile].astype(F32)
        moved = pltpu.roll(last, LANE // 2, 1)
        in_low, in_high = (last, moved) if at == 0 else (moved, last)
        for half in range(2):
            left[half, rows, 0:LANE] = center[main]
            left[half, rows, LANE:2 * LANE] = center[second]
        left[0, rows, 2 * LANE:] = jnp.where(low, in_low, zero).astype(BF16)
        left[1, rows, 2 * LANE:] = jnp.where(low, zero, in_high).astype(BF16)


def build_products(left, near, own, far, m2, p2, products):
    rows = 6 * GROUP
    for d in range(SLAB):
        columns = []
        first, second, last, half = tiles_of(d)
        for tile in (first, second, last):
            columns.append(jnp.concatenate(
                [near[tile], own[tile], far[tile], m2[tile], p2[tile], far[tile, 32:, :]], axis=0))
        right = jnp.concatenate(columns, axis=1)
        block = lax.dot_general(left[half], right, (((1,), (1,)), ((), ())), preferred_element_type=F32)
        block = block.reshape(2, 6, GROUPS, GROUP, WIDE)
        for chunk in range(2):
            for g in range(GROUPS):
                part = block[chunk, :, g].reshape(rows, WIDE)
                products[chunk, g, d * rows:(d + 1) * rows, :] = part.astype(BF16)


def contract(one, two, products, g):
    return (jnp.dot(one[...], products[0, g], preferred_element_type=F32)
            + jnp.dot(two[...], products[1, g], preferred_element_type=F32))


def first_kernel(center, m1, own, p1, m2, p2, one, two, energy, pair, raw, divisor, left, products):
    shape = divisor.shape
    second = jnp.broadcast_to(energy[...], shape)
    row = lax.axis_index("row") * ROWS + lax.broadcasted_iota(jnp.int32, shape, 0)
    mine = lax.broadcasted_iota(jnp.int32, shape, 1) == row
    first = jnp.sum(jnp.where(mine, second, 0.0), axis=1, keepdims=True)
    divisor[...] = first + second - pair[lax.axis_index("col")]
    build_left(center, left)
    build_products(left, m1, own, p1, m2, p2, products)
    for g in range(GROUPS):
        raw[g] = contract(one, two, products, g)


def second_kernel(center, m1, own, p1, m2, p2, one, two, raw, keep, send, left, products):
    build_left(center, left)
    build_products(left, p1, own, m1, m2, p2, products)
    half = PAIRS * GROUP
    lane = lax.broadcasted_iota(jnp.int32, (half, LANE), 1)
    here = core_here() == 0
    shape = (2, 4, 2, GROUP, LANE)
    for g in range(0, GROUPS, 2):
        staying, going = [], []
        for step in range(2):
            mine = contract(one, two, products, g + step)
            other = raw[g + step]
            for at, inside in enumerate((LANE, 5 * ROWS - LANE, 2 * ROWS)):
                lanes = slice(LANE, WIDE) if at == 1 else slice(0, LANE)
                row = slice(half, 2 * half) if at == 2 else slice(0, half)
                back = slice(half, 2 * half)
                down, up = other[row, lanes], mine[row, lanes]
                if at > 0:
                    down, up = (jnp.where(lane < inside, down, mine[back, lanes]),
                                jnp.where(lane < inside, up, other[back, lanes]))
                staying.append(jnp.where(here, down, up).reshape(shape))
                going.append(jnp.where(here, up, down).reshape(shape))
        rows = pl.ds(g * GROUP, 2 * GROUP)
        for at in range(3):
            lanes = pl.ds(at * LANE, LANE)
            keep[:, :, :, rows, lanes] = jnp.concatenate([staying[at], staying[3 + at]], axis=3)
            send[:, :, :, rows, lanes] = jnp.concatenate([going[at], going[3 + at]], axis=3).astype(BF16)


def scratch():
    return [
        pltpu.VMEM((2, SLAB * ROWS, 3 * LANE), BF16),
        pltpu.VMEM((2, GROUPS, DEPTH, WIDE), BF16),
    ]


def first_star(center, others, weights, vir_energy, pair_energy):
    return pl.pallas_call(
        first_kernel,
        out_shape=(jax.ShapeDtypeStruct((GROUPS, 2 * PAIRS * GROUP, WIDE), F32),
                   jax.ShapeDtypeStruct((ROWS, 16 * ROWS), F32)),
        in_specs=full(9) + [pl.BlockSpec(memory_space=pltpu.SMEM)],
        out_specs=tuple(full(2)),
        scratch_shapes=scratch(),
        compiler_params=params(),
        name="first_star",
    )(center, *others, *weights, vir_energy[None, :], pair_energy)


def second_star(center, others, weights, raw):
    shape = (2, 4, 2, ROWS, OUT)
    return pl.pallas_call(
        second_kernel,
        out_shape=(jax.ShapeDtypeStruct(shape, F32), jax.ShapeDtypeStruct(shape, BF16)),
        in_specs=full(9),
        out_specs=tuple(full(2)),
        scratch_shapes=scratch(),
        compiler_params=params(),
        name="second_star",
    )(center, *others, *weights, raw)


def core_kernel(keep, got, stay, one, two, three):
    x = lax.rem(lax.div(lax.axis_index("col"), 2), 4)
    for step, out in enumerate((stay, one, two, three)):
        at = lax.rem(x + step, 4)
        out[...] = (keep[:, at] + got[:, at].astype(F32)).astype(out.dtype)


def add_cores(keep, got):
    shape = (2, 2, ROWS, OUT)
    return pl.pallas_call(
        core_kernel,
        out_shape=(jax.ShapeDtypeStruct(shape, F32),) + (jax.ShapeDtypeStruct(shape, BF16),) * 3,
        in_specs=full(2),
        out_specs=tuple(full(4)),
        compiler_params=params(),
        name="add_cores",
    )(keep, got)


def x_kernel(stay, two, three, one, keep, send):
    y_hi = lax.div(lax.axis_index("col"), 8)
    for at, out in ((y_hi, keep), (1 - y_hi, send)):
        total = stay[at] + one[at].astype(F32) + two[at].astype(F32) + three[at].astype(F32)
        out[...] = total.astype(out.dtype)


def add_x(*parts):
    shape = (2, ROWS, OUT)
    return pl.pallas_call(
        x_kernel,
        out_shape=(jax.ShapeDtypeStruct(shape, F32), jax.ShapeDtypeStruct(shape, BF16)),
        in_specs=full(4),
        out_specs=tuple(full(2)),
        compiler_params=params(),
        name="add_x",
    )(*parts)


def sum_kernel(keep, got, plain, mirror, stays, stays_other):
    lane = lax.broadcasted_iota(jnp.int32, (ROWS, LANE), 1)
    pad = jnp.zeros((LANE - 2 * ROWS, LANE), F32)
    totals = [keep[pair] + got[pair].astype(F32) for pair in range(2)]
    here = core_here() == 0
    ordered = (jnp.where(here, totals[0], totals[1]), jnp.where(here, totals[1], totals[0]))
    for at, total in enumerate(ordered):
        plain[at] = total[:, :WIDE]
        last = total[:, WIDE:]
        second = jnp.where(lane < 32, pltpu.roll(last, 32, 1), pltpu.roll(total[:, LANE:WIDE], 48, 1))
        turned = jnp.concatenate([last, second, pad], axis=0).T
        mirror[at] = turned[0:ROWS]
        (stays, stays_other)[at][...] = turned[ROWS:2 * ROWS]


def sum_parts(keep, got):
    slim = jax.ShapeDtypeStruct((ROWS, LANE), F32)
    return pl.pallas_call(
        sum_kernel,
        out_shape=(jax.ShapeDtypeStruct((2, ROWS, WIDE), F32), jax.ShapeDtypeStruct((2, ROWS, LANE), F32), slim, slim),
        in_specs=full(2),
        out_specs=tuple(full(4)),
        compiler_params=params(),
        name="sum_parts",
    )(keep, got)


def place_kernel(plain, plain_other, mirror, mirror_other, stays, stays_other, divisor, residual, update):
    row = lax.axis_index("row")
    z, y_lo = lax.div(row, 2), lax.rem(row, 2)
    here = core_here() == 0

    def both(near, far):
        return jnp.where(here, near, far), jnp.where(here, far, near)

    plain_0, plain_1 = both(plain[0], plain_other[...])
    mirror_0, mirror_1 = both(mirror[0], mirror_other[...])
    stays_0, stays_1 = both(stays[...], stays_other[...])

    def piece(array, at):
        return array[:, at * ROWS:(at + 1) * ROWS]

    wide = jnp.concatenate([
        piece(plain_0, 3), piece(plain_1, 4),
        piece(plain_0, 0), piece(mirror_1, 0),
        piece(plain_0, 1), piece(stays_1, 0),
        piece(plain_0, 2), piece(mirror_0, 1),
        piece(plain_0, 4), piece(plain_1, 3),
        piece(mirror_1, 1), piece(plain_1, 2),
        piece(stays_0, 0), piece(plain_1, 1),
        piece(mirror_0, 0), piece(plain_1, 0)], axis=1)
    count = wide.shape[1]
    even = lax.rem(lax.broadcasted_iota(jnp.int32, (1, count), 1), 2 * ROWS) < ROWS
    swapped = jnp.where(even, pltpu.roll(wide, count - ROWS, 1), pltpu.roll(wide, ROWS, 1))
    value = pltpu.roll(jnp.where(y_lo == 0, wide, swapped), z * (2 * ROWS), 1)
    residual[0] = value
    update[0] = value / divisor[...]


def place(*parts):
    out = jax.ShapeDtypeStruct((1, ROWS, 16 * ROWS), F32)
    return pl.pallas_call(
        place_kernel,
        out_shape=(out, out),
        in_specs=full(7),
        out_specs=tuple(full(2)),
        compiler_params=params(),
        name="place",
    )(*parts)


def contraction_weights(amplitudes):
    plain = jnp.swapaxes(amplitudes, 1, 2).reshape(PAIRS, SLAB * SLAB)
    mirror = amplitudes.reshape(PAIRS, SLAB * SLAB)
    both = jnp.concatenate([plain, mirror], axis=0)
    column = np.arange(DEPTH)
    same = np.arange(GROUP)[:, None] == column[None, :] % GROUP
    chunks = []
    for chunk in range(2):
        source = column // (6 * GROUP) * SLAB + 6 * chunk + column // GROUP % 6
        spread = source[None, :] == np.arange(SLAB * SLAB)[:, None]
        wide = jnp.dot(both, jnp.asarray(spread, BF16), preferred_element_type=F32).astype(BF16)
        wide = jnp.where(jnp.asarray(same)[None], wide[:, None, :], jnp.zeros((), BF16))
        chunks.append(wide.reshape(2 * PAIRS * GROUP, DEPTH))
    return chunks


def per_device(factors, amplitudes, vir_energy, pair_energy):
    own = pack_block(factors)
    p1 = shift(own, dz=-1)
    m1 = shift(own, dz=1)
    weights = contraction_weights(amplitudes)
    p2 = shift(p1, dz=-1)
    m2 = shift(m1, dz=1)
    cross = shift(p2, dy=1)
    others = (m1, own, p1, m2, p2)
    raw, divisor = first_star(m2, others, weights, vir_energy, pair_energy)
    keep, send = second_star(cross, others, weights, raw)
    stay, one, two, three = add_cores(keep, shift(send, dc=1))
    keep, send = add_x(stay, shift(two, dx=2), shift(three, dx=-1), shift(one, dx=1))
    plain, mirror, stays, stays_other = sum_parts(keep, shift(send, dh=1))
    stays_other = shift(stays_other, dc=1)
    plain = to_rows(plain, ((-2, 0), (2, 1)))
    mirror = to_rows(mirror, ((-1, 0), (1, 0)))
    plain_other = shift(plain[1], dc=1)
    mirror_other = shift(mirror[1], dc=1)
    return place(plain, plain_other, mirror, mirror_other, stays, stays_other, divisor)


def solution(mesh):
    return jax.shard_map(
        per_device,
        mesh=mesh,
        in_specs=(P("row", None, "col"), P(), P(), P()),
        out_specs=(P("col", "row", None), P("col", "row", None)),
        check_vma=False,
    )
```

time: 75.1 us -> 70.1 us (0.933)
  the two profiles are of different devices: /device:TPU:6 before, /device:TPU:1 now
where the time goes in v2:
time: 70.1 us; the launch traced here: 69.8 us
  starting transfers between devices  29.7 us (42%)
  waiting for transfers between devices  24.5 us (35%)
  Pallas kernels  8.74 us (12%)
  local copies, waits for them, and re-layouts  3.79 us (5%)
  matrix products  2.13 us (3%)
  between operations  0.73 us (1%)
    ppermute x13, starting transfers between devices, shift(): return lax.ppermute(array, ('row', 'col'), pairs)  27.1 us
    ppermute x13, waiting for transfers between devices, shift(): return lax.ppermute(array, ('row', 'col'), pairs)  23 us
    pallas_call x1, Pallas kernels, first_star(): pl.pallas_call(first_kernel, out_shape=(jax.ShapeDtypeStruct((GROUPS, 2 *...  3.84 us
    pallas_call x1, Pallas kernels, second_star(): pl.pallas_call(second_kernel, out_shape=(jax.ShapeDtypeStruct(shape, F32)...  3.34 us
    ppermute x2, starting transfers between devices, to_rows(): return lax.ppermute(array, ('row', 'col'), pairs)  2.6 us
    dot_general x2, matrix products, contraction_weights(): jnp.dot(both, jnp.asarray(spread, BF16), preferred_element_type=F32)  2.13 us
    unnamed x8, local copies, waits for them, and re-layouts  1.83 us
    ppermute x2, waiting for transfers between devices, to_rows(): return lax.ppermute(array, ('row', 'col'), pairs)  1.52 us
  transfers between devices with their start and end apart: 15, of which 10 were waited for; matrix products, arithmetic and copies ran while one was open for 7% of the time, Pallas kernels for 5%

profile of v2, /device:TPU:1, one launch (start us, length us, event | category | flops | bytes accessed | tf_op | source)
XLA Modules:
  0.0 69.8 jit_solution(15117401238185632171)
XLA Ops:
  0.6 1.0 %copy-done = bf16[48,12,320]{2,0,1:T(8,128)(2,1)S(1)} copy-done((bf16[48,12,320]{2,0,1:T(8,128)(2,1)S(1)}, bf16[48,12,320]{2,0,1:T(8,128)(2,1)}, u32[]{:S(2)}) %copy-start) | copy-done | bytes 368664
  1.8 6.5 %collective-permute-start = (bf16[30,48,128]{2,1,0:T(8,128)(2,1)S(1)}, bf16[30,48,128]{2,1,0:T(8,128)(2,1)S(1)}, u32[]{:S(2)}, u32[]{:S(2)}) collective-permute-start(bf16[30,48,128]{2,1,0:T(8,128)(2,1)S(1)} %pack.1.own), channel_id=1, source_target_pairs={{0,224},{1,225},{2,226},{3,227},{4,228},{5,229},{6,230},{7,231},{8... | collective-permute-start | bytes 1105928 | tf_op jit(solution)/shard_map/ppermute | solution.py:37
  8.2 1.0 %copy.9 = bf16[16,12,12]{2,1,0:T(8,128)(2,1)S(1)} copy(bf16[16,12,12]{1,0,2:T(8,128)(2,1)} %bitcast.15) | data formatting | bytes 9216 | tf_op jit(solution)/shard_map/transpose | solution.py:310
  9.4 6.1 %collective-permute-done.p1 = bf16[30,48,128]{2,1,0:T(8,128)(2,1)S(1)} collective-permute-done((bf16[30,48,128]{2,1,0:T(8,128)(2,1)S(1)}, bf16[30,48,128]{2,1,0:T(8,128)(2,1)S(1)}, u32[]{:S(2)}, u32[]{:S(2)}) %collective-permute-start) | collective-permute-done | bytes 368672 | tf_op jit(solution)/shard_map/ppermute | solution.py:37
  15.5 3.4 %collective-permute-start.1 = (bf16[30,48,128]{2,1,0:T(8,128)(2,1)S(1)}, bf16[30,48,128]{2,1,0:T(8,128)(2,1)S(1)}, u32[]{:S(2)}, u32[]{:S(2)}) collective-permute-start(bf16[30,48,128]{2,1,0:T(8,128)(2,1)S(1)} %collective-permute-done.p1), channel_id=1, source_target_pairs={{0,224},{1,225},{2,226},{3,227},{4,228},{5,229},{6,230},{7,231},{8... | collective-permute-start | bytes 1105928 | tf_op jit(solution)/shard_map/ppermute | solution.py:37
  20.5 1.1 %convolution_convert_fusion = bf16[32,576]{1,0:T(8,128)(2,1)S(1)} fusion(bf16[32,144]{1,0:T(8,128)(2,1)S(1)} %constant_dynamic-update-slice_fusion, bf16[144,576]{1,0:T(8,128)(2,1)} %constant.10.clone), kind=kOutput, calls=%fused_computation | convolution fusion | flops 5326848 | bytes 211968 | tf_op jit(solution)/shard_map/dot_general | solution.py:319
  21.7 3.5 %collective-permute-done.1.p2 = bf16[30,48,128]{2,1,0:T(8,128)(2,1)S(1)} collective-permute-done((bf16[30,48,128]{2,1,0:T(8,128)(2,1)S(1)}, bf16[30,48,128]{2,1,0:T(8,128)(2,1)S(1)}, u32[]{:S(2)}, u32[]{:S(2)}) %collective-permute-start.1) | collective-permute-done | bytes 368672 | tf_op jit(solution)/shard_map/ppermute | solution.py:37
  25.2 1.3 %collective-permute-start.2 = (bf16[30,48,128]{2,1,0:T(8,128)(2,1)S(1)}, bf16[30,48,128]{2,1,0:T(8,128)(2,1)S(1)}, u32[]{:S(2)}, u32[]{:S(2)}) collective-permute-start(bf16[30,48,128]{2,1,0:T(8,128)(2,1)S(1)} %collective-permute-done.1.p2), channel_id=1, source_target_pairs={{0,16},{1,17},{2,18},{3,19},{4,20},{5,21},{6,22},{7,23},{8,24},{9,... | collective-permute-start | bytes 1105928 | tf_op jit(solution)/shard_map/ppermute | solution.py:37
  26.5 1.1 %convolution_convert_fusion.1 = bf16[32,576]{1,0:T(8,128)(2,1)S(1)} fusion(bf16[32,144]{1,0:T(8,128)(2,1)S(1)} %constant_dynamic-update-slice_fusion, bf16[144,576]{1,0:T(8,128)(2,1)} %constant.8.clone), kind=kOutput, calls=%fused_computation.1 | convolution fusion | flops 5326848 | bytes 211968 | tf_op jit(solution)/shard_map/dot_general | solution.py:319
  27.8 3.4 %collective-permute-done.4.center.m2 = bf16[30,48,128]{2,1,0:T(8,128)(2,1)S(1)} collective-permute-done((bf16[30,48,128]{2,1,0:T(8,128)(2,1)S(1)}, bf16[30,48,128]{2,1,0:T(8,128)(2,1)S(1)}, u32[]{:S(2)}, u32[]{:S(2)}) %collective-permute-start.4) | collective-permute-done | bytes 368672 | tf_op jit(solution)/shard_map/ppermute | solution.py:37
  31.2 3.8 %first_star.1 = (f32[6,256,256]{2,1,0:T(8,128)S(1)}, f32[48,768]{1,0:T(8,128)S(1)}) custom-call(bf16[30,48,128]{2,1,0:T(8,128)(2,1)S(1)} %collective-permute-done.4.center.m2, bf16[30,48,128]{2,1,0:T(8,128)(2,1)S(1)} %collective-permute-done.3.m1, bf16[30,48,128]{2,1,0:T(8,128)(2,1)S(1)} %pack.1.own, bf16[30,48,128]{2,1,0:T(8,128)(2,1)S(1)} %collective-permute-done.p1, ...), custom_call_target="tpu_custom_call" | custom-call | tf_op jit(solution)/shard_map/first_star/pallas_call | solution.py:175
  35.0 3.3 %second_star.1 = (f32[2,4,2,48,384]{4,3,2,1,0:T(8,128)S(1)}, bf16[2,4,2,48,384]{4,3,2,1,0:T(8,128)(2,1)S(1)}) custom-call(bf16[30,48,128]{2,1,0:T(8,128)(2,1)S(1)} %collective-permute-done.2.center, bf16[30,48,128]{2,1,0:T(8,128)(2,1)S(1)} %collective-permute-done.3.m1, bf16[30,48,128]{2,1,0:T(8,128)(2,1)S(1)} %pack.1.own, ...), custom_call_target="tpu_custom_call" | custom-call | tf_op jit(solution)/shard_map/second_star/pallas_call | solution.py:189
  38.4 2.8 %collective-permute-start.5 = (bf16[2,4,2,48,384]{4,3,2,1,0:T(8,128)(2,1)S(1)}, bf16[2,4,2,48,384]{4,3,2,1,0:T(8,128)(2,1)S(1)}, u32[]{:S(2)}, u32[]{:S(2)}) collective-permute-start(bf16[2,4,2,48,384]{4,3,2,1,0:T(8,128)(2,1)S(1)} %get-tuple-element.18), channel_id=1, source_target_pairs={{0,1},{1,0},{2,3},{3,2},{4,5},{5,4},{6,7},{7,6},{8,9},{9,8},{10,11... | collective-permute-start | bytes 1769480 | tf_op jit(solution)/shard_map/ppermute | solution.py:37
  41.2 1.6 %collective-permute-done.5.got = bf16[2,4,2,48,384]{4,3,2,1,0:T(8,128)(2,1)S(1)} collective-permute-done((bf16[2,4,2,48,384]{4,3,2,1,0:T(8,128)(2,1)S(1)}, bf16[2,4,2,48,384]{4,3,2,1,0:T(8,128)(2,1)S(1)}, u32[]{:S(2)}, u32[]{:S(2)}) %collective-permute-start.5) | collective-permute-done | bytes 589856 | tf_op jit(solution)/shard_map/ppermute | solution.py:37
  43.0 2.8 %collective-permute-start.6 = (bf16[2,2,48,384]{3,2,1,0:T(8,128)(2,1)S(1)}, bf16[2,2,48,384]{3,2,1,0:T(8,128)(2,1)S(1)}, u32[]{:S(2)}, u32[]{:S(2)}) collective-permute-start(bf16[2,2,48,384]{3,2,1,0:T(8,128)(2,1)S(1)} %get-tuple-element.20), channel_id=1, source_target_pairs={{0,4},{1,5},{2,6},{3,7},{4,0},{5,1},{6,2},{7,3},{8,12},{9,13},{10,... | collective-permute-start | bytes 442376 | tf_op jit(solution)/shard_map/ppermute | solution.py:37
  47.2 2.4 %collective-permute-done.6.two = bf16[2,2,48,384]{3,2,1,0:T(8,128)(2,1)S(1)} collective-permute-done((bf16[2,2,48,384]{3,2,1,0:T(8,128)(2,1)S(1)}, bf16[2,2,48,384]{3,2,1,0:T(8,128)(2,1)S(1)}, u32[]{:S(2)}, u32[]{:S(2)}) %collective-permute-start.6) | collective-permute-done | bytes 147488 | tf_op jit(solution)/shard_map/ppermute | solution.py:37
  49.6 3.2 %collective-permute-done.7.three = bf16[2,2,48,384]{3,2,1,0:T(8,128)(2,1)S(1)} collective-permute-done((bf16[2,2,48,384]{3,2,1,0:T(8,128)(2,1)S(1)}, bf16[2,2,48,384]{3,2,1,0:T(8,128)(2,1)S(1)}, u32[]{:S(2)}, u32[]{:S(2)}) %collective-permute-start.7) | collective-permute-done | bytes 147488 | tf_op jit(solution)/shard_map/ppermute | solution.py:37
  53.0 3.0 %collective-permute-start.9 = (bf16[2,48,384]{2,1,0:T(8,128)(2,1)S(1)}, bf16[2,48,384]{2,1,0:T(8,128)(2,1)S(1)}, u32[]{:S(2)}, u32[]{:S(2)}) collective-permute-start(bf16[2,48,384]{2,1,0:T(8,128)(2,1)S(1)} %get-tuple-element.24), channel_id=1, source_target_pairs={{0,8},{1,9},{2,10},{3,11},{4,12},{5,13},{6,14},{7,15},{8,0},{9,1},... | collective-permute-start | bytes 221192 | tf_op jit(solution)/shard_map/ppermute | solution.py:37
  56.0 1.8 %collective-permute-done.9.got = bf16[2,48,384]{2,1,0:T(8,128)(2,1)S(1)} collective-permute-done((bf16[2,48,384]{2,1,0:T(8,128)(2,1)S(1)}, bf16[2,48,384]{2,1,0:T(8,128)(2,1)S(1)}, u32[]{:S(2)}, u32[]{:S(2)}) %collective-permute-start.9) | collective-permute-done | bytes 73760 | tf_op jit(solution)/shard_map/ppermute | solution.py:37
  58.2 3.5 %collective-permute-start.14 = (f32[48,128]{1,0:T(8,128)S(1)}, f32[48,128]{1,0:T(8,128)S(1)}, u32[]{:S(2)}, u32[]{:S(2)}) collective-permute-start(f32[48,128]{1,0:T(8,128)S(1)} %get-tuple-element.28), channel_id=1, source_target_pairs={{0,1},{1,0},{2,3},{3,2},{4,5},{5,4},{6,7},{7,6},{8,9},{9,8},{10,11... | collective-permute-start | bytes 73736 | tf_op jit(solution)/shard_map/ppermute | solution.py:37
  61.7 2.4 %collective-permute-start.12 = (f32[2,48,128]{2,1,0:T(8,128)S(1)}, f32[2,48,128]{2,1,0:T(8,128)S(1)}, u32[]{:S(2)}, u32[]{:S(2)}) collective-permute-start(f32[2,48,128]{2,1,0:T(8,128)S(1)} %get-tuple-element.26), channel_id=1, source_target_pairs={{0,224},{1,33},{2,226},{3,35},{4,228},{5,37},{6,230},{7,39},{8,232... | collective-permute-start | bytes 147464 | tf_op jit(solution)/shard_map/ppermute | solution.py:46
  64.1 1.5 %collective-permute-done.10.plain = f32[2,48,256]{2,1,0:T(8,128)S(1)} collective-permute-done((f32[2,48,256]{2,1,0:T(8,128)S(1)}, f32[2,48,256]{2,1,0:T(8,128)S(1)}, u32[]{:S(2)}, u32[]{:S(2)}) %collective-permute-start.10) | collective-permute-done | bytes 98336 | tf_op jit(solution)/shard_map/ppermute | solution.py:46
  66.3 1.5 %collective-permute-start.13 = (f32[48,128]{1,0:T(8,128)S(1)}, f32[48,128]{1,0:T(8,128)S(1)}, u32[]{:S(2)}, u32[]{:S(2)}) collective-permute-start(f32[48,128]{1,0:T(8,128)S(1)} %slice_bitcast_fusion.1), channel_id=1, source_target_pairs={{0,1},{1,0},{2,3},{3,2},{4,5},{5,4},{6,7},{7,6},{8,9},{9,8},{10,11... | collective-permute-start | bytes 73736 | tf_op jit(solution)/shard_map/ppermute | solution.py:37
  68.7 1.1 %place.1 = (f32[1,48,768]{2,1,0:T(8,128)}, f32[1,48,768]{2,1,0:T(8,128)}) custom-call(f32[2,48,256]{2,1,0:T(8,128)S(1)} %collective-permute-done.10.plain, f32[48,256]{1,0:T(8,128)S(1)} %collective-permute-done.11.plain_other, f32[2,48,128]{2,1,0:T(8,128)S(1)} %collective-permute-done.12.mirror, f32[48,128]{1,0:T(8,128)S(1)} %collective-permute-done.13.mirror_other, ...), custom_call_target="tpu_custom_call" | custom-call | tf_op jit(solution)/shard_map/place/pallas_call | solution.py:299
  (31 shorter events, 5.7 us)
Async XLA Ops:
  0.6 30.5 %copy-start.1 = (f32[16]{0:T(128)S(1)}, f32[16]{0:T(128)}, u32[]{:S(2)}) copy-start(f32[16]{0:T(128)} %pair.1) | copy-start | bytes 196
  0.6 1.0 %copy-start = (bf16[48,12,320]{2,0,1:T(8,128)(2,1)S(1)}, bf16[48,12,320]{2,0,1:T(8,128)(2,1)}, u32[]{:S(2)}) copy-start(bf16[48,12,320]{2,0,1:T(8,128)(2,1)} %param.7) | copy-start | bytes 1105924
  1.7 25.9 %copy-start.2 = (pred[8,576]{1,0:T(8,128)(4,1)S(1)}, pred[8,576]{1,0:T(8,128)(4,1)}, u32[]{:S(2)}) copy-start(pred[8,576]{1,0:T(8,128)(4,1)} %constant.9.clone) | copy-start | bytes 13828
  1.8 13.7 %collective-permute-start = (bf16[30,48,128]{2,1,0:T(8,128)(2,1)S(1)}, bf16[30,48,128]{2,1,0:T(8,128)(2,1)S(1)}, u32[]{:S(2)}, u32[]{:S(2)}) collective-permute-start(bf16[30,48,128]{2,1,0:T(8,128)(2,1)S(1)} %pack.1.own), channel_id=1, source_target_pairs={{0,224},{1,225},{2,226},{3,227},{4,228},{5,229},{6,230},{7,231},{8... | collective-permute-start | bytes 1105928 | tf_op jit(solution)/shard_map/ppermute | solution.py:37
  8.2 13.4 %collective-permute-start.3 = (bf16[30,48,128]{2,1,0:T(8,128)(2,1)S(1)}, bf16[30,48,128]{2,1,0:T(8,128)(2,1)S(1)}, u32[]{:S(2)}, u32[]{:S(2)}) collective-permute-start(bf16[30,48,128]{2,1,0:T(8,128)(2,1)S(1)} %pack.1.own), channel_id=1, source_target_pairs={{0,32},{1,33},{2,34},{3,35},{4,36},{5,37},{6,38},{7,39},{8,40},{9,... | collective-permute-start | bytes 1105928 | tf_op jit(solution)/shard_map/ppermute | solution.py:37
  15.5 9.7 %collective-permute-start.1 = (bf16[30,48,128]{2,1,0:T(8,128)(2,1)S(1)}, bf16[30,48,128]{2,1,0:T(8,128)(2,1)S(1)}, u32[]{:S(2)}, u32[]{:S(2)}) collective-permute-start(bf16[30,48,128]{2,1,0:T(8,128)(2,1)S(1)} %collective-permute-done.p1), channel_id=1, source_target_pairs={{0,224},{1,225},{2,226},{3,227},{4,228},{5,229},{6,230},{7,231},{8... | collective-permute-start | bytes 1105928 | tf_op jit(solution)/shard_map/ppermute | solution.py:37
  21.6 9.5 %collective-permute-start.4 = (bf16[30,48,128]{2,1,0:T(8,128)(2,1)S(1)}, bf16[30,48,128]{2,1,0:T(8,128)(2,1)S(1)}, u32[]{:S(2)}, u32[]{:S(2)}) collective-permute-start(bf16[30,48,128]{2,1,0:T(8,128)(2,1)S(1)} %collective-permute-done.3.m1), channel_id=1, source_target_pairs={{0,32},{1,33},{2,34},{3,35},{4,36},{5,37},{6,38},{7,39},{8,40},{9,... | collective-permute-start | bytes 1105928 | tf_op jit(solution)/shard_map/ppermute | solution.py:37
  25.2 9.8 %collective-permute-start.2 = (bf16[30,48,128]{2,1,0:T(8,128)(2,1)S(1)}, bf16[30,48,128]{2,1,0:T(8,128)(2,1)S(1)}, u32[]{:S(2)}, u32[]{:S(2)}) collective-permute-start(bf16[30,48,128]{2,1,0:T(8,128)(2,1)S(1)} %collective-permute-done.1.p2), channel_id=1, source_target_pairs={{0,16},{1,17},{2,18},{3,19},{4,20},{5,21},{6,22},{7,23},{8,24},{9,... | collective-permute-start | bytes 1105928 | tf_op jit(solution)/shard_map/ppermute | solution.py:37
  38.4 4.5 %collective-permute-start.5 = (bf16[2,4,2,48,384]{4,3,2,1,0:T(8,128)(2,1)S(1)}, bf16[2,4,2,48,384]{4,3,2,1,0:T(8,128)(2,1)S(1)}, u32[]{:S(2)}, u32[]{:S(2)}) collective-permute-start(bf16[2,4,2,48,384]{4,3,2,1,0:T(8,128)(2,1)S(1)} %get-tuple-element.18), channel_id=1, source_target_pairs={{0,1},{1,0},{2,3},{3,2},{4,5},{5,4},{6,7},{7,6},{8,9},{9,8},{10,11... | collective-permute-start | bytes 1769480 | tf_op jit(solution)/shard_map/ppermute | solution.py:37
  43.0 6.7 %collective-permute-start.6 = (bf16[2,2,48,384]{3,2,1,0:T(8,128)(2,1)S(1)}, bf16[2,2,48,384]{3,2,1,0:T(8,128)(2,1)S(1)}, u32[]{:S(2)}, u32[]{:S(2)}) collective-permute-start(bf16[2,2,48,384]{3,2,1,0:T(8,128)(2,1)S(1)} %get-tuple-element.20), channel_id=1, source_target_pairs={{0,4},{1,5},{2,6},{3,7},{4,0},{5,1},{6,2},{7,3},{8,12},{9,13},{10,... | collective-permute-start | bytes 442376 | tf_op jit(solution)/shard_map/ppermute | solution.py:37
  45.8 7.1 %collective-permute-start.7 = (bf16[2,2,48,384]{3,2,1,0:T(8,128)(2,1)S(1)}, bf16[2,2,48,384]{3,2,1,0:T(8,128)(2,1)S(1)}, u32[]{:S(2)}, u32[]{:S(2)}) collective-permute-start(bf16[2,2,48,384]{3,2,1,0:T(8,128)(2,1)S(1)} %get-tuple-element.21), channel_id=1, source_target_pairs={{0,6},{1,7},{2,0},{3,1},{4,2},{5,3},{6,4},{7,5},{8,14},{9,15},{10,... | collective-permute-start | bytes 442376 | tf_op jit(solution)/shard_map/ppermute | solution.py:37
  46.7 6.3 %collective-permute-start.8 = (bf16[2,2,48,384]{3,2,1,0:T(8,128)(2,1)S(1)}, bf16[2,2,48,384]{3,2,1,0:T(8,128)(2,1)S(1)}, u32[]{:S(2)}, u32[]{:S(2)}) collective-permute-start(bf16[2,2,48,384]{3,2,1,0:T(8,128)(2,1)S(1)} %get-tuple-element.22), channel_id=1, source_target_pairs={{0,2},{1,3},{2,4},{3,5},{4,6},{5,7},{6,0},{7,1},{8,10},{9,11},{10,... | collective-permute-start | bytes 442376 | tf_op jit(solution)/shard_map/ppermute | solution.py:37
  53.0 4.8 %collective-permute-start.9 = (bf16[2,48,384]{2,1,0:T(8,128)(2,1)S(1)}, bf16[2,48,384]{2,1,0:T(8,128)(2,1)S(1)}, u32[]{:S(2)}, u32[]{:S(2)}) collective-permute-start(bf16[2,48,384]{2,1,0:T(8,128)(2,1)S(1)} %get-tuple-element.24), channel_id=1, source_target_pairs={{0,8},{1,9},{2,10},{3,11},{4,12},{5,13},{6,14},{7,15},{8,0},{9,1},... | collective-permute-start | bytes 221192 | tf_op jit(solution)/shard_map/ppermute | solution.py:37
  58.0 7.6 %collective-permute-start.10 = (f32[2,48,256]{2,1,0:T(8,128)S(1)}, f32[2,48,256]{2,1,0:T(8,128)S(1)}, u32[]{:S(2)}, u32[]{:S(2)}) collective-permute-start(f32[2,48,256]{2,1,0:T(8,128)S(1)} %get-tuple-element.25), channel_id=1, source_target_pairs={{0,192},{1,81},{2,194},{3,83},{4,196},{5,85},{6,198},{7,87},{8,200... | collective-permute-start | bytes 294920 | tf_op jit(solution)/shard_map/ppermute | solution.py:46
  58.2 9.6 %collective-permute-start.14 = (f32[48,128]{1,0:T(8,128)S(1)}, f32[48,128]{1,0:T(8,128)S(1)}, u32[]{:S(2)}, u32[]{:S(2)}) collective-permute-start(f32[48,128]{1,0:T(8,128)S(1)} %get-tuple-element.28), channel_id=1, source_target_pairs={{0,1},{1,0},{2,3},{3,2},{4,5},{5,4},{6,7},{7,6},{8,9},{9,8},{10,11... | collective-permute-start | bytes 73736 | tf_op jit(solution)/shard_map/ppermute | solution.py:37
  61.7 4.6 %collective-permute-start.12 = (f32[2,48,128]{2,1,0:T(8,128)S(1)}, f32[2,48,128]{2,1,0:T(8,128)S(1)}, u32[]{:S(2)}, u32[]{:S(2)}) collective-permute-start(f32[2,48,128]{2,1,0:T(8,128)S(1)} %get-tuple-element.26), channel_id=1, source_target_pairs={{0,224},{1,33},{2,226},{3,35},{4,228},{5,37},{6,230},{7,39},{8,232... | collective-permute-start | bytes 147464 | tf_op jit(solution)/shard_map/ppermute | solution.py:46
  65.6 3.1 %collective-permute-start.11 = (f32[48,256]{1,0:T(8,128)S(1)}, f32[48,256]{1,0:T(8,128)S(1)}, u32[]{:S(2)}, u32[]{:S(2)}) collective-permute-start(f32[48,256]{1,0:T(8,128)S(1)} %slice_bitcast_fusion), channel_id=1, source_target_pairs={{0,1},{1,0},{2,3},{3,2},{4,5},{5,4},{6,7},{7,6},{8,9},{9,8},{10,11... | collective-permute-start | bytes 147464 | tf_op jit(solution)/shard_map/ppermute | solution.py:37
  66.3 2.4 %collective-permute-start.13 = (f32[48,128]{1,0:T(8,128)S(1)}, f32[48,128]{1,0:T(8,128)S(1)}, u32[]{:S(2)}, u32[]{:S(2)}) collective-permute-start(f32[48,128]{1,0:T(8,128)S(1)} %slice_bitcast_fusion.1), channel_id=1, source_target_pairs={{0,1},{1,0},{2,3},{3,2},{4,5},{5,4},{6,7},{7,6},{8,9},{9,8},{10,11... | collective-permute-start | bytes 73736 | tf_op jit(solution)/shard_map/ppermute | solution.py:37

commit v3 on v2

--- a/solution.py
+++ b/solution.py
@@ -14,7 +14,7 @@
 CHUNK = 15
 GROUP = 8
 GROUPS = ROWS // GROUP
-DEPTH = SLAB * SLAB * GROUP // 2
+DEPTH = SLAB * SLAB * GROUP
 OUT = 3 * LANE
 BF16 = jnp.bfloat16
 F32 = jnp.float32
@@ -101,7 +101,7 @@
 
 
 def build_products(left, near, own, far, m2, p2, products):
-    rows = 6 * GROUP
+    rows = SLAB * GROUP
     for d in range(SLAB):
         columns = []
         first, second, last, half = tiles_of(d)
@@ -110,19 +110,13 @@
                 [near[tile], own[tile], far[tile], m2[tile], p2[tile], far[tile, 32:, :]], axis=0))
         right = jnp.concatenate(columns, axis=1)
         block = lax.dot_general(left[half], right, (((1,), (1,)), ((), ())), preferred_element_type=F32)
-        block = block.reshape(2, 6, GROUPS, GROUP, WIDE)
-        for chunk in range(2):
-            for g in range(GROUPS):
-                part = block[chunk, :, g].reshape(rows, WIDE)
-                products[chunk, g, d * rows:(d + 1) * rows, :] = part.astype(BF16)
-
-
-def contract(one, two, products, g):
-    return (jnp.dot(one[...], products[0, g], preferred_element_type=F32)
-            + jnp.dot(two[...], products[1, g], preferred_element_type=F32))
-
-
-def first_kernel(center, m1, own, p1, m2, p2, one, two, energy, pair, raw, divisor, left, products):
+        block = block.reshape(SLAB, GROUPS, GROUP, WIDE)
+        for g in range(GROUPS):
+            part = block[:, g].reshape(rows, WIDE)
+            products[g, d * rows:(d + 1) * rows, :] = part.astype(BF16)
+
+
+def first_kernel(center, m1, own, p1, m2, p2, weights, energy, pair, raw, divisor, left, products):
     shape = divisor.shape
     second = jnp.broadcast_to(energy[...], shape)
     row = lax.axis_index("row") * ROWS + lax.broadcasted_iota(jnp.int32, shape, 0)
@@ -132,20 +126,24 @@
     build_left(center, left)
     build_products(left, m1, own, p1, m2, p2, products)
     for g in range(GROUPS):
-        raw[g] = contract(one, two, products, g)
-
-
-def second_kernel(center, m1, own, p1, m2, p2, one, two, raw, keep, send, left, products):
+        raw[g] = jnp.dot(weights[...], products[g], preferred_element_type=F32)
+
+
+def second_kernel(center, m1, own, p1, m2, p2, weights, raw, keep_far, send_far, keep_near, send_near, left, products):
     build_left(center, left)
     build_products(left, p1, own, m1, m2, p2, products)
     half = PAIRS * GROUP
     lane = lax.broadcasted_iota(jnp.int32, (half, LANE), 1)
+    wide = lax.broadcasted_iota(jnp.int32, (2, 4, GROUP, LANE), 3)
+    inner = (wide >= ROWS) & (wide < 2 * ROWS)
     here = core_here() == 0
+    first_half = lax.div(lax.axis_index("col"), 8) == 0
     shape = (2, 4, 2, GROUP, LANE)
+    outs = ((keep_far, send_far), (keep_near, send_near))
     for g in range(0, GROUPS, 2):
-        staying, going = [], []
+        held = [[], []]
         for step in range(2):
-            mine = contract(one, two, products, g + step)
+            mine = jnp.dot(weights[...], products[g + step], preferred_element_type=F32)
             other = raw[g + step]
             for at, inside in enumerate((LANE, 5 * ROWS - LANE, 2 * ROWS)):
                 lanes = slice(LANE, WIDE) if at == 1 else slice(0, LANE)
@@ -155,19 +153,29 @@
                 if at > 0:
                     down, up = (jnp.where(lane < inside, down, mine[back, lanes]),
                                 jnp.where(lane < inside, up, other[back, lanes]))
-                staying.append(jnp.where(here, down, up).reshape(shape))
-                going.append(jnp.where(here, up, down).reshape(shape))
+                down, up = down.reshape(shape), up.reshape(shape)
+                if at == 2:
+                    down, up = (
+                        jnp.stack([down[:, :, 0], jnp.where(inner, up[:, :, 0], down[:, :, 1])], axis=2),
+                        jnp.stack([jnp.where(inner, up[:, :, 1], up[:, :, 0]),
+                                   jnp.where(inner, down[:, :, 1], up[:, :, 1])], axis=2))
+                held[0].append(jnp.where(here, down, up))
+                held[1].append(jnp.where(here, up, down))
         rows = pl.ds(g * GROUP, 2 * GROUP)
-        for at in range(3):
-            lanes = pl.ds(at * LANE, LANE)
-            keep[:, :, :, rows, lanes] = jnp.concatenate([staying[at], staying[3 + at]], axis=3)
-            send[:, :, :, rows, lanes] = jnp.concatenate([going[at], going[3 + at]], axis=3).astype(BF16)
+        for way in range(2):
+            for at in range(3):
+                lanes = pl.ds(at * LANE, LANE)
+                value = jnp.concatenate([held[way][at], held[way][3 + at]], axis=3)
+                near = jnp.where(first_half, value[0], value[1])
+                far = jnp.where(first_half, value[1], value[0])
+                for out, part in ((outs[0][way], far), (outs[1][way], near)):
+                    out[:, :, rows, lanes] = part.astype(out.dtype)
 
 
 def scratch():
     return [
         pltpu.VMEM((2, SLAB * ROWS, 3 * LANE), BF16),
-        pltpu.VMEM((2, GROUPS, DEPTH, WIDE), BF16),
+        pltpu.VMEM((GROUPS, DEPTH, WIDE), BF16),
     ]
 
 
@@ -176,36 +184,37 @@
         first_kernel,
         out_shape=(jax.ShapeDtypeStruct((GROUPS, 2 * PAIRS * GROUP, WIDE), F32),
                    jax.ShapeDtypeStruct((ROWS, 16 * ROWS), F32)),
-        in_specs=full(9) + [pl.BlockSpec(memory_space=pltpu.SMEM)],
+        in_specs=full(8) + [pl.BlockSpec(memory_space=pltpu.SMEM)],
         out_specs=tuple(full(2)),
         scratch_shapes=scratch(),
         compiler_params=params(),
         name="first_star",
-    )(center, *others, *weights, vir_energy[None, :], pair_energy)
+    )(center, *others, weights, vir_energy[None, :], pair_energy)
 
 
 def second_star(center, others, weights, raw):
-    shape = (2, 4, 2, ROWS, OUT)
+    shape = (4, 2, ROWS, OUT)
+    half = (jax.ShapeDtypeStruct(shape, F32), jax.ShapeDtypeStruct(shape, BF16))
     return pl.pallas_call(
         second_kernel,
-        out_shape=(jax.ShapeDtypeStruct(shape, F32), jax.ShapeDtypeStruct(shape, BF16)),
-        in_specs=full(9),
-        out_specs=tuple(full(2)),
+        out_shape=half + half,
+        in_specs=full(8),
+        out_specs=tuple(full(4)),
         scratch_shapes=scratch(),
         compiler_params=params(),
         name="second_star",
-    )(center, *others, *weights, raw)
-
-
-def core_kernel(keep, got, stay, one, two, three):
+    )(center, *others, weights, raw)
+
+
+def core_kernel(keep, got, *outs):
     x = lax.rem(lax.div(lax.axis_index("col"), 2), 4)
-    for step, out in enumerate((stay, one, two, three)):
+    for step, out in enumerate(outs):
         at = lax.rem(x + step, 4)
-        out[...] = (keep[:, at] + got[:, at].astype(F32)).astype(out.dtype)
+        out[...] = (keep[at] + got[at].astype(F32)).astype(out.dtype)
 
 
 def add_cores(keep, got):
-    shape = (2, 2, ROWS, OUT)
+    shape = (2, ROWS, OUT)
     return pl.pallas_call(
         core_kernel,
         out_shape=(jax.ShapeDtypeStruct(shape, F32),) + (jax.ShapeDtypeStruct(shape, BF16),) * 3,
@@ -216,29 +225,31 @@
     )(keep, got)
 
 
-def x_kernel(stay, two, three, one, keep, send):
-    y_hi = lax.div(lax.axis_index("col"), 8)
-    for at, out in ((y_hi, keep), (1 - y_hi, send)):
-        total = stay[at] + one[at].astype(F32) + two[at].astype(F32) + three[at].astype(F32)
-        out[...] = total.astype(out.dtype)
+def x_kernel(stay, two, three, one, send):
+    total = stay[...] + one[...].astype(F32) + two[...].astype(F32) + three[...].astype(F32)
+    send[...] = total.astype(BF16)
 
 
 def add_x(*parts):
-    shape = (2, ROWS, OUT)
     return pl.pallas_call(
         x_kernel,
-        out_shape=(jax.ShapeDtypeStruct(shape, F32), jax.ShapeDtypeStruct(shape, BF16)),
+        out_shape=jax.ShapeDtypeStruct((2, ROWS, OUT), BF16),
         in_specs=full(4),
-        out_specs=tuple(full(2)),
+        out_specs=full(1)[0],
         compiler_params=params(),
         name="add_x",
     )(*parts)
 
 
-def sum_kernel(keep, got, plain, mirror, stays, stays_other):
+def sum_kernel(stay, two, three, one, got, plain, mirror, stays, stays_other):
     lane = lax.broadcasted_iota(jnp.int32, (ROWS, LANE), 1)
     pad = jnp.zeros((LANE - 2 * ROWS, LANE), F32)
-    totals = [keep[pair] + got[pair].astype(F32) for pair in range(2)]
+    totals = []
+    for pair in range(2):
+        total = stay[pair]
+        for part in (one, two, three, got):
+            total = total + part[pair].astype(F32)
+        totals.append(total)
     here = core_here() == 0
     ordered = (jnp.where(here, totals[0], totals[1]), jnp.where(here, totals[1], totals[0]))
     for at, total in enumerate(ordered):
@@ -250,16 +261,16 @@
         (stays, stays_other)[at][...] = turned[ROWS:2 * ROWS]
 
 
-def sum_parts(keep, got):
+def sum_parts(*parts):
     slim = jax.ShapeDtypeStruct((ROWS, LANE), F32)
     return pl.pallas_call(
         sum_kernel,
         out_shape=(jax.ShapeDtypeStruct((2, ROWS, WIDE), F32), jax.ShapeDtypeStruct((2, ROWS, LANE), F32), slim, slim),
-        in_specs=full(2),
+        in_specs=full(5),
         out_specs=tuple(full(4)),
         compiler_params=params(),
         name="sum_parts",
-    )(keep, got)
+    )(*parts)
 
 
 def place_kernel(plain, plain_other, mirror, mirror_other, stays, stays_other, divisor, residual, update):
@@ -272,7 +283,7 @@
 
     plain_0, plain_1 = both(plain[0], plain_other[...])
     mirror_0, mirror_1 = both(mirror[0], mirror_other[...])
-    stays_0, stays_1 = both(stays[...], stays_other[...])
+    stays_0, stays_1 = stays[...], stays_other[...]
 
     def piece(array, at):
         return array[:, at * ROWS:(at + 1) * ROWS]
@@ -312,14 +323,10 @@
     both = jnp.concatenate([plain, mirror], axis=0)
     column = np.arange(DEPTH)
     same = np.arange(GROUP)[:, None] == column[None, :] % GROUP
-    chunks = []
-    for chunk in range(2):
-        source = column // (6 * GROUP) * SLAB + 6 * chunk + column // GROUP % 6
-        spread = source[None, :] == np.arange(SLAB * SLAB)[:, None]
-        wide = jnp.dot(both, jnp.asarray(spread, BF16), preferred_element_type=F32).astype(BF16)
-        wide = jnp.where(jnp.asarray(same)[None], wide[:, None, :], jnp.zeros((), BF16))
-        chunks.append(wide.reshape(2 * PAIRS * GROUP, DEPTH))
-    return chunks
+    spread = column[None, :] // GROUP == np.arange(SLAB * SLAB)[:, None]
+    wide = jnp.dot(both, jnp.asarray(spread, BF16), preferred_element_type=F32).astype(BF16)
+    wide = jnp.where(jnp.asarray(same)[None], wide[:, None, :], jnp.zeros((), BF16))
+    return wide.reshape(2 * PAIRS * GROUP, DEPTH)
 
 
 def per_device(factors, amplitudes, vir_energy, pair_energy):
@@ -332,11 +339,15 @@
     cross = shift(p2, dy=1)
     others = (m1, own, p1, m2, p2)
     raw, divisor = first_star(m2, others, weights, vir_energy, pair_energy)
-    keep, send = second_star(cross, others, weights, raw)
-    stay, one, two, three = add_cores(keep, shift(send, dc=1))
-    keep, send = add_x(stay, shift(two, dx=2), shift(three, dx=-1), shift(one, dx=1))
-    plain, mirror, stays, stays_other = sum_parts(keep, shift(send, dh=1))
-    stays_other = shift(stays_other, dc=1)
+    keep_far, send_far, keep_near, send_near = second_star(cross, others, weights, raw)
+    far = add_cores(keep_far, shift(send_far, dc=1))
+    near = add_cores(keep_near, shift(send_near, dc=1))
+
+    def along_x(stay, one, two, three):
+        return stay, shift(two, dx=2), shift(three, dx=-1), shift(one, dx=1)
+
+    got = shift(add_x(*along_x(*far)), dh=1)
+    plain, mirror, stays, stays_other = sum_parts(*along_x(*near), got)
     plain = to_rows(plain, ((-2, 0), (2, 1)))
     mirror = to_rows(mirror, ((-1, 0), (1, 0)))
     plain_other = shift(plain[1], dc=1)

time: 70.1 us -> 69.3 us (0.989)
  matrix products: 2.13 us -> 1.14 us
  waiting for transfers between devices: 24.5 us -> 25.3 us
    ppermute x2, waiting for transfers between devices: 1.52 us -> 5.37 us  [to_rows(): return lax.ppermute(array, ('row', 'col'), pairs)]
    ppermute x13 -> x16, waiting for transfers between devices: 23 us -> 20 us  [shift(): return lax.ppermute(array, ('row', 'col'), pairs)]
    dot_general x2 -> x1, matrix products: 2.13 us -> 1.14 us  [contraction_weights(): jnp.dot(both, jnp.asarray(spread, BF16), preferred_element_type=F32)]
    ppermute x2, starting transfers between devices: 2.6 us -> 1.65 us  [to_rows(): return lax.ppermute(array, ('row', 'col'), pairs)]
    ppermute x13 -> x16, starting transfers between devices: 27.1 us -> 27.9 us  [shift(): return lax.ppermute(array, ('row', 'col'), pairs)]
    unnamed x8 -> x7, local copies, waits for them, and re-layouts: 1.83 us -> 1.83 us
  transfers between devices with their start and end apart: 15 -> 18, of which waited for: 10 -> 9; matrix products, arithmetic and copies ran while one was open for 7% -> 6% of each run, Pallas kernels for 5% -> 5%
where the time goes in v3:
time: 69.3 us; the launch traced here: 69 us
  starting transfers between devices  29.5 us (43%)
  waiting for transfers between devices  25.3 us (37%)
  Pallas kernels  8.36 us (12%)
  local copies, waits for them, and re-layouts  3.78 us (5%)
  matrix products  1.14 us (2%)
  between operations  0.74 us (1%)
    ppermute x16, starting transfers between devices, shift(): return lax.ppermute(array, ('row', 'col'), pairs)  27.9 us
    ppermute x16, waiting for transfers between devices, shift(): return lax.ppermute(array, ('row', 'col'), pairs)  20 us
    ppermute x2, waiting for transfers between devices, to_rows(): return lax.ppermute(array, ('row', 'col'), pairs)  5.37 us
    pallas_call x1, Pallas kernels, first_star(): pl.pallas_call(first_kernel, out_shape=(jax.ShapeDtypeStruct((GROUPS, 2 *...  3.61 us
    pallas_call x1, Pallas kernels, second_star(): pl.pallas_call(second_kernel, out_shape=half + half, in_specs=full(8), ou...  3.21 us
    unnamed x7, local copies, waits for them, and re-layouts  1.83 us
    ppermute x2, starting transfers between devices, to_rows(): return lax.ppermute(array, ('row', 'col'), pairs)  1.65 us
  transfers between devices with their start and end apart: 18, of which 9 were waited for; matrix products, arithmetic and copies ran while one was open for 6% of the time, Pallas kernels for 5%

profile of v3, /device:TPU:1, one launch (start us, length us, event | category | flops | bytes accessed | tf_op | source)
XLA Modules:
  0.0 69.0 jit_solution(2985405523823651305)
XLA Ops:
  0.6 1.0 %copy-done = bf16[48,12,320]{2,0,1:T(8,128)(2,1)S(1)} copy-done((bf16[48,12,320]{2,0,1:T(8,128)(2,1)S(1)}, bf16[48,12,320]{2,0,1:T(8,128)(2,1)}, u32[]{:S(2)}) %copy-start) | copy-done | bytes 368664
  1.8 6.5 %collective-permute-start = (bf16[30,48,128]{2,1,0:T(8,128)(2,1)S(1)}, bf16[30,48,128]{2,1,0:T(8,128)(2,1)S(1)}, u32[]{:S(2)}, u32[]{:S(2)}) collective-permute-start(bf16[30,48,128]{2,1,0:T(8,128)(2,1)S(1)} %pack.1.own), channel_id=1, source_target_pairs={{0,224},{1,225},{2,226},{3,227},{4,228},{5,229},{6,230},{7,231},{8... | collective-permute-start | bytes 1105928 | tf_op jit(solution)/shard_map/ppermute | solution.py:37
  8.2 7.3 %collective-permute-done.p1 = bf16[30,48,128]{2,1,0:T(8,128)(2,1)S(1)} collective-permute-done((bf16[30,48,128]{2,1,0:T(8,128)(2,1)S(1)}, bf16[30,48,128]{2,1,0:T(8,128)(2,1)S(1)}, u32[]{:S(2)}, u32[]{:S(2)}) %collective-permute-start) | collective-permute-done | bytes 368672 | tf_op jit(solution)/shard_map/ppermute | solution.py:37
  15.5 3.4 %collective-permute-start.1 = (bf16[30,48,128]{2,1,0:T(8,128)(2,1)S(1)}, bf16[30,48,128]{2,1,0:T(8,128)(2,1)S(1)}, u32[]{:S(2)}, u32[]{:S(2)}) collective-permute-start(bf16[30,48,128]{2,1,0:T(8,128)(2,1)S(1)} %collective-permute-done.p1), channel_id=1, source_target_pairs={{0,224},{1,225},{2,226},{3,227},{4,228},{5,229},{6,230},{7,231},{8... | collective-permute-start | bytes 1105928 | tf_op jit(solution)/shard_map/ppermute | solution.py:37
  20.4 1.0 %copy.8 = bf16[16,12,12]{2,1,0:T(8,128)(2,1)S(1)} copy(bf16[16,12,12]{1,0,2:T(8,128)(2,1)} %bitcast.10) | data formatting | bytes 9216 | tf_op jit(solution)/shard_map/transpose | solution.py:321
  21.7 1.1 %convolution_convert_fusion = bf16[32,1152]{1,0:T(8,128)(2,1)S(1)} fusion(bf16[144,1152]{1,0:T(8,128)(2,1)} %constant.6.clone, bf16[16,144]{1,0:T(8,128)(2,1)S(1)} %reshape.18, bf16[16,144]{1,0:T(8,128)(2,1)S(1)} %reshape.17), kind=kOutput, calls=%fused_computation | convolution fusion | flops 10672128 | bytes 414720 | tf_op jit(solution)/shard_map/dot_general | solution.py:327
  22.9 2.3 %collective-permute-done.1.p2 = bf16[30,48,128]{2,1,0:T(8,128)(2,1)S(1)} collective-permute-done((bf16[30,48,128]{2,1,0:T(8,128)(2,1)S(1)}, bf16[30,48,128]{2,1,0:T(8,128)(2,1)S(1)}, u32[]{:S(2)}, u32[]{:S(2)}) %collective-permute-start.1) | collective-permute-done | bytes 368672 | tf_op jit(solution)/shard_map/ppermute | solution.py:37
  25.2 1.3 %collective-permute-start.2 = (bf16[30,48,128]{2,1,0:T(8,128)(2,1)S(1)}, bf16[30,48,128]{2,1,0:T(8,128)(2,1)S(1)}, u32[]{:S(2)}, u32[]{:S(2)}) collective-permute-start(bf16[30,48,128]{2,1,0:T(8,128)(2,1)S(1)} %collective-permute-done.1.p2), channel_id=1, source_target_pairs={{0,16},{1,17},{2,18},{3,19},{4,20},{5,21},{6,22},{7,23},{8,24},{9,... | collective-permute-start | bytes 1105928 | tf_op jit(solution)/shard_map/ppermute | solution.py:37
  26.7 5.7 %collective-permute-done.4.center.m2 = bf16[30,48,128]{2,1,0:T(8,128)(2,1)S(1)} collective-permute-done((bf16[30,48,128]{2,1,0:T(8,128)(2,1)S(1)}, bf16[30,48,128]{2,1,0:T(8,128)(2,1)S(1)}, u32[]{:S(2)}, u32[]{:S(2)}) %collective-permute-start.4) | collective-permute-done | bytes 368672 | tf_op jit(solution)/shard_map/ppermute | solution.py:37
  32.4 3.6 %first_star.1 = (f32[6,256,256]{2,1,0:T(8,128)S(1)}, f32[48,768]{1,0:T(8,128)S(1)}) custom-call(bf16[30,48,128]{2,1,0:T(8,128)(2,1)S(1)} %collective-permute-done.4.center.m2, bf16[30,48,128]{2,1,0:T(8,128)(2,1)S(1)} %collective-permute-done.3.m1, bf16[30,48,128]{2,1,0:T(8,128)(2,1)S(1)} %pack.1.own, bf16[30,48,128]{2,1,0:T(8,128)(2,1)S(1)} %collective-permute-done.p1, ...), custom_call_target="tpu_custom_call" | custom-call | tf_op jit(solution)/shard_map/first_star/pallas_call | solution.py:183
  36.0 3.2 %second_star.1 = (f32[4,2,48,384]{3,2,1,0:T(8,128)S(1)}, bf16[4,2,48,384]{3,2,1,0:T(8,128)(2,1)S(1)}, f32[4,2,48,384]{3,2,1,0:T(8,128)S(1)}, bf16[4,2,48,384]{3,2,1,0:T(8,128)(2,1)S(1)}) custom-call(bf16[30,48,128]{2,1,0:T(8,128)(2,1)S(1)} %collective-permute-done.2.center, bf16[30,48,128]{2,1,0:T(8,128)(2,1)S(1)} %collective-permute-done.3.m1, ...), custom_call_target="tpu_custom_call" | custom-call | tf_op jit(solution)/shard_map/second_star/pallas_call | solution.py:198
  39.2 2.8 %collective-permute-start.9 = (bf16[4,2,48,384]{3,2,1,0:T(8,128)(2,1)S(1)}, bf16[4,2,48,384]{3,2,1,0:T(8,128)(2,1)S(1)}, u32[]{:S(2)}, u32[]{:S(2)}) collective-permute-start(bf16[4,2,48,384]{3,2,1,0:T(8,128)(2,1)S(1)} %get-tuple-element.28), channel_id=1, source_target_pairs={{0,1},{1,0},{2,3},{3,2},{4,5},{5,4},{6,7},{7,6},{8,9},{9,8},{10,11... | collective-permute-start | bytes 884744 | tf_op jit(solution)/shard_map/ppermute | solution.py:37
  42.1 1.1 %collective-permute-done.9.got = bf16[4,2,48,384]{3,2,1,0:T(8,128)(2,1)S(1)} collective-permute-done((bf16[4,2,48,384]{3,2,1,0:T(8,128)(2,1)S(1)}, bf16[4,2,48,384]{3,2,1,0:T(8,128)(2,1)S(1)}, u32[]{:S(2)}, u32[]{:S(2)}) %collective-permute-start.9) | collective-permute-done | bytes 294944 | tf_op jit(solution)/shard_map/ppermute | solution.py:37
  43.3 2.8 %collective-permute-start.10 = (bf16[2,48,384]{2,1,0:T(8,128)(2,1)S(1)}, bf16[2,48,384]{2,1,0:T(8,128)(2,1)S(1)}, u32[]{:S(2)}, u32[]{:S(2)}) collective-permute-start(bf16[2,48,384]{2,1,0:T(8,128)(2,1)S(1)} %get-tuple-element.30), channel_id=1, source_target_pairs={{0,4},{1,5},{2,6},{3,7},{4,0},{5,1},{6,2},{7,3},{8,12},{9,13},{10,... | collective-permute-start | bytes 221192 | tf_op jit(solution)/shard_map/ppermute | solution.py:37
  48.4 2.1 %collective-permute-start.7 = (bf16[2,48,384]{2,1,0:T(8,128)(2,1)S(1)}, bf16[2,48,384]{2,1,0:T(8,128)(2,1)S(1)}, u32[]{:S(2)}, u32[]{:S(2)}) collective-permute-start(bf16[2,48,384]{2,1,0:T(8,128)(2,1)S(1)} %get-tuple-element.25), channel_id=1, source_target_pairs={{0,6},{1,7},{2,0},{3,1},{4,2},{5,3},{6,4},{7,5},{8,14},{9,15},{10,... | collective-permute-start | bytes 221192 | tf_op jit(solution)/shard_map/ppermute | solution.py:37
  50.5 0.9 %collective-permute-done.12.one = bf16[2,48,384]{2,1,0:T(8,128)(2,1)S(1)} collective-permute-done((bf16[2,48,384]{2,1,0:T(8,128)(2,1)S(1)}, bf16[2,48,384]{2,1,0:T(8,128)(2,1)S(1)}, u32[]{:S(2)}, u32[]{:S(2)}) %collective-permute-start.12) | collective-permute-done | bytes 73760 | tf_op jit(solution)/shard_map/ppermute | solution.py:37
  51.5 3.0 %collective-permute-start.13 = (bf16[2,48,384]{2,1,0:T(8,128)(2,1)S(1)}, bf16[2,48,384]{2,1,0:T(8,128)(2,1)S(1)}, u32[]{:S(2)}, u32[]{:S(2)}) collective-permute-start(bf16[2,48,384]{2,1,0:T(8,128)(2,1)S(1)} %add_x.1), channel_id=1, source_target_pairs={{0,8},{1,9},{2,10},{3,11},{4,12},{5,13},{6,14},{7,15},{8,0},{9,1},... | collective-permute-start | bytes 221192 | tf_op jit(solution)/shard_map/ppermute | solution.py:37
  55.3 0.9 %collective-permute-done.13.got = bf16[2,48,384]{2,1,0:T(8,128)(2,1)S(1)} collective-permute-done((bf16[2,48,384]{2,1,0:T(8,128)(2,1)S(1)}, bf16[2,48,384]{2,1,0:T(8,128)(2,1)S(1)}, u32[]{:S(2)}, u32[]{:S(2)}) %collective-permute-start.13) | collective-permute-done | bytes 73760 | tf_op jit(solution)/shard_map/ppermute | solution.py:37
  56.5 1.6 %collective-permute-start.16 = (f32[2,48,128]{2,1,0:T(8,128)S(1)}, f32[2,48,128]{2,1,0:T(8,128)S(1)}, u32[]{:S(2)}, u32[]{:S(2)}) collective-permute-start(f32[2,48,128]{2,1,0:T(8,128)S(1)} %get-tuple-element.34), channel_id=1, source_target_pairs={{0,224},{1,33},{2,226},{3,35},{4,228},{5,37},{6,230},{7,39},{8,232... | collective-permute-start | bytes 147464 | tf_op jit(solution)/shard_map/ppermute | solution.py:46
  58.1 5.4 %collective-permute-done.14.plain = f32[2,48,256]{2,1,0:T(8,128)S(1)} collective-permute-done((f32[2,48,256]{2,1,0:T(8,128)S(1)}, f32[2,48,256]{2,1,0:T(8,128)S(1)}, u32[]{:S(2)}, u32[]{:S(2)}) %collective-permute-start.14) | collective-permute-done | bytes 98336 | tf_op jit(solution)/shard_map/ppermute | solution.py:46
  63.5 2.6 %collective-permute-start.15 = (f32[48,256]{1,0:T(8,128)S(1)}, f32[48,256]{1,0:T(8,128)S(1)}, u32[]{:S(2)}, u32[]{:S(2)}) collective-permute-start(f32[48,256]{1,0:T(8,128)S(1)} %slice_bitcast_fusion), channel_id=1, source_target_pairs={{0,1},{1,0},{2,3},{3,2},{4,5},{5,4},{6,7},{7,6},{8,9},{9,8},{10,11... | collective-permute-start | bytes 147464 | tf_op jit(solution)/shard_map/ppermute | solution.py:37
  66.1 0.9 %collective-permute-start.17 = (f32[48,128]{1,0:T(8,128)S(1)}, f32[48,128]{1,0:T(8,128)S(1)}, u32[]{:S(2)}, u32[]{:S(2)}) collective-permute-start(f32[48,128]{1,0:T(8,128)S(1)} %slice_bitcast_fusion.1), channel_id=1, source_target_pairs={{0,1},{1,0},{2,3},{3,2},{4,5},{5,4},{6,7},{7,6},{8,9},{9,8},{10,11... | collective-permute-start | bytes 73736 | tf_op jit(solution)/shard_map/ppermute | solution.py:37
  67.0 0.8 %collective-permute-done.17.mirror_other = f32[48,128]{1,0:T(8,128)S(1)} collective-permute-done((f32[48,128]{1,0:T(8,128)S(1)}, f32[48,128]{1,0:T(8,128)S(1)}, u32[]{:S(2)}, u32[]{:S(2)}) %collective-permute-start.17) | collective-permute-done | bytes 24608 | tf_op jit(solution)/shard_map/ppermute | solution.py:37
  67.9 1.1 %place.1 = (f32[1,48,768]{2,1,0:T(8,128)}, f32[1,48,768]{2,1,0:T(8,128)}) custom-call(f32[2,48,256]{2,1,0:T(8,128)S(1)} %collective-permute-done.14.plain, f32[48,256]{1,0:T(8,128)S(1)} %collective-permute-done.15.plain_other, f32[2,48,128]{2,1,0:T(8,128)S(1)} %collective-permute-done.16.mirror, f32[48,128]{1,0:T(8,128)S(1)} %collective-permute-done.17.mirror_other, ...), custom_call_target="tpu_custom_call" | custom-call | tf_op jit(solution)/shard_map/place/pallas_call | solution.py:310
  (35 shorter events, 5.6 us)
Async XLA Ops:
  0.6 31.7 %copy-start.1 = (f32[16]{0:T(128)S(1)}, f32[16]{0:T(128)}, u32[]{:S(2)}) copy-start(f32[16]{0:T(128)} %pair.1) | copy-start | bytes 196
  0.6 1.0 %copy-start = (bf16[48,12,320]{2,0,1:T(8,128)(2,1)S(1)}, bf16[48,12,320]{2,0,1:T(8,128)(2,1)}, u32[]{:S(2)}) copy-start(bf16[48,12,320]{2,0,1:T(8,128)(2,1)} %param.6) | copy-start | bytes 1105924
  1.7 24.9 %copy-start.2 = (pred[8,1152]{1,0:T(8,128)(4,1)S(1)}, pred[8,1152]{1,0:T(8,128)(4,1)}, u32[]{:S(2)}) copy-start(pred[8,1152]{1,0:T(8,128)(4,1)} %constant.7.clone) | copy-start | bytes 27652
  1.8 13.7 %collective-permute-start = (bf16[30,48,128]{2,1,0:T(8,128)(2,1)S(1)}, bf16[30,48,128]{2,1,0:T(8,128)(2,1)S(1)}, u32[]{:S(2)}, u32[]{:S(2)}) collective-permute-start(bf16[30,48,128]{2,1,0:T(8,128)(2,1)S(1)} %pack.1.own), channel_id=1, source_target_pairs={{0,224},{1,225},{2,226},{3,227},{4,228},{5,229},{6,230},{7,231},{8... | collective-permute-start | bytes 1105928 | tf_op jit(solution)/shard_map/ppermute | solution.py:37
  8.2 14.6 %collective-permute-start.3 = (bf16[30,48,128]{2,1,0:T(8,128)(2,1)S(1)}, bf16[30,48,128]{2,1,0:T(8,128)(2,1)S(1)}, u32[]{:S(2)}, u32[]{:S(2)}) collective-permute-start(bf16[30,48,128]{2,1,0:T(8,128)(2,1)S(1)} %pack.1.own), channel_id=1, source_target_pairs={{0,32},{1,33},{2,34},{3,35},{4,36},{5,37},{6,38},{7,39},{8,40},{9,... | collective-permute-start | bytes 1105928 | tf_op jit(solution)/shard_map/ppermute | solution.py:37
  15.5 9.7 %collective-permute-start.1 = (bf16[30,48,128]{2,1,0:T(8,128)(2,1)S(1)}, bf16[30,48,128]{2,1,0:T(8,128)(2,1)S(1)}, u32[]{:S(2)}, u32[]{:S(2)}) collective-permute-start(bf16[30,48,128]{2,1,0:T(8,128)(2,1)S(1)} %collective-permute-done.p1), channel_id=1, source_target_pairs={{0,224},{1,225},{2,226},{3,227},{4,228},{5,229},{6,230},{7,231},{8... | collective-permute-start | bytes 1105928 | tf_op jit(solution)/shard_map/ppermute | solution.py:37
  22.8 9.5 %collective-permute-start.4 = (bf16[30,48,128]{2,1,0:T(8,128)(2,1)S(1)}, bf16[30,48,128]{2,1,0:T(8,128)(2,1)S(1)}, u32[]{:S(2)}, u32[]{:S(2)}) collective-permute-start(bf16[30,48,128]{2,1,0:T(8,128)(2,1)S(1)} %collective-permute-done.3.m1), channel_id=1, source_target_pairs={{0,32},{1,33},{2,34},{3,35},{4,36},{5,37},{6,38},{7,39},{8,40},{9,... | collective-permute-start | bytes 1105928 | tf_op jit(solution)/shard_map/ppermute | solution.py:37
  25.2 10.7 %collective-permute-start.2 = (bf16[30,48,128]{2,1,0:T(8,128)(2,1)S(1)}, bf16[30,48,128]{2,1,0:T(8,128)(2,1)S(1)}, u32[]{:S(2)}, u32[]{:S(2)}) collective-permute-start(bf16[30,48,128]{2,1,0:T(8,128)(2,1)S(1)} %collective-permute-done.1.p2), channel_id=1, source_target_pairs={{0,16},{1,17},{2,18},{3,19},{4,20},{5,21},{6,22},{7,23},{8,24},{9,... | collective-permute-start | bytes 1105928 | tf_op jit(solution)/shard_map/ppermute | solution.py:37
  39.2 4.0 %collective-permute-start.9 = (bf16[4,2,48,384]{3,2,1,0:T(8,128)(2,1)S(1)}, bf16[4,2,48,384]{3,2,1,0:T(8,128)(2,1)S(1)}, u32[]{:S(2)}, u32[]{:S(2)}) collective-permute-start(bf16[4,2,48,384]{3,2,1,0:T(8,128)(2,1)S(1)} %get-tuple-element.28), channel_id=1, source_target_pairs={{0,1},{1,0},{2,3},{3,2},{4,5},{5,4},{6,7},{7,6},{8,9},{9,8},{10,11... | collective-permute-start | bytes 884744 | tf_op jit(solution)/shard_map/ppermute | solution.py:37
  42.0 5.6 %collective-permute-start.5 = (bf16[4,2,48,384]{3,2,1,0:T(8,128)(2,1)S(1)}, bf16[4,2,48,384]{3,2,1,0:T(8,128)(2,1)S(1)}, u32[]{:S(2)}, u32[]{:S(2)}) collective-permute-start(bf16[4,2,48,384]{3,2,1,0:T(8,128)(2,1)S(1)} %get-tuple-element.22), channel_id=1, source_target_pairs={{0,1},{1,0},{2,3},{3,2},{4,5},{5,4},{6,7},{7,6},{8,9},{9,8},{10,11... | collective-permute-start | bytes 884744 | tf_op jit(solution)/shard_map/ppermute | solution.py:37
  43.3 7.2 %collective-permute-start.10 = (bf16[2,48,384]{2,1,0:T(8,128)(2,1)S(1)}, bf16[2,48,384]{2,1,0:T(8,128)(2,1)S(1)}, u32[]{:S(2)}, u32[]{:S(2)}) collective-permute-start(bf16[2,48,384]{2,1,0:T(8,128)(2,1)S(1)} %get-tuple-element.30), channel_id=1, source_target_pairs={{0,4},{1,5},{2,6},{3,7},{4,0},{5,1},{6,2},{7,3},{8,12},{9,13},{10,... | collective-permute-start | bytes 221192 | tf_op jit(solution)/shard_map/ppermute | solution.py:37
  46.2 4.3 %collective-permute-start.11 = (bf16[2,48,384]{2,1,0:T(8,128)(2,1)S(1)}, bf16[2,48,384]{2,1,0:T(8,128)(2,1)S(1)}, u32[]{:S(2)}, u32[]{:S(2)}) collective-permute-start(bf16[2,48,384]{2,1,0:T(8,128)(2,1)S(1)} %get-tuple-element.31), channel_id=1, source_target_pairs={{0,6},{1,7},{2,0},{3,1},{4,2},{5,3},{6,4},{7,5},{8,14},{9,15},{10,... | collective-permute-start | bytes 221192 | tf_op jit(solution)/shard_map/ppermute | solution.py:37
  47.0 4.4 %collective-permute-start.12 = (bf16[2,48,384]{2,1,0:T(8,128)(2,1)S(1)}, bf16[2,48,384]{2,1,0:T(8,128)(2,1)S(1)}, u32[]{:S(2)}, u32[]{:S(2)}) collective-permute-start(bf16[2,48,384]{2,1,0:T(8,128)(2,1)S(1)} %get-tuple-element.32), channel_id=1, source_target_pairs={{0,2},{1,3},{2,4},{3,5},{4,6},{5,7},{6,0},{7,1},{8,10},{9,11},{10,... | collective-permute-start | bytes 221192 | tf_op jit(solution)/shard_map/ppermute | solution.py:37
  47.7 6.8 %collective-permute-start.6 = (bf16[2,48,384]{2,1,0:T(8,128)(2,1)S(1)}, bf16[2,48,384]{2,1,0:T(8,128)(2,1)S(1)}, u32[]{:S(2)}, u32[]{:S(2)}) collective-permute-start(bf16[2,48,384]{2,1,0:T(8,128)(2,1)S(1)} %get-tuple-element.24), channel_id=1, source_target_pairs={{0,4},{1,5},{2,6},{3,7},{4,0},{5,1},{6,2},{7,3},{8,12},{9,13},{10,... | collective-permute-start | bytes 221192 | tf_op jit(solution)/shard_map/ppermute | solution.py:37
  48.4 6.1 %collective-permute-start.7 = (bf16[2,48,384]{2,1,0:T(8,128)(2,1)S(1)}, bf16[2,48,384]{2,1,0:T(8,128)(2,1)S(1)}, u32[]{:S(2)}, u32[]{:S(2)}) collective-permute-start(bf16[2,48,384]{2,1,0:T(8,128)(2,1)S(1)} %get-tuple-element.25), channel_id=1, source_target_pairs={{0,6},{1,7},{2,0},{3,1},{4,2},{5,3},{6,4},{7,5},{8,14},{9,15},{10,... | collective-permute-start | bytes 221192 | tf_op jit(solution)/shard_map/ppermute | solution.py:37
  50.5 4.8 %collective-permute-start.8 = (bf16[2,48,384]{2,1,0:T(8,128)(2,1)S(1)}, bf16[2,48,384]{2,1,0:T(8,128)(2,1)S(1)}, u32[]{:S(2)}, u32[]{:S(2)}) collective-permute-start(bf16[2,48,384]{2,1,0:T(8,128)(2,1)S(1)} %get-tuple-element.26), channel_id=1, source_target_pairs={{0,2},{1,3},{2,4},{3,5},{4,6},{5,7},{6,0},{7,1},{8,10},{9,11},{10,... | collective-permute-start | bytes 221192 | tf_op jit(solution)/shard_map/ppermute | solution.py:37
  51.5 4.8 %collective-permute-start.13 = (bf16[2,48,384]{2,1,0:T(8,128)(2,1)S(1)}, bf16[2,48,384]{2,1,0:T(8,128)(2,1)S(1)}, u32[]{:S(2)}, u32[]{:S(2)}) collective-permute-start(bf16[2,48,384]{2,1,0:T(8,128)(2,1)S(1)} %add_x.1), channel_id=1, source_target_pairs={{0,8},{1,9},{2,10},{3,11},{4,12},{5,13},{6,14},{7,15},{8,0},{9,1},... | collective-permute-start | bytes 221192 | tf_op jit(solution)/shard_map/ppermute | solution.py:37
  56.4 7.0 %collective-permute-start.14 = (f32[2,48,256]{2,1,0:T(8,128)S(1)}, f32[2,48,256]{2,1,0:T(8,128)S(1)}, u32[]{:S(2)}, u32[]{:S(2)}) collective-permute-start(f32[2,48,256]{2,1,0:T(8,128)S(1)} %get-tuple-element.33), channel_id=1, source_target_pairs={{0,192},{1,81},{2,194},{3,83},{4,196},{5,85},{6,198},{7,87},{8,200... | collective-permute-start | bytes 294920 | tf_op jit(solution)/shard_map/ppermute | solution.py:46
  56.5 9.6 %collective-permute-start.16 = (f32[2,48,128]{2,1,0:T(8,128)S(1)}, f32[2,48,128]{2,1,0:T(8,128)S(1)}, u32[]{:S(2)}, u32[]{:S(2)}) collective-permute-start(f32[2,48,128]{2,1,0:T(8,128)S(1)} %get-tuple-element.34), channel_id=1, source_target_pairs={{0,224},{1,33},{2,226},{3,35},{4,228},{5,37},{6,230},{7,39},{8,232... | collective-permute-start | bytes 147464 | tf_op jit(solution)/shard_map/ppermute | solution.py:46
  63.5 4.4 %collective-permute-start.15 = (f32[48,256]{1,0:T(8,128)S(1)}, f32[48,256]{1,0:T(8,128)S(1)}, u32[]{:S(2)}, u32[]{:S(2)}) collective-permute-start(f32[48,256]{1,0:T(8,128)S(1)} %slice_bitcast_fusion), channel_id=1, source_target_pairs={{0,1},{1,0},{2,3},{3,2},{4,5},{5,4},{6,7},{7,6},{8,9},{9,8},{10,11... | collective-permute-start | bytes 147464 | tf_op jit(solution)/shard_map/ppermute | solution.py:37
  66.1 1.8 %collective-permute-start.17 = (f32[48,128]{1,0:T(8,128)S(1)}, f32[48,128]{1,0:T(8,128)S(1)}, u32[]{:S(2)}, u32[]{:S(2)}) collective-permute-start(f32[48,128]{1,0:T(8,128)S(1)} %slice_bitcast_fusion.1), channel_id=1, source_target_pairs={{0,1},{1,0},{2,3},{3,2},{4,5},{5,4},{6,7},{7,6},{8,9},{9,8},{10,11... | collective-permute-start | bytes 73736 | tf_op jit(solution)/shard_map/ppermute | solution.py:37

commit v4 on v3

--- a/solution.py
+++ b/solution.py
@@ -116,60 +116,66 @@
             products[g, d * rows:(d + 1) * rows, :] = part.astype(BF16)
 
 
-def first_kernel(center, m1, own, p1, m2, p2, weights, energy, pair, raw, divisor, left, products):
-    shape = divisor.shape
-    second = jnp.broadcast_to(energy[...], shape)
-    row = lax.axis_index("row") * ROWS + lax.broadcasted_iota(jnp.int32, shape, 0)
-    mine = lax.broadcasted_iota(jnp.int32, shape, 1) == row
-    first = jnp.sum(jnp.where(mine, second, 0.0), axis=1, keepdims=True)
-    divisor[...] = first + second - pair[lax.axis_index("col")]
+def first_kernel(center, m1, own, p1, m2, p2, weights, raw, held, arrived, left, products):
+    copy = pltpu.make_async_copy(weights, held, arrived)
+    copy.start()
     build_left(center, left)
     build_products(left, m1, own, p1, m2, p2, products)
+    copy.wait()
     for g in range(GROUPS):
-        raw[g] = jnp.dot(weights[...], products[g], preferred_element_type=F32)
-
-
-def second_kernel(center, m1, own, p1, m2, p2, weights, raw, keep_far, send_far, keep_near, send_near, left, products):
-    build_left(center, left)
-    build_products(left, p1, own, m1, m2, p2, products)
-    half = PAIRS * GROUP
+        raw[g] = jnp.dot(held[...], products[g], preferred_element_type=F32)
+
+
+def share(weights, products, raw, keep, send, y_hi):
+    half = 4 * 2 * GROUP
     lane = lax.broadcasted_iota(jnp.int32, (half, LANE), 1)
-    wide = lax.broadcasted_iota(jnp.int32, (2, 4, GROUP, LANE), 3)
+    wide = lax.broadcasted_iota(jnp.int32, (4, GROUP, LANE), 2)
     inner = (wide >= ROWS) & (wide < 2 * ROWS)
     here = core_here() == 0
-    first_half = lax.div(lax.axis_index("col"), 8) == 0
-    shape = (2, 4, 2, GROUP, LANE)
-    outs = ((keep_far, send_far), (keep_near, send_near))
+    shape = (4, 2, GROUP, LANE)
+    start = pl.multiple_of(y_hi * half, half)
+    taken = [pl.ds(start, half), pl.ds(pl.multiple_of(2 * half + start, half), half)]
+    chosen = jnp.concatenate([weights[rows, :] for rows in taken], axis=0)
     for g in range(0, GROUPS, 2):
         held = [[], []]
         for step in range(2):
-            mine = jnp.dot(weights[...], products[g + step], preferred_element_type=F32)
-            other = raw[g + step]
+            mine = jnp.dot(chosen, products[g + step], preferred_element_type=F32)
+            mine = [mine[:half], mine[half:]]
+            other = [raw[g + step, rows, :] for rows in taken]
             for at, inside in enumerate((LANE, 5 * ROWS - LANE, 2 * ROWS)):
                 lanes = slice(LANE, WIDE) if at == 1 else slice(0, LANE)
-                row = slice(half, 2 * half) if at == 2 else slice(0, half)
-                back = slice(half, 2 * half)
-                down, up = other[row, lanes], mine[row, lanes]
+                order = 1 if at == 2 else 0
+                down, up = other[order][:, lanes], mine[order][:, lanes]
                 if at > 0:
-                    down, up = (jnp.where(lane < inside, down, mine[back, lanes]),
-                                jnp.where(lane < inside, up, other[back, lanes]))
+                    down, up = (jnp.where(lane < inside, down, mine[1][:, lanes]),
+                                jnp.where(lane < inside, up, other[1][:, lanes]))
                 down, up = down.reshape(shape), up.reshape(shape)
                 if at == 2:
                     down, up = (
-                        jnp.stack([down[:, :, 0], jnp.where(inner, up[:, :, 0], down[:, :, 1])], axis=2),
-                        jnp.stack([jnp.where(inner, up[:, :, 1], up[:, :, 0]),
-                                   jnp.where(inner, down[:, :, 1], up[:, :, 1])], axis=2))
+                        jnp.stack([down[:, 0], jnp.where(inner, up[:, 0], down[:, 1])], axis=1),
+                        jnp.stack([jnp.where(inner, up[:, 1], up[:, 0]),
+                                   jnp.where(inner, down[:, 1], up[:, 1])], axis=1))
                 held[0].append(jnp.where(here, down, up))
                 held[1].append(jnp.where(here, up, down))
         rows = pl.ds(g * GROUP, 2 * GROUP)
-        for way in range(2):
+        for out, parts in ((keep, held[0]), (send, held[1])):
             for at in range(3):
-                lanes = pl.ds(at * LANE, LANE)
-                value = jnp.concatenate([held[way][at], held[way][3 + at]], axis=3)
-                near = jnp.where(first_half, value[0], value[1])
-                far = jnp.where(first_half, value[1], value[0])
-                for out, part in ((outs[0][way], far), (outs[1][way], near)):
-                    out[:, :, rows, lanes] = part.astype(out.dtype)
+                value = jnp.concatenate([parts[at], parts[3 + at]], axis=2)
+                out[:, :, rows, at * LANE:(at + 1) * LANE] = value.astype(out.dtype)
+
+
+def y_hi_here():
+    return lax.div(lax.axis_index("col"), 8)
+
+
+def second_kernel(center, m1, own, p1, m2, p2, weights, raw, keep, send, products, left):
+    build_left(center, left)
+    build_products(left, p1, own, m1, m2, p2, products)
+    share(weights, products, raw, keep, send, 1 - y_hi_here())
+
+
+def last_kernel(products, weights, raw, keep, send):
+    share(weights, products, raw, keep, send, y_hi_here())
 
 
 def scratch():
@@ -179,31 +185,53 @@
     ]
 
 
-def first_star(center, others, weights, vir_energy, pair_energy):
+def weights_scratch():
+    return [pltpu.VMEM((2 * PAIRS * GROUP, DEPTH), BF16), pltpu.SemaphoreType.DMA]
+
+
+def star_cost():
+    return pl.CostEstimate(flops=10_000_000_000, bytes_accessed=4_000_000, transcendentals=0)
+
+
+def first_star(center, others, weights):
     return pl.pallas_call(
         first_kernel,
-        out_shape=(jax.ShapeDtypeStruct((GROUPS, 2 * PAIRS * GROUP, WIDE), F32),
-                   jax.ShapeDtypeStruct((ROWS, 16 * ROWS), F32)),
-        in_specs=full(8) + [pl.BlockSpec(memory_space=pltpu.SMEM)],
-        out_specs=tuple(full(2)),
-        scratch_shapes=scratch(),
-        compiler_params=params(),
+        out_shape=jax.ShapeDtypeStruct((GROUPS, 2 * PAIRS * GROUP, WIDE), F32),
+        in_specs=full(6) + [pl.BlockSpec(memory_space=pl.ANY)],
+        out_specs=full(1)[0],
+        scratch_shapes=weights_scratch() + scratch(),
+        compiler_params=params(),
+        cost_estimate=star_cost(),
         name="first_star",
-    )(center, *others, weights, vir_energy[None, :], pair_energy)
+    )(center, *others, weights)
+
+
+def halves():
+    shape = (4, 2, ROWS, OUT)
+    return jax.ShapeDtypeStruct(shape, F32), jax.ShapeDtypeStruct(shape, BF16)
 
 
 def second_star(center, others, weights, raw):
-    shape = (4, 2, ROWS, OUT)
-    half = (jax.ShapeDtypeStruct(shape, F32), jax.ShapeDtypeStruct(shape, BF16))
     return pl.pallas_call(
         second_kernel,
-        out_shape=half + half,
+        out_shape=halves() + (jax.ShapeDtypeStruct((GROUPS, DEPTH, WIDE), BF16),),
         in_specs=full(8),
-        out_specs=tuple(full(4)),
-        scratch_shapes=scratch(),
+        out_specs=tuple(full(3)),
+        scratch_shapes=scratch()[:1],
         compiler_params=params(),
         name="second_star",
     )(center, *others, weights, raw)
+
+
+def last_star(products, weights, raw):
+    return pl.pallas_call(
+        last_kernel,
+        out_shape=halves(),
+        in_specs=full(3),
+        out_specs=tuple(full(2)),
+        compiler_params=params(),
+        name="last_star",
+    )(products, weights, raw)
 
 
 def core_kernel(keep, got, *outs):
@@ -317,31 +345,54 @@
     )(*parts)
 
 
-def contraction_weights(amplitudes):
-    plain = jnp.swapaxes(amplitudes, 1, 2).reshape(PAIRS, SLAB * SLAB)
-    mirror = amplitudes.reshape(PAIRS, SLAB * SLAB)
-    both = jnp.concatenate([plain, mirror], axis=0)
-    column = np.arange(DEPTH)
-    same = np.arange(GROUP)[:, None] == column[None, :] % GROUP
-    spread = column[None, :] // GROUP == np.arange(SLAB * SLAB)[:, None]
-    wide = jnp.dot(both, jnp.asarray(spread, BF16), preferred_element_type=F32).astype(BF16)
-    wide = jnp.where(jnp.asarray(same)[None], wide[:, None, :], jnp.zeros((), BF16))
-    return wide.reshape(2 * PAIRS * GROUP, DEPTH)
+def setup_kernel(amplitudes, energy, pair, weights, divisor):
+    shape = divisor.shape
+    second = jnp.broadcast_to(energy[...].reshape(1, shape[1]), shape)
+    row = lax.axis_index("row") * ROWS + lax.broadcasted_iota(jnp.int32, shape, 0)
+    mine = lax.broadcasted_iota(jnp.int32, shape, 1) == row
+    first = jnp.sum(jnp.where(mine, second, 0.0), axis=1, keepdims=True)
+    divisor[...] = first + second - pair[lax.axis_index("col")]
+    flat = amplitudes[...].reshape(SLAB * PAIRS, SLAB)
+    column = lax.broadcasted_iota(jnp.int32, (1, DEPTH), 1)
+    slab = lax.broadcasted_iota(jnp.int32, (SLAB, DEPTH), 0)
+    within = lax.broadcasted_iota(jnp.int32, (PAIRS * GROUP, DEPTH), 0)
+    same = lax.rem(within, GROUP) == lax.rem(column, GROUP)
+    d, c = lax.div(column, SLAB * GROUP), lax.rem(lax.div(column, GROUP), SLAB)
+    for order, (outer, inner) in enumerate(((c, d), (d, c))):
+        spread = jnp.where(slab == inner, 1.0, 0.0).astype(BF16)
+        wide = jnp.dot(flat, spread, preferred_element_type=F32).reshape(SLAB, PAIRS, DEPTH)
+        total = jnp.where(outer == 0, wide[0], 0.0)
+        for at in range(1, SLAB):
+            total = jnp.where(outer == at, wide[at], total)
+        total = jnp.broadcast_to(total[:, None, :], (PAIRS, GROUP, DEPTH)).reshape(PAIRS * GROUP, DEPTH)
+        weights[order * PAIRS * GROUP:(order + 1) * PAIRS * GROUP, :] = jnp.where(same, total, 0.0).astype(BF16)
+
+
+def setup(amplitudes, vir_energy, pair_energy):
+    return pl.pallas_call(
+        setup_kernel,
+        out_shape=(jax.ShapeDtypeStruct((2 * PAIRS * GROUP, DEPTH), BF16), jax.ShapeDtypeStruct((ROWS, 16 * ROWS), F32)),
+        in_specs=full(2) + [pl.BlockSpec(memory_space=pltpu.SMEM)],
+        out_specs=tuple(full(2)),
+        compiler_params=params(),
+        name="setup",
+    )(jnp.transpose(amplitudes, (1, 0, 2)), vir_energy, pair_energy)
 
 
 def per_device(factors, amplitudes, vir_energy, pair_energy):
     own = pack_block(factors)
     p1 = shift(own, dz=-1)
     m1 = shift(own, dz=1)
-    weights = contraction_weights(amplitudes)
+    weights, divisor = setup(amplitudes, vir_energy, pair_energy)
     p2 = shift(p1, dz=-1)
     m2 = shift(m1, dz=1)
     cross = shift(p2, dy=1)
     others = (m1, own, p1, m2, p2)
-    raw, divisor = first_star(m2, others, weights, vir_energy, pair_energy)
-    keep_far, send_far, keep_near, send_near = second_star(cross, others, weights, raw)
-    far = add_cores(keep_far, shift(send_far, dc=1))
-    near = add_cores(keep_near, shift(send_near, dc=1))
+    raw = first_star(m2, others, weights)
+    keep, send, products = second_star(cross, others, weights, raw)
+    far = add_cores(keep, shift(send, dc=1))
+    keep, send = last_star(products, weights, raw)
+    near = add_cores(keep, shift(send, dc=1))
 
     def along_x(stay, one, two, three):
         return stay, shift(two, dx=2), shift(three, dx=-1), shift(one, dx=1)

time: 69.3 us -> 67.6 us (0.975)
  waiting for transfers between devices: 25.3 us -> 19.8 us
  starting transfers between devices: 29.5 us -> 34.4 us
  matrix products: 1.14 us -> 0 us
  Pallas kernels: 8.36 us -> 9.29 us
    ppermute x2, waiting for transfers between devices: 5.37 us -> 2.53 us  [to_rows(): return lax.ppermute(array, ('row', 'col'), pairs)]
    ppermute x16, waiting for transfers between devices: 20 us -> 17.3 us  [shift(): return lax.ppermute(array, ('row', 'col'), pairs)]
    ppermute x2, starting transfers between devices: 1.65 us -> 4.13 us  [to_rows(): return lax.ppermute(array, ('row', 'col'), pairs)]
    ppermute x16, starting transfers between devices: 27.9 us -> 30.2 us  [shift(): return lax.ppermute(array, ('row', 'col'), pairs)]
    unnamed x7 -> x8, local copies, waits for them, and re-layouts: 1.83 us -> 3.14 us
    dot_general x1 -> x0, matrix products: 1.14 us -> none  [contraction_weights(): jnp.dot(both, jnp.asarray(spread, BF16), preferred_element_type=F32)]
    transpose x1 -> x0, local copies, waits for them, and re-layouts: 1.02 us -> none  [contraction_weights(): plain = jnp.swapaxes(amplitudes, 1, 2).reshape(PAIRS, SLAB * SLAB)]
    pallas_call x2 -> x4, Pallas kernels: 6.82 us -> 7.75 us  [the longest x1 3.35 us: first_star(): pl.pallas_call(first_kernel, out_shape=jax.ShapeDtypeStruct((GROUPS, 2 *...]
  transfers between devices with their start and end apart: 18 -> 18, of which waited for: 9 -> 10; matrix products, arithmetic and copies ran while one was open for 6% -> 0% of each run, Pallas kernels for 5% -> 8%
where the time goes in v4:
time: 67.6 us; the launch traced here: 67.3 us
  starting transfers between devices  34.4 us (51%)
  waiting for transfers between devices  19.8 us (29%)
  Pallas kernels  9.29 us (14%)
  local copies, waits for them, and re-layouts  3.15 us (5%)
  between operations  0.71 us (1%)
    ppermute x16, starting transfers between devices, shift(): return lax.ppermute(array, ('row', 'col'), pairs)  30.2 us
    ppermute x16, waiting for transfers between devices, shift(): return lax.ppermute(array, ('row', 'col'), pairs)  17.3 us
    ppermute x2, starting transfers between devices, to_rows(): return lax.ppermute(array, ('row', 'col'), pairs)  4.13 us
    pallas_call x1, Pallas kernels, first_star(): pl.pallas_call(first_kernel, out_shape=jax.ShapeDtypeStruct((GROUPS, 2 *...  3.35 us
    unnamed x8, local copies, waits for them, and re-layouts  3.14 us
    pallas_call x1, Pallas kernels, second_star(): pl.pallas_call(second_kernel, out_shape=halves() + (jax.ShapeDtypeStruct(...  2.62 us
    ppermute x2, waiting for transfers between devices, to_rows(): return lax.ppermute(array, ('row', 'col'), pairs)  2.53 us
  transfers between devices with their start and end apart: 18, of which 10 were waited for; matrix products, arithmetic and copies ran while one was open for 0% of the time, Pallas kernels for 8%

profile of v4, /device:TPU:1, one launch (start us, length us, event | category | flops | bytes accessed | tf_op | source)
XLA Modules:
  0.0 67.3 jit_solution(5982737335033409025)
XLA Ops:
  0.6 1.0 %copy-done = bf16[48,12,320]{2,0,1:T(8,128)(2,1)S(1)} copy-done((bf16[48,12,320]{2,0,1:T(8,128)(2,1)S(1)}, bf16[48,12,320]{2,0,1:T(8,128)(2,1)}, u32[]{:S(2)}) %copy-start) | copy-done | bytes 368664
  1.7 6.5 %collective-permute-start = (bf16[30,48,128]{2,1,0:T(8,128)(2,1)S(1)}, bf16[30,48,128]{2,1,0:T(8,128)(2,1)S(1)}, u32[]{:S(2)}, u32[]{:S(2)}) collective-permute-start(bf16[30,48,128]{2,1,0:T(8,128)(2,1)S(1)} %pack.1.own), channel_id=1, source_target_pairs={{0,224},{1,225},{2,226},{3,227},{4,228},{5,229},{6,230},{7,231},{8... | collective-permute-start | bytes 1105928 | tf_op jit(solution)/shard_map/ppermute | solution.py:37
  8.2 7.3 %collective-permute-done.p1 = bf16[30,48,128]{2,1,0:T(8,128)(2,1)S(1)} collective-permute-done((bf16[30,48,128]{2,1,0:T(8,128)(2,1)S(1)}, bf16[30,48,128]{2,1,0:T(8,128)(2,1)S(1)}, u32[]{:S(2)}, u32[]{:S(2)}) %collective-permute-start) | collective-permute-done | bytes 368672 | tf_op jit(solution)/shard_map/ppermute | solution.py:37
  15.5 3.4 %collective-permute-start.1 = (bf16[30,48,128]{2,1,0:T(8,128)(2,1)S(1)}, bf16[30,48,128]{2,1,0:T(8,128)(2,1)S(1)}, u32[]{:S(2)}, u32[]{:S(2)}) collective-permute-start(bf16[30,48,128]{2,1,0:T(8,128)(2,1)S(1)} %collective-permute-done.p1), channel_id=1, source_target_pairs={{0,224},{1,225},{2,226},{3,227},{4,228},{5,229},{6,230},{7,231},{8... | collective-permute-start | bytes 1105928 | tf_op jit(solution)/shard_map/ppermute | solution.py:37
  21.0 1.0 %setup.1 = (bf16[256,1152]{1,0:T(8,128)(2,1)S(1)}, f32[48,768]{1,0:T(8,128)S(1)}) custom-call(bf16[12,16,12]{2,1,0:T(8,128)(2,1)S(1)} %bitcast.7, f32[768]{0:T(1024)S(1)} %copy-done.2, f32[16]{0:T(128)S(1)} %copy-done.3), custom_call_target="tpu_custom_call" | custom-call | tf_op jit(solution)/shard_map/setup/pallas_call | solution.py:372
  22.1 3.1 %collective-permute-done.1.p2 = bf16[30,48,128]{2,1,0:T(8,128)(2,1)S(1)} collective-permute-done((bf16[30,48,128]{2,1,0:T(8,128)(2,1)S(1)}, bf16[30,48,128]{2,1,0:T(8,128)(2,1)S(1)}, u32[]{:S(2)}, u32[]{:S(2)}) %collective-permute-start.1) | collective-permute-done | bytes 368672 | tf_op jit(solution)/shard_map/ppermute | solution.py:37
  25.2 1.3 %collective-permute-start.2 = (bf16[30,48,128]{2,1,0:T(8,128)(2,1)S(1)}, bf16[30,48,128]{2,1,0:T(8,128)(2,1)S(1)}, u32[]{:S(2)}, u32[]{:S(2)}) collective-permute-start(bf16[30,48,128]{2,1,0:T(8,128)(2,1)S(1)} %collective-permute-done.1.p2), channel_id=1, source_target_pairs={{0,16},{1,17},{2,18},{3,19},{4,20},{5,21},{6,22},{7,23},{8,24},{9,... | collective-permute-start | bytes 1105928 | tf_op jit(solution)/shard_map/ppermute | solution.py:37
  26.5 1.8 %collective-permute-done.4.center.m2 = bf16[30,48,128]{2,1,0:T(8,128)(2,1)S(1)} collective-permute-done((bf16[30,48,128]{2,1,0:T(8,128)(2,1)S(1)}, bf16[30,48,128]{2,1,0:T(8,128)(2,1)S(1)}, u32[]{:S(2)}, u32[]{:S(2)}) %collective-permute-start.4) | collective-permute-done | bytes 368672 | tf_op jit(solution)/shard_map/ppermute | solution.py:37
  28.4 3.3 %first_star.1.raw = f32[6,256,256]{2,1,0:T(8,128)S(1)} custom-call(bf16[30,48,128]{2,1,0:T(8,128)(2,1)S(1)} %collective-permute-done.4.center.m2, bf16[30,48,128]{2,1,0:T(8,128)(2,1)S(1)} %collective-permute-done.3.m1, bf16[30,48,128]{2,1,0:T(8,128)(2,1)S(1)} %pack.1.own, bf16[30,48,128]{2,1,0:T(8,128)(2,1)S(1)} %collective-permute-done.p1, ...), custom_call_target="tpu_custom_call" | custom-call | flops 10000000000 | bytes 4000000 | tf_op jit(solution)/shard_map/first_star/pallas_call | solution.py:197
  31.7 1.1 %collective-permute-done.2.center = bf16[30,48,128]{2,1,0:T(8,128)(2,1)S(1)} collective-permute-done((bf16[30,48,128]{2,1,0:T(8,128)(2,1)S(1)}, bf16[30,48,128]{2,1,0:T(8,128)(2,1)S(1)}, u32[]{:S(2)}, u32[]{:S(2)}) %collective-permute-start.2) | collective-permute-done | bytes 368672 | tf_op jit(solution)/shard_map/ppermute | solution.py:37
  32.8 2.6 %second_star.1 = (f32[4,2,48,384]{3,2,1,0:T(8,128)S(1)}, bf16[4,2,48,384]{3,2,1,0:T(8,128)(2,1)S(1)}, bf16[6,1152,256]{2,1,0:T(8,128)(2,1)S(1)}) custom-call(bf16[30,48,128]{2,1,0:T(8,128)(2,1)S(1)} %collective-permute-done.2.center, bf16[30,48,128]{2,1,0:T(8,128)(2,1)S(1)} %collective-permute-done.3.m1, bf16[30,48,128]{2,1,0:T(8,128)(2,1)S(1)} %pack.1.own, ...), custom_call_target="tpu_custom_call" | custom-call | tf_op jit(solution)/shard_map/second_star/pallas_call | solution.py:215
  35.5 3.5 %collective-permute-start.9 = (bf16[4,2,48,384]{3,2,1,0:T(8,128)(2,1)S(1)}, bf16[4,2,48,384]{3,2,1,0:T(8,128)(2,1)S(1)}, u32[]{:S(2)}, u32[]{:S(2)}) collective-permute-start(bf16[4,2,48,384]{3,2,1,0:T(8,128)(2,1)S(1)} %get-tuple-element.30), channel_id=1, source_target_pairs={{0,1},{1,0},{2,3},{3,2},{4,5},{5,4},{6,7},{7,6},{8,9},{9,8},{10,11... | collective-permute-start | bytes 884744 | tf_op jit(solution)/shard_map/ppermute | solution.py:37
  40.2 2.8 %collective-permute-start.10 = (bf16[2,48,384]{2,1,0:T(8,128)(2,1)S(1)}, bf16[2,48,384]{2,1,0:T(8,128)(2,1)S(1)}, u32[]{:S(2)}, u32[]{:S(2)}) collective-permute-start(bf16[2,48,384]{2,1,0:T(8,128)(2,1)S(1)} %get-tuple-element.32), channel_id=1, source_target_pairs={{0,4},{1,5},{2,6},{3,7},{4,0},{5,1},{6,2},{7,3},{8,12},{9,13},{10,... | collective-permute-start | bytes 221192 | tf_op jit(solution)/shard_map/ppermute | solution.py:37
  43.0 0.9 %collective-permute-start.11 = (bf16[2,48,384]{2,1,0:T(8,128)(2,1)S(1)}, bf16[2,48,384]{2,1,0:T(8,128)(2,1)S(1)}, u32[]{:S(2)}, u32[]{:S(2)}) collective-permute-start(bf16[2,48,384]{2,1,0:T(8,128)(2,1)S(1)} %get-tuple-element.33), channel_id=1, source_target_pairs={{0,6},{1,7},{2,0},{3,1},{4,2},{5,3},{6,4},{7,5},{8,14},{9,15},{10,... | collective-permute-start | bytes 221192 | tf_op jit(solution)/shard_map/ppermute | solution.py:37
  45.3 2.1 %collective-permute-start.7 = (bf16[2,48,384]{2,1,0:T(8,128)(2,1)S(1)}, bf16[2,48,384]{2,1,0:T(8,128)(2,1)S(1)}, u32[]{:S(2)}, u32[]{:S(2)}) collective-permute-start(bf16[2,48,384]{2,1,0:T(8,128)(2,1)S(1)} %get-tuple-element.27), channel_id=1, source_target_pairs={{0,6},{1,7},{2,0},{3,1},{4,2},{5,3},{6,4},{7,5},{8,14},{9,15},{10,... | collective-permute-start | bytes 221192 | tf_op jit(solution)/shard_map/ppermute | solution.py:37
  47.4 0.9 %collective-permute-done.12.one = bf16[2,48,384]{2,1,0:T(8,128)(2,1)S(1)} collective-permute-done((bf16[2,48,384]{2,1,0:T(8,128)(2,1)S(1)}, bf16[2,48,384]{2,1,0:T(8,128)(2,1)S(1)}, u32[]{:S(2)}, u32[]{:S(2)}) %collective-permute-start.12) | collective-permute-done | bytes 73760 | tf_op jit(solution)/shard_map/ppermute | solution.py:37
  48.4 3.0 %collective-permute-start.13 = (bf16[2,48,384]{2,1,0:T(8,128)(2,1)S(1)}, bf16[2,48,384]{2,1,0:T(8,128)(2,1)S(1)}, u32[]{:S(2)}, u32[]{:S(2)}) collective-permute-start(bf16[2,48,384]{2,1,0:T(8,128)(2,1)S(1)} %add_x.1), channel_id=1, source_target_pairs={{0,8},{1,9},{2,10},{3,11},{4,12},{5,13},{6,14},{7,15},{8,0},{9,1},... | collective-permute-start | bytes 221192 | tf_op jit(solution)/shard_map/ppermute | solution.py:37
  52.2 0.9 %collective-permute-done.13.got = bf16[2,48,384]{2,1,0:T(8,128)(2,1)S(1)} collective-permute-done((bf16[2,48,384]{2,1,0:T(8,128)(2,1)S(1)}, bf16[2,48,384]{2,1,0:T(8,128)(2,1)S(1)}, u32[]{:S(2)}, u32[]{:S(2)}) %collective-permute-start.13) | collective-permute-done | bytes 73760 | tf_op jit(solution)/shard_map/ppermute | solution.py:37
  53.3 1.7 %collective-permute-start.14 = (f32[2,48,256]{2,1,0:T(8,128)S(1)}, f32[2,48,256]{2,1,0:T(8,128)S(1)}, u32[]{:S(2)}, u32[]{:S(2)}) collective-permute-start(f32[2,48,256]{2,1,0:T(8,128)S(1)} %get-tuple-element.35), channel_id=1, source_target_pairs={{0,192},{1,81},{2,194},{3,83},{4,196},{5,85},{6,198},{7,87},{8,200... | collective-permute-start | bytes 294920 | tf_op jit(solution)/shard_map/ppermute | solution.py:46
  55.1 2.4 %collective-permute-start.16 = (f32[2,48,128]{2,1,0:T(8,128)S(1)}, f32[2,48,128]{2,1,0:T(8,128)S(1)}, u32[]{:S(2)}, u32[]{:S(2)}) collective-permute-start(f32[2,48,128]{2,1,0:T(8,128)S(1)} %get-tuple-element.36), channel_id=1, source_target_pairs={{0,224},{1,33},{2,226},{3,35},{4,228},{5,37},{6,230},{7,39},{8,232... | collective-permute-start | bytes 147464 | tf_op jit(solution)/shard_map/ppermute | solution.py:46
  57.5 2.5 %collective-permute-done.14.plain = f32[2,48,256]{2,1,0:T(8,128)S(1)} collective-permute-done((f32[2,48,256]{2,1,0:T(8,128)S(1)}, f32[2,48,256]{2,1,0:T(8,128)S(1)}, u32[]{:S(2)}, u32[]{:S(2)}) %collective-permute-start.14) | collective-permute-done | bytes 98336 | tf_op jit(solution)/shard_map/ppermute | solution.py:46
  60.0 3.7 %collective-permute-start.15 = (f32[48,256]{1,0:T(8,128)S(1)}, f32[48,256]{1,0:T(8,128)S(1)}, u32[]{:S(2)}, u32[]{:S(2)}) collective-permute-start(f32[48,256]{1,0:T(8,128)S(1)} %slice_bitcast_fusion), channel_id=1, source_target_pairs={{0,1},{1,0},{2,3},{3,2},{4,5},{5,4},{6,7},{7,6},{8,9},{9,8},{10,11... | collective-permute-start | bytes 147464 | tf_op jit(solution)/shard_map/ppermute | solution.py:37
  63.7 1.7 %collective-permute-start.17 = (f32[48,128]{1,0:T(8,128)S(1)}, f32[48,128]{1,0:T(8,128)S(1)}, u32[]{:S(2)}, u32[]{:S(2)}) collective-permute-start(f32[48,128]{1,0:T(8,128)S(1)} %slice_bitcast_fusion.1), channel_id=1, source_target_pairs={{0,1},{1,0},{2,3},{3,2},{4,5},{5,4},{6,7},{7,6},{8,9},{9,8},{10,11... | collective-permute-start | bytes 73736 | tf_op jit(solution)/shard_map/ppermute | solution.py:37
  66.2 1.1 %place.1 = (f32[1,48,768]{2,1,0:T(8,128)}, f32[1,48,768]{2,1,0:T(8,128)}) custom-call(f32[2,48,256]{2,1,0:T(8,128)S(1)} %collective-permute-done.14.plain, f32[48,256]{1,0:T(8,128)S(1)} %collective-permute-done.15.plain_other, f32[2,48,128]{2,1,0:T(8,128)S(1)} %collective-permute-done.16.mirror, f32[48,128]{1,0:T(8,128)S(1)} %collective-permute-done.17.mirror_other, ...), custom_call_target="tpu_custom_call" | custom-call | tf_op jit(solution)/shard_map/place/pallas_call | solution.py:338
  (32 shorter events, 6.8 us)
Async XLA Ops:
  0.6 1.0 %copy-start = (bf16[48,12,320]{2,0,1:T(8,128)(2,1)S(1)}, bf16[48,12,320]{2,0,1:T(8,128)(2,1)}, u32[]{:S(2)}) copy-start(bf16[48,12,320]{2,0,1:T(8,128)(2,1)} %param.4) | copy-start | bytes 1105924
  1.7 13.7 %collective-permute-start = (bf16[30,48,128]{2,1,0:T(8,128)(2,1)S(1)}, bf16[30,48,128]{2,1,0:T(8,128)(2,1)S(1)}, u32[]{:S(2)}, u32[]{:S(2)}) collective-permute-start(bf16[30,48,128]{2,1,0:T(8,128)(2,1)S(1)} %pack.1.own), channel_id=1, source_target_pairs={{0,224},{1,225},{2,226},{3,227},{4,228},{5,229},{6,230},{7,231},{8... | collective-permute-start | bytes 1105928 | tf_op jit(solution)/shard_map/ppermute | solution.py:37
  8.2 10.7 %collective-permute-start.3 = (bf16[30,48,128]{2,1,0:T(8,128)(2,1)S(1)}, bf16[30,48,128]{2,1,0:T(8,128)(2,1)S(1)}, u32[]{:S(2)}, u32[]{:S(2)}) collective-permute-start(bf16[30,48,128]{2,1,0:T(8,128)(2,1)S(1)} %pack.1.own), channel_id=1, source_target_pairs={{0,32},{1,33},{2,34},{3,35},{4,36},{5,37},{6,38},{7,39},{8,40},{9,... | collective-permute-start | bytes 1105928 | tf_op jit(solution)/shard_map/ppermute | solution.py:37
  15.5 9.7 %collective-permute-start.1 = (bf16[30,48,128]{2,1,0:T(8,128)(2,1)S(1)}, bf16[30,48,128]{2,1,0:T(8,128)(2,1)S(1)}, u32[]{:S(2)}, u32[]{:S(2)}) collective-permute-start(bf16[30,48,128]{2,1,0:T(8,128)(2,1)S(1)} %collective-permute-done.p1), channel_id=1, source_target_pairs={{0,224},{1,225},{2,226},{3,227},{4,228},{5,229},{6,230},{7,231},{8... | collective-permute-start | bytes 1105928 | tf_op jit(solution)/shard_map/ppermute | solution.py:37
  18.9 9.5 %collective-permute-start.4 = (bf16[30,48,128]{2,1,0:T(8,128)(2,1)S(1)}, bf16[30,48,128]{2,1,0:T(8,128)(2,1)S(1)}, u32[]{:S(2)}, u32[]{:S(2)}) collective-permute-start(bf16[30,48,128]{2,1,0:T(8,128)(2,1)S(1)} %collective-permute-done.3.m1), channel_id=1, source_target_pairs={{0,32},{1,33},{2,34},{3,35},{4,36},{5,37},{6,38},{7,39},{8,40},{9,... | collective-permute-start | bytes 1105928 | tf_op jit(solution)/shard_map/ppermute | solution.py:37
  18.9 0.8 %copy-start.1 = (bf16[16,12,12]{2,0,1:T(8,128)(2,1)S(1)}, bf16[16,12,12]{2,0,1:T(8,128)(2,1)}, u32[]{:S(2)}) copy-start(bf16[16,12,12]{2,0,1:T(8,128)(2,1)} %param.5) | copy-start | bytes 13828
  19.7 0.7 %copy-start.2 = (f32[768]{0:T(1024)S(1)}, f32[768]{0:T(1024)}, u32[]{:S(2)}) copy-start(f32[768]{0:T(1024)} %energy.1) | copy-start | bytes 9220
  20.4 0.7 copy-start.3
  25.2 7.6 %collective-permute-start.2 = (bf16[30,48,128]{2,1,0:T(8,128)(2,1)S(1)}, bf16[30,48,128]{2,1,0:T(8,128)(2,1)S(1)}, u32[]{:S(2)}, u32[]{:S(2)}) collective-permute-start(bf16[30,48,128]{2,1,0:T(8,128)(2,1)S(1)} %collective-permute-done.1.p2), channel_id=1, source_target_pairs={{0,16},{1,17},{2,18},{3,19},{4,20},{5,21},{6,22},{7,23},{8,24},{9,... | collective-permute-start | bytes 1105928 | tf_op jit(solution)/shard_map/ppermute | solution.py:37
  35.5 4.7 %collective-permute-start.9 = (bf16[4,2,48,384]{3,2,1,0:T(8,128)(2,1)S(1)}, bf16[4,2,48,384]{3,2,1,0:T(8,128)(2,1)S(1)}, u32[]{:S(2)}, u32[]{:S(2)}) collective-permute-start(bf16[4,2,48,384]{3,2,1,0:T(8,128)(2,1)S(1)} %get-tuple-element.30), channel_id=1, source_target_pairs={{0,1},{1,0},{2,3},{3,2},{4,5},{5,4},{6,7},{7,6},{8,9},{9,8},{10,11... | collective-permute-start | bytes 884744 | tf_op jit(solution)/shard_map/ppermute | solution.py:37
  39.7 4.8 %collective-permute-start.5 = (bf16[4,2,48,384]{3,2,1,0:T(8,128)(2,1)S(1)}, bf16[4,2,48,384]{3,2,1,0:T(8,128)(2,1)S(1)}, u32[]{:S(2)}, u32[]{:S(2)}) collective-permute-start(bf16[4,2,48,384]{3,2,1,0:T(8,128)(2,1)S(1)} %get-tuple-element.24), channel_id=1, source_target_pairs={{0,1},{1,0},{2,3},{3,2},{4,5},{5,4},{6,7},{7,6},{8,9},{9,8},{10,11... | collective-permute-start | bytes 884744 | tf_op jit(solution)/shard_map/ppermute | solution.py:37
  40.2 7.2 %collective-permute-start.10 = (bf16[2,48,384]{2,1,0:T(8,128)(2,1)S(1)}, bf16[2,48,384]{2,1,0:T(8,128)(2,1)S(1)}, u32[]{:S(2)}, u32[]{:S(2)}) collective-permute-start(bf16[2,48,384]{2,1,0:T(8,128)(2,1)S(1)} %get-tuple-element.32), channel_id=1, source_target_pairs={{0,4},{1,5},{2,6},{3,7},{4,0},{5,1},{6,2},{7,3},{8,12},{9,13},{10,... | collective-permute-start | bytes 221192 | tf_op jit(solution)/shard_map/ppermute | solution.py:37
  43.0 4.3 %collective-permute-start.11 = (bf16[2,48,384]{2,1,0:T(8,128)(2,1)S(1)}, bf16[2,48,384]{2,1,0:T(8,128)(2,1)S(1)}, u32[]{:S(2)}, u32[]{:S(2)}) collective-permute-start(bf16[2,48,384]{2,1,0:T(8,128)(2,1)S(1)} %get-tuple-element.33), channel_id=1, source_target_pairs={{0,6},{1,7},{2,0},{3,1},{4,2},{5,3},{6,4},{7,5},{8,14},{9,15},{10,... | collective-permute-start | bytes 221192 | tf_op jit(solution)/shard_map/ppermute | solution.py:37
  43.9 4.4 %collective-permute-start.12 = (bf16[2,48,384]{2,1,0:T(8,128)(2,1)S(1)}, bf16[2,48,384]{2,1,0:T(8,128)(2,1)S(1)}, u32[]{:S(2)}, u32[]{:S(2)}) collective-permute-start(bf16[2,48,384]{2,1,0:T(8,128)(2,1)S(1)} %get-tuple-element.34), channel_id=1, source_target_pairs={{0,2},{1,3},{2,4},{3,5},{4,6},{5,7},{6,0},{7,1},{8,10},{9,11},{10,... | collective-permute-start | bytes 221192 | tf_op jit(solution)/shard_map/ppermute | solution.py:37
  44.6 6.8 %collective-permute-start.6 = (bf16[2,48,384]{2,1,0:T(8,128)(2,1)S(1)}, bf16[2,48,384]{2,1,0:T(8,128)(2,1)S(1)}, u32[]{:S(2)}, u32[]{:S(2)}) collective-permute-start(bf16[2,48,384]{2,1,0:T(8,128)(2,1)S(1)} %get-tuple-element.26), channel_id=1, source_target_pairs={{0,4},{1,5},{2,6},{3,7},{4,0},{5,1},{6,2},{7,3},{8,12},{9,13},{10,... | collective-permute-start | bytes 221192 | tf_op jit(solution)/shard_map/ppermute | solution.py:37
  45.3 6.1 %collective-permute-start.7 = (bf16[2,48,384]{2,1,0:T(8,128)(2,1)S(1)}, bf16[2,48,384]{2,1,0:T(8,128)(2,1)S(1)}, u32[]{:S(2)}, u32[]{:S(2)}) collective-permute-start(bf16[2,48,384]{2,1,0:T(8,128)(2,1)S(1)} %get-tuple-element.27), channel_id=1, source_target_pairs={{0,6},{1,7},{2,0},{3,1},{4,2},{5,3},{6,4},{7,5},{8,14},{9,15},{10,... | collective-permute-start | bytes 221192 | tf_op jit(solution)/shard_map/ppermute | solution.py:37
  47.4 4.8 %collective-permute-start.8 = (bf16[2,48,384]{2,1,0:T(8,128)(2,1)S(1)}, bf16[2,48,384]{2,1,0:T(8,128)(2,1)S(1)}, u32[]{:S(2)}, u32[]{:S(2)}) collective-permute-start(bf16[2,48,384]{2,1,0:T(8,128)(2,1)S(1)} %get-tuple-element.28), channel_id=1, source_target_pairs={{0,2},{1,3},{2,4},{3,5},{4,6},{5,7},{6,0},{7,1},{8,10},{9,11},{10,... | collective-permute-start | bytes 221192 | tf_op jit(solution)/shard_map/ppermute | solution.py:37
  48.4 4.8 %collective-permute-start.13 = (bf16[2,48,384]{2,1,0:T(8,128)(2,1)S(1)}, bf16[2,48,384]{2,1,0:T(8,128)(2,1)S(1)}, u32[]{:S(2)}, u32[]{:S(2)}) collective-permute-start(bf16[2,48,384]{2,1,0:T(8,128)(2,1)S(1)} %add_x.1), channel_id=1, source_target_pairs={{0,8},{1,9},{2,10},{3,11},{4,12},{5,13},{6,14},{7,15},{8,0},{9,1},... | collective-permute-start | bytes 221192 | tf_op jit(solution)/shard_map/ppermute | solution.py:37
  53.3 6.7 %collective-permute-start.14 = (f32[2,48,256]{2,1,0:T(8,128)S(1)}, f32[2,48,256]{2,1,0:T(8,128)S(1)}, u32[]{:S(2)}, u32[]{:S(2)}) collective-permute-start(f32[2,48,256]{2,1,0:T(8,128)S(1)} %get-tuple-element.35), channel_id=1, source_target_pairs={{0,192},{1,81},{2,194},{3,83},{4,196},{5,85},{6,198},{7,87},{8,200... | collective-permute-start | bytes 294920 | tf_op jit(solution)/shard_map/ppermute | solution.py:46
  55.1 8.6 %collective-permute-start.16 = (f32[2,48,128]{2,1,0:T(8,128)S(1)}, f32[2,48,128]{2,1,0:T(8,128)S(1)}, u32[]{:S(2)}, u32[]{:S(2)}) collective-permute-start(f32[2,48,128]{2,1,0:T(8,128)S(1)} %get-tuple-element.36), channel_id=1, source_target_pairs={{0,224},{1,33},{2,226},{3,35},{4,228},{5,37},{6,230},{7,39},{8,232... | collective-permute-start | bytes 147464 | tf_op jit(solution)/shard_map/ppermute | solution.py:46
  60.0 6.2 %collective-permute-start.15 = (f32[48,256]{1,0:T(8,128)S(1)}, f32[48,256]{1,0:T(8,128)S(1)}, u32[]{:S(2)}, u32[]{:S(2)}) collective-permute-start(f32[48,256]{1,0:T(8,128)S(1)} %slice_bitcast_fusion), channel_id=1, source_target_pairs={{0,1},{1,0},{2,3},{3,2},{4,5},{5,4},{6,7},{7,6},{8,9},{9,8},{10,11... | collective-permute-start | bytes 147464 | tf_op jit(solution)/shard_map/ppermute | solution.py:37
  63.7 2.5 %collective-permute-start.17 = (f32[48,128]{1,0:T(8,128)S(1)}, f32[48,128]{1,0:T(8,128)S(1)}, u32[]{:S(2)}, u32[]{:S(2)}) collective-permute-start(f32[48,128]{1,0:T(8,128)S(1)} %slice_bitcast_fusion.1), channel_id=1, source_target_pairs={{0,1},{1,0},{2,3},{3,2},{4,5},{5,4},{6,7},{7,6},{8,9},{9,8},{10,11... | collective-permute-start | bytes 73736 | tf_op jit(solution)/shard_map/ppermute | solution.py:37

commit v5 on v4

--- a/solution.py
+++ b/solution.py
@@ -58,12 +58,25 @@
     return lax.rem(lax.axis_index("col"), 2)
 
 
+class Halves:
+    def __init__(self, one, two):
+        self.parts = one, two
+
+    def __getitem__(self, at):
+        tile, rest = (at[0], at[1:]) if isinstance(at, tuple) else (at, ())
+        return self.parts[tile // CHUNK][(tile % CHUNK, *rest)]
+
+    def __setitem__(self, tile, value):
+        self.parts[tile // CHUNK][tile % CHUNK] = value
+
+
 def tiles_of(c):
     start, within = CHUNK * (c // 6), c % 6
     return start + 2 * within, start + 2 * within + 1, start + 12 + within % 3, within // 3
 
 
-def pack_kernel(factors, packed):
+def pack_kernel(factors, one, two):
+    packed = Halves(one, two)
     for c in range(SLAB):
         first, second, last, half = tiles_of(c)
         packed[first] = factors[c, :, 0:LANE]
@@ -76,9 +89,9 @@
 def pack_block(factors):
     return pl.pallas_call(
         pack_kernel,
-        out_shape=jax.ShapeDtypeStruct((2 * CHUNK, ROWS, LANE), BF16),
+        out_shape=(jax.ShapeDtypeStruct((CHUNK, ROWS, LANE), BF16),) * 2,
         in_specs=full(1),
-        out_specs=full(1)[0],
+        out_specs=tuple(full(2)),
         compiler_params=params(),
         name="pack",
     )(jnp.transpose(factors, (1, 0, 2)))
@@ -116,10 +129,16 @@
             products[g, d * rows:(d + 1) * rows, :] = part.astype(BF16)
 
 
-def first_kernel(center, m1, own, p1, m2, p2, weights, raw, held, arrived, left, products):
+def paired(refs):
+    return [Halves(refs[at], refs[at + 1]) for at in range(0, len(refs), 2)]
+
+
+def first_kernel(*refs):
+    m1, own, p1, m2, p2 = paired(refs[:10])
+    weights, raw, held, arrived, left, products = refs[10:]
     copy = pltpu.make_async_copy(weights, held, arrived)
     copy.start()
-    build_left(center, left)
+    build_left(m2, left)
     build_products(left, m1, own, p1, m2, p2, products)
     copy.wait()
     for g in range(GROUPS):
@@ -168,14 +187,28 @@
     return lax.div(lax.axis_index("col"), 8)
 
 
-def second_kernel(center, m1, own, p1, m2, p2, weights, raw, keep, send, products, left):
+def second_kernel(*refs):
+    center, m1, own, p1, m2, p2 = paired(refs[:12])
+    weights, raw, keep, send, products, left = refs[12:]
     build_left(center, left)
     build_products(left, p1, own, m1, m2, p2, products)
     share(weights, products, raw, keep, send, 1 - y_hi_here())
 
 
-def last_kernel(products, weights, raw, keep, send):
+def last_kernel(products, weights, raw, vir_energy, pair_energy, keep, send, divisor, energy, pair, arrived):
+    copies = (pltpu.make_async_copy(vir_energy, energy, arrived.at[0]),
+              pltpu.make_async_copy(pair_energy, pair, arrived.at[1]))
+    for copy in copies:
+        copy.start()
     share(weights, products, raw, keep, send, y_hi_here())
+    for copy in copies:
+        copy.wait()
+    shape = divisor.shape
+    second = jnp.broadcast_to(energy[...].reshape(1, shape[1]), shape)
+    row = lax.axis_index("row") * ROWS + lax.broadcasted_iota(jnp.int32, shape, 0)
+    mine = lax.broadcasted_iota(jnp.int32, shape, 1) == row
+    first = jnp.sum(jnp.where(mine, second, 0.0), axis=1, keepdims=True)
+    divisor[...] = first + second - pair[lax.axis_index("col")]
 
 
 def scratch():
@@ -193,17 +226,17 @@
     return pl.CostEstimate(flops=10_000_000_000, bytes_accessed=4_000_000, transcendentals=0)
 
 
-def first_star(center, others, weights):
+def first_star(others, weights):
     return pl.pallas_call(
         first_kernel,
         out_shape=jax.ShapeDtypeStruct((GROUPS, 2 * PAIRS * GROUP, WIDE), F32),
-        in_specs=full(6) + [pl.BlockSpec(memory_space=pl.ANY)],
+        in_specs=full(10) + [pl.BlockSpec(memory_space=pl.ANY)],
         out_specs=full(1)[0],
         scratch_shapes=weights_scratch() + scratch(),
         compiler_params=params(),
         cost_estimate=star_cost(),
         name="first_star",
-    )(center, *others, weights)
+    )(*others, weights)
 
 
 def halves():
@@ -215,23 +248,28 @@
     return pl.pallas_call(
         second_kernel,
         out_shape=halves() + (jax.ShapeDtypeStruct((GROUPS, DEPTH, WIDE), BF16),),
-        in_specs=full(8),
+        in_specs=full(14),
         out_specs=tuple(full(3)),
         scratch_shapes=scratch()[:1],
         compiler_params=params(),
         name="second_star",
-    )(center, *others, weights, raw)
-
-
-def last_star(products, weights, raw):
+    )(*center, *others, weights, raw)
+
+
+def last_star(products, weights, raw, vir_energy, pair_energy):
     return pl.pallas_call(
         last_kernel,
-        out_shape=halves(),
-        in_specs=full(3),
-        out_specs=tuple(full(2)),
+        out_shape=halves() + (jax.ShapeDtypeStruct((ROWS, 16 * ROWS), F32),),
+        in_specs=full(3) + [pl.BlockSpec(memory_space=pl.ANY)] * 2,
+        out_specs=tuple(full(3)),
+        scratch_shapes=[
+            pltpu.VMEM(vir_energy.shape, F32),
+            pltpu.SMEM(pair_energy.shape, F32),
+            pltpu.SemaphoreType.DMA((2,)),
+        ],
         compiler_params=params(),
         name="last_star",
-    )(products, weights, raw)
+    )(products, weights, raw, vir_energy, pair_energy)
 
 
 def core_kernel(keep, got, *outs):
@@ -345,19 +383,16 @@
     )(*parts)
 
 
-def setup_kernel(amplitudes, energy, pair, weights, divisor):
-    shape = divisor.shape
-    second = jnp.broadcast_to(energy[...].reshape(1, shape[1]), shape)
-    row = lax.axis_index("row") * ROWS + lax.broadcasted_iota(jnp.int32, shape, 0)
-    mine = lax.broadcasted_iota(jnp.int32, shape, 1) == row
-    first = jnp.sum(jnp.where(mine, second, 0.0), axis=1, keepdims=True)
-    divisor[...] = first + second - pair[lax.axis_index("col")]
-    flat = amplitudes[...].reshape(SLAB * PAIRS, SLAB)
+def weights_kernel(amplitudes, weights, held, arrived):
+    copy = pltpu.make_async_copy(amplitudes, held, arrived)
+    copy.start()
     column = lax.broadcasted_iota(jnp.int32, (1, DEPTH), 1)
     slab = lax.broadcasted_iota(jnp.int32, (SLAB, DEPTH), 0)
     within = lax.broadcasted_iota(jnp.int32, (PAIRS * GROUP, DEPTH), 0)
     same = lax.rem(within, GROUP) == lax.rem(column, GROUP)
     d, c = lax.div(column, SLAB * GROUP), lax.rem(lax.div(column, GROUP), SLAB)
+    copy.wait()
+    flat = held[...].reshape(SLAB * PAIRS, SLAB)
     for order, (outer, inner) in enumerate(((c, d), (d, c))):
         spread = jnp.where(slab == inner, 1.0, 0.0).astype(BF16)
         wide = jnp.dot(flat, spread, preferred_element_type=F32).reshape(SLAB, PAIRS, DEPTH)
@@ -368,30 +403,34 @@
         weights[order * PAIRS * GROUP:(order + 1) * PAIRS * GROUP, :] = jnp.where(same, total, 0.0).astype(BF16)
 
 
-def setup(amplitudes, vir_energy, pair_energy):
-    return pl.pallas_call(
-        setup_kernel,
-        out_shape=(jax.ShapeDtypeStruct((2 * PAIRS * GROUP, DEPTH), BF16), jax.ShapeDtypeStruct((ROWS, 16 * ROWS), F32)),
-        in_specs=full(2) + [pl.BlockSpec(memory_space=pltpu.SMEM)],
-        out_specs=tuple(full(2)),
-        compiler_params=params(),
-        name="setup",
-    )(jnp.transpose(amplitudes, (1, 0, 2)), vir_energy, pair_energy)
+def contraction_weights(amplitudes):
+    return pl.pallas_call(
+        weights_kernel,
+        out_shape=jax.ShapeDtypeStruct((2 * PAIRS * GROUP, DEPTH), BF16),
+        in_specs=[pl.BlockSpec(memory_space=pl.ANY)],
+        out_specs=full(1)[0],
+        scratch_shapes=[pltpu.VMEM((SLAB, PAIRS, SLAB), BF16), pltpu.SemaphoreType.DMA],
+        compiler_params=params(),
+        name="weights",
+    )(jnp.transpose(amplitudes, (1, 0, 2)))
 
 
 def per_device(factors, amplitudes, vir_energy, pair_energy):
+    def moved(block, **by):
+        return [shift(part, **by) for part in block]
+
     own = pack_block(factors)
-    p1 = shift(own, dz=-1)
-    m1 = shift(own, dz=1)
-    weights, divisor = setup(amplitudes, vir_energy, pair_energy)
-    p2 = shift(p1, dz=-1)
-    m2 = shift(m1, dz=1)
-    cross = shift(p2, dy=1)
-    others = (m1, own, p1, m2, p2)
-    raw = first_star(m2, others, weights)
+    p1 = moved(own, dz=-1)
+    m1 = moved(own, dz=1)
+    weights = contraction_weights(amplitudes)
+    p2 = moved(p1, dz=-1)
+    m2 = moved(m1, dz=1)
+    cross = moved(p2, dy=1)
+    others = (*m1, *own, *p1, *m2, *p2)
+    raw = first_star(others, weights)
     keep, send, products = second_star(cross, others, weights, raw)
     far = add_cores(keep, shift(send, dc=1))
-    keep, send = last_star(products, weights, raw)
+    keep, send, divisor = last_star(products, weights, raw, vir_energy, pair_energy)
     near = add_cores(keep, shift(send, dc=1))
 
     def along_x(stay, one, two, three):

time: 67.6 us -> 63.9 us (0.945)
  waiting for transfers between devices: 19.8 us -> 16.4 us
  local copies, waits for them, and re-layouts: 3.15 us -> 1.82 us
  starting transfers between devices: 34.4 us -> 35.7 us
    ppermute x16 -> x21, waiting for transfers between devices: 17.3 us -> 10.3 us  [shift(): return lax.ppermute(array, ('row', 'col'), pairs)]
    ppermute x16 -> x21, starting transfers between devices: 30.2 us -> 34.8 us  [shift(): return lax.ppermute(array, ('row', 'col'), pairs)]
    ppermute x2, waiting for transfers between devices: 2.53 us -> 6.05 us  [to_rows(): return lax.ppermute(array, ('row', 'col'), pairs)]
    ppermute x2, starting transfers between devices: 4.13 us -> 0.91 us  [to_rows(): return lax.ppermute(array, ('row', 'col'), pairs)]
    unnamed x8, local copies, waits for them, and re-layouts: 3.14 us -> 1.82 us
  transfers between devices with their start and end apart: 18 -> 23, of which waited for: 10 -> 12; matrix products, arithmetic and copies ran while one was open for 0% -> 0% of each run, Pallas kernels for 8% -> 8%
where the time goes in v5:
time: 63.9 us; the launch traced here: 63.7 us
  starting transfers between devices  35.7 us (56%)
  waiting for transfers between devices  16.4 us (26%)
  Pallas kernels  9.04 us (14%)
  local copies, waits for them, and re-layouts  1.82 us (3%)
  between operations  0.76 us (1%)
    ppermute x21, starting transfers between devices, shift(): return lax.ppermute(array, ('row', 'col'), pairs)  34.8 us
    ppermute x21, waiting for transfers between devices, shift(): return lax.ppermute(array, ('row', 'col'), pairs)  10.3 us
    ppermute x2, waiting for transfers between devices, to_rows(): return lax.ppermute(array, ('row', 'col'), pairs)  6.05 us
    pallas_call x1, Pallas kernels, first_star(): pl.pallas_call(first_kernel, out_shape=jax.ShapeDtypeStruct((GROUPS, 2 *...  3.36 us
    pallas_call x1, Pallas kernels, second_star(): pl.pallas_call(second_kernel, out_shape=halves() + (jax.ShapeDtypeStruct(...  2.61 us
    unnamed x8, local copies, waits for them, and re-layouts  1.82 us
  transfers between devices with their start and end apart: 23, of which 12 were waited for; matrix products, arithmetic and copies ran while one was open for 0% of the time, Pallas kernels for 8%

profile of v5, /device:TPU:1, one launch (start us, length us, event | category | flops | bytes accessed | tf_op | source)
XLA Modules:
  0.0 63.7 jit_solution(15604980349278003710)
XLA Ops:
  0.6 1.0 %copy-done = bf16[48,12,320]{2,0,1:T(8,128)(2,1)S(1)} copy-done((bf16[48,12,320]{2,0,1:T(8,128)(2,1)S(1)}, bf16[48,12,320]{2,0,1:T(8,128)(2,1)}, u32[]{:S(2)}) %copy-start) | copy-done | bytes 368664
  1.7 6.5 %collective-permute-start = (bf16[15,48,128]{2,1,0:T(8,128)(2,1)S(1)}, bf16[15,48,128]{2,1,0:T(8,128)(2,1)S(1)}, u32[]{:S(2)}, u32[]{:S(2)}) collective-permute-start(bf16[15,48,128]{2,1,0:T(8,128)(2,1)S(1)} %get-tuple-element.22.refs_2_.refs_4_), channel_id=1, source_target_pairs={{0,224},{1,225},{2,226},{3,227},{4,228},{5,229},{6,230},{7,231},{8... | collective-permute-start | bytes 552968 | tf_op jit(solution)/shard_map/ppermute | solution.py:37
  9.7 1.8 %collective-permute-done.refs_4_.refs_6_ = bf16[15,48,128]{2,1,0:T(8,128)(2,1)S(1)} collective-permute-done((bf16[15,48,128]{2,1,0:T(8,128)(2,1)S(1)}, bf16[15,48,128]{2,1,0:T(8,128)(2,1)S(1)}, u32[]{:S(2)}, u32[]{:S(2)}) %collective-permute-start) | collective-permute-done | bytes 184352 | tf_op jit(solution)/shard_map/ppermute | solution.py:37
  11.5 3.4 %collective-permute-start.1 = (bf16[15,48,128]{2,1,0:T(8,128)(2,1)S(1)}, bf16[15,48,128]{2,1,0:T(8,128)(2,1)S(1)}, u32[]{:S(2)}, u32[]{:S(2)}) collective-permute-start(bf16[15,48,128]{2,1,0:T(8,128)(2,1)S(1)} %collective-permute-done.refs_4_.refs_6_), channel_id=1, source_target_pairs={{0,224},{1,225},{2,226},{3,227},{4,228},{5,229},{6,230},{7,231},{8... | collective-permute-start | bytes 552968 | tf_op jit(solution)/shard_map/ppermute | solution.py:37
  15.5 3.4 %collective-permute-start.4 = (bf16[15,48,128]{2,1,0:T(8,128)(2,1)S(1)}, bf16[15,48,128]{2,1,0:T(8,128)(2,1)S(1)}, u32[]{:S(2)}, u32[]{:S(2)}) collective-permute-start(bf16[15,48,128]{2,1,0:T(8,128)(2,1)S(1)} %collective-permute-done.3.refs_5_.refs_7_), channel_id=1, source_target_pairs={{0,224},{1,225},{2,226},{3,227},{4,228},{5,229},{6,230},{7,231},{8... | collective-permute-start | bytes 552968 | tf_op jit(solution)/shard_map/ppermute | solution.py:37
  20.3 1.4 %collective-permute-start.2 = (bf16[15,48,128]{2,1,0:T(8,128)(2,1)S(1)}, bf16[15,48,128]{2,1,0:T(8,128)(2,1)S(1)}, u32[]{:S(2)}, u32[]{:S(2)}) collective-permute-start(bf16[15,48,128]{2,1,0:T(8,128)(2,1)S(1)} %collective-permute-done.1.refs_8_.refs_10_), channel_id=1, source_target_pairs={{0,16},{1,17},{2,18},{3,19},{4,20},{5,21},{6,22},{7,23},{8,24},{9,... | collective-permute-start | bytes 552968 | tf_op jit(solution)/shard_map/ppermute | solution.py:37
  22.6 1.3 %collective-permute-start.5 = (bf16[15,48,128]{2,1,0:T(8,128)(2,1)S(1)}, bf16[15,48,128]{2,1,0:T(8,128)(2,1)S(1)}, u32[]{:S(2)}, u32[]{:S(2)}) collective-permute-start(bf16[15,48,128]{2,1,0:T(8,128)(2,1)S(1)} %collective-permute-done.4.refs_9_.refs_11_), channel_id=1, source_target_pairs={{0,16},{1,17},{2,18},{3,19},{4,20},{5,21},{6,22},{7,23},{8,24},{9,... | collective-permute-start | bytes 552968 | tf_op jit(solution)/shard_map/ppermute | solution.py:37
  24.5 2.7 %collective-permute-done.9.refs_7_.refs_9_ = bf16[15,48,128]{2,1,0:T(8,128)(2,1)S(1)} collective-permute-done((bf16[15,48,128]{2,1,0:T(8,128)(2,1)S(1)}, bf16[15,48,128]{2,1,0:T(8,128)(2,1)S(1)}, u32[]{:S(2)}, u32[]{:S(2)}) %collective-permute-start.9) | collective-permute-done | bytes 184352 | tf_op jit(solution)/shard_map/ppermute | solution.py:37
  27.2 3.4 %first_star.1.refs_13_.raw = f32[6,256,256]{2,1,0:T(8,128)S(1)} custom-call(bf16[15,48,128]{2,1,0:T(8,128)(2,1)S(1)} %collective-permute-done.6.refs_0_.refs_2_, bf16[15,48,128]{2,1,0:T(8,128)(2,1)S(1)} %collective-permute-done.7.refs_1_.refs_3_, bf16[15,48,128]{2,1,0:T(8,128)(2,1)S(1)} %get-tuple-element.22.refs_2_.refs_4_, ...), custom_call_target="tpu_custom_call" | custom-call | flops 10000000000 | bytes 4000000 | tf_op jit(solution)/shard_map/first_star/pallas_call | solution.py:230
  30.6 2.6 %second_star.1 = (f32[4,2,48,384]{3,2,1,0:T(8,128)S(1)}, bf16[4,2,48,384]{3,2,1,0:T(8,128)(2,1)S(1)}, bf16[6,1152,256]{2,1,0:T(8,128)(2,1)S(1)}) custom-call(bf16[15,48,128]{2,1,0:T(8,128)(2,1)S(1)} %collective-permute-done.2.refs_0_, bf16[15,48,128]{2,1,0:T(8,128)(2,1)S(1)} %collective-permute-done.5.refs_1_, ...), custom_call_target="tpu_custom_call" | custom-call | tf_op jit(solution)/shard_map/second_star/pallas_call | solution.py:248
  33.2 4.2 %collective-permute-start.14 = (bf16[4,2,48,384]{3,2,1,0:T(8,128)(2,1)S(1)}, bf16[4,2,48,384]{3,2,1,0:T(8,128)(2,1)S(1)}, u32[]{:S(2)}, u32[]{:S(2)}) collective-permute-start(bf16[4,2,48,384]{3,2,1,0:T(8,128)(2,1)S(1)} %get-tuple-element.32), channel_id=1, source_target_pairs={{0,1},{1,0},{2,3},{3,2},{4,5},{5,4},{6,7},{7,6},{8,9},{9,8},{10,11... | collective-permute-start | bytes 884744 | tf_op jit(solution)/shard_map/ppermute | solution.py:37
  37.4 1.0 %last_star.1 = (f32[4,2,48,384]{3,2,1,0:T(8,128)S(1)}, bf16[4,2,48,384]{3,2,1,0:T(8,128)(2,1)S(1)}, f32[48,768]{1,0:T(8,128)S(1)}) custom-call(bf16[6,1152,256]{2,1,0:T(8,128)(2,1)S(1)} %get-tuple-element.24.products, bf16[256,1152]{1,0:T(8,128)(2,1)S(1)} %weights.1.refs_10_.refs_12_, f32[6,256,256]{2,1,0:T(8,128)S(1)} %first_star.1.refs_13_.raw, ...), custom_call_target="tpu_custom_call" | custom-call | tf_op jit(solution)/shard_map/last_star/pallas_call | solution.py:260
  38.7 2.8 %collective-permute-start.15 = (bf16[2,48,384]{2,1,0:T(8,128)(2,1)S(1)}, bf16[2,48,384]{2,1,0:T(8,128)(2,1)S(1)}, u32[]{:S(2)}, u32[]{:S(2)}) collective-permute-start(bf16[2,48,384]{2,1,0:T(8,128)(2,1)S(1)} %get-tuple-element.34), channel_id=1, source_target_pairs={{0,4},{1,5},{2,6},{3,7},{4,0},{5,1},{6,2},{7,3},{8,12},{9,13},{10,... | collective-permute-start | bytes 221192 | tf_op jit(solution)/shard_map/ppermute | solution.py:37
  41.5 0.9 %collective-permute-start.16 = (bf16[2,48,384]{2,1,0:T(8,128)(2,1)S(1)}, bf16[2,48,384]{2,1,0:T(8,128)(2,1)S(1)}, u32[]{:S(2)}, u32[]{:S(2)}) collective-permute-start(bf16[2,48,384]{2,1,0:T(8,128)(2,1)S(1)} %get-tuple-element.35), channel_id=1, source_target_pairs={{0,6},{1,7},{2,0},{3,1},{4,2},{5,3},{6,4},{7,5},{8,14},{9,15},{10,... | collective-permute-start | bytes 221192 | tf_op jit(solution)/shard_map/ppermute | solution.py:37
  43.8 2.1 %collective-permute-start.12 = (bf16[2,48,384]{2,1,0:T(8,128)(2,1)S(1)}, bf16[2,48,384]{2,1,0:T(8,128)(2,1)S(1)}, u32[]{:S(2)}, u32[]{:S(2)}) collective-permute-start(bf16[2,48,384]{2,1,0:T(8,128)(2,1)S(1)} %get-tuple-element.29), channel_id=1, source_target_pairs={{0,6},{1,7},{2,0},{3,1},{4,2},{5,3},{6,4},{7,5},{8,14},{9,15},{10,... | collective-permute-start | bytes 221192 | tf_op jit(solution)/shard_map/ppermute | solution.py:37
  45.9 0.9 %collective-permute-done.17.one = bf16[2,48,384]{2,1,0:T(8,128)(2,1)S(1)} collective-permute-done((bf16[2,48,384]{2,1,0:T(8,128)(2,1)S(1)}, bf16[2,48,384]{2,1,0:T(8,128)(2,1)S(1)}, u32[]{:S(2)}, u32[]{:S(2)}) %collective-permute-start.17) | collective-permute-done | bytes 73760 | tf_op jit(solution)/shard_map/ppermute | solution.py:37
  46.8 3.0 %collective-permute-start.18 = (bf16[2,48,384]{2,1,0:T(8,128)(2,1)S(1)}, bf16[2,48,384]{2,1,0:T(8,128)(2,1)S(1)}, u32[]{:S(2)}, u32[]{:S(2)}) collective-permute-start(bf16[2,48,384]{2,1,0:T(8,128)(2,1)S(1)} %add_x.1), channel_id=1, source_target_pairs={{0,8},{1,9},{2,10},{3,11},{4,12},{5,13},{6,14},{7,15},{8,0},{9,1},... | collective-permute-start | bytes 221192 | tf_op jit(solution)/shard_map/ppermute | solution.py:37
  49.8 0.9 %collective-permute-done.13.one = bf16[2,48,384]{2,1,0:T(8,128)(2,1)S(1)} collective-permute-done((bf16[2,48,384]{2,1,0:T(8,128)(2,1)S(1)}, bf16[2,48,384]{2,1,0:T(8,128)(2,1)S(1)}, u32[]{:S(2)}, u32[]{:S(2)}) %collective-permute-start.13) | collective-permute-done | bytes 73760 | tf_op jit(solution)/shard_map/ppermute | solution.py:37
  50.7 0.9 %collective-permute-done.18.got = bf16[2,48,384]{2,1,0:T(8,128)(2,1)S(1)} collective-permute-done((bf16[2,48,384]{2,1,0:T(8,128)(2,1)S(1)}, bf16[2,48,384]{2,1,0:T(8,128)(2,1)S(1)}, u32[]{:S(2)}, u32[]{:S(2)}) %collective-permute-start.18) | collective-permute-done | bytes 73760 | tf_op jit(solution)/shard_map/ppermute | solution.py:37
  51.9 0.8 %collective-permute-start.21 = (f32[2,48,128]{2,1,0:T(8,128)S(1)}, f32[2,48,128]{2,1,0:T(8,128)S(1)}, u32[]{:S(2)}, u32[]{:S(2)}) collective-permute-start(f32[2,48,128]{2,1,0:T(8,128)S(1)} %get-tuple-element.38), channel_id=1, source_target_pairs={{0,224},{1,33},{2,226},{3,35},{4,228},{5,37},{6,230},{7,39},{8,232... | collective-permute-start | bytes 147464 | tf_op jit(solution)/shard_map/ppermute | solution.py:46
  52.7 6.0 %collective-permute-done.19.plain = f32[2,48,256]{2,1,0:T(8,128)S(1)} collective-permute-done((f32[2,48,256]{2,1,0:T(8,128)S(1)}, f32[2,48,256]{2,1,0:T(8,128)S(1)}, u32[]{:S(2)}, u32[]{:S(2)}) %collective-permute-start.19) | collective-permute-done | bytes 98336 | tf_op jit(solution)/shard_map/ppermute | solution.py:46
  58.8 2.4 %collective-permute-start.20 = (f32[48,256]{1,0:T(8,128)S(1)}, f32[48,256]{1,0:T(8,128)S(1)}, u32[]{:S(2)}, u32[]{:S(2)}) collective-permute-start(f32[48,256]{1,0:T(8,128)S(1)} %slice_bitcast_fusion), channel_id=1, source_target_pairs={{0,1},{1,0},{2,3},{3,2},{4,5},{5,4},{6,7},{7,6},{8,9},{9,8},{10,11... | collective-permute-start | bytes 147464 | tf_op jit(solution)/shard_map/ppermute | solution.py:37
  61.7 0.8 %collective-permute-done.22.mirror_other = f32[48,128]{1,0:T(8,128)S(1)} collective-permute-done((f32[48,128]{1,0:T(8,128)S(1)}, f32[48,128]{1,0:T(8,128)S(1)}, u32[]{:S(2)}, u32[]{:S(2)}) %collective-permute-start.22) | collective-permute-done | bytes 24608 | tf_op jit(solution)/shard_map/ppermute | solution.py:37
  62.6 1.1 %place.1 = (f32[1,48,768]{2,1,0:T(8,128)}, f32[1,48,768]{2,1,0:T(8,128)}) custom-call(f32[2,48,256]{2,1,0:T(8,128)S(1)} %collective-permute-done.19.plain, f32[48,256]{1,0:T(8,128)S(1)} %collective-permute-done.20.plain_other, f32[2,48,128]{2,1,0:T(8,128)S(1)} %collective-permute-done.21.mirror, f32[48,128]{1,0:T(8,128)S(1)} %collective-permute-done.22.mirror_other, ...), custom_call_target="tpu_custom_call" | custom-call | tf_op jit(solution)/shard_map/place/pallas_call | solution.py:376
  (42 shorter events, 7.5 us)
Async XLA Ops:
  1.7 9.8 %collective-permute-start = (bf16[15,48,128]{2,1,0:T(8,128)(2,1)S(1)}, bf16[15,48,128]{2,1,0:T(8,128)(2,1)S(1)}, u32[]{:S(2)}, u32[]{:S(2)}) collective-permute-start(bf16[15,48,128]{2,1,0:T(8,128)(2,1)S(1)} %get-tuple-element.22.refs_2_.refs_4_), channel_id=1, source_target_pairs={{0,224},{1,225},{2,226},{3,227},{4,228},{5,229},{6,230},{7,231},{8... | collective-permute-start | bytes 552968 | tf_op jit(solution)/shard_map/ppermute | solution.py:37
  8.2 7.3 %collective-permute-start.3 = (bf16[15,48,128]{2,1,0:T(8,128)(2,1)S(1)}, bf16[15,48,128]{2,1,0:T(8,128)(2,1)S(1)}, u32[]{:S(2)}, u32[]{:S(2)}) collective-permute-start(bf16[15,48,128]{2,1,0:T(8,128)(2,1)S(1)} %get-tuple-element.23.refs_3_.refs_5_), channel_id=1, source_target_pairs={{0,224},{1,225},{2,226},{3,227},{4,228},{5,229},{6,230},{7,231},{8... | collective-permute-start | bytes 552968 | tf_op jit(solution)/shard_map/ppermute | solution.py:37
  9.0 9.9 %collective-permute-start.6 = (bf16[15,48,128]{2,1,0:T(8,128)(2,1)S(1)}, bf16[15,48,128]{2,1,0:T(8,128)(2,1)S(1)}, u32[]{:S(2)}, u32[]{:S(2)}) collective-permute-start(bf16[15,48,128]{2,1,0:T(8,128)(2,1)S(1)} %get-tuple-element.22.refs_2_.refs_4_), channel_id=1, source_target_pairs={{0,32},{1,33},{2,34},{3,35},{4,36},{5,37},{6,38},{7,39},{8,40},{9,... | collective-permute-start | bytes 552968 | tf_op jit(solution)/shard_map/ppermute | solution.py:37
  9.7 9.3 %collective-permute-start.7 = (bf16[15,48,128]{2,1,0:T(8,128)(2,1)S(1)}, bf16[15,48,128]{2,1,0:T(8,128)(2,1)S(1)}, u32[]{:S(2)}, u32[]{:S(2)}) collective-permute-start(bf16[15,48,128]{2,1,0:T(8,128)(2,1)S(1)} %get-tuple-element.23.refs_3_.refs_5_), channel_id=1, source_target_pairs={{0,32},{1,33},{2,34},{3,35},{4,36},{5,37},{6,38},{7,39},{8,40},{9,... | collective-permute-start | bytes 552968 | tf_op jit(solution)/shard_map/ppermute | solution.py:37
  11.5 8.8 %collective-permute-start.1 = (bf16[15,48,128]{2,1,0:T(8,128)(2,1)S(1)}, bf16[15,48,128]{2,1,0:T(8,128)(2,1)S(1)}, u32[]{:S(2)}, u32[]{:S(2)}) collective-permute-start(bf16[15,48,128]{2,1,0:T(8,128)(2,1)S(1)} %collective-permute-done.refs_4_.refs_6_), channel_id=1, source_target_pairs={{0,224},{1,225},{2,226},{3,227},{4,228},{5,229},{6,230},{7,231},{8... | collective-permute-start | bytes 552968 | tf_op jit(solution)/shard_map/ppermute | solution.py:37
  15.5 7.1 %collective-permute-start.4 = (bf16[15,48,128]{2,1,0:T(8,128)(2,1)S(1)}, bf16[15,48,128]{2,1,0:T(8,128)(2,1)S(1)}, u32[]{:S(2)}, u32[]{:S(2)}) collective-permute-start(bf16[15,48,128]{2,1,0:T(8,128)(2,1)S(1)} %collective-permute-done.3.refs_5_.refs_7_), channel_id=1, source_target_pairs={{0,224},{1,225},{2,226},{3,227},{4,228},{5,229},{6,230},{7,231},{8... | collective-permute-start | bytes 552968 | tf_op jit(solution)/shard_map/ppermute | solution.py:37
  18.9 5.6 %collective-permute-start.8 = (bf16[15,48,128]{2,1,0:T(8,128)(2,1)S(1)}, bf16[15,48,128]{2,1,0:T(8,128)(2,1)S(1)}, u32[]{:S(2)}, u32[]{:S(2)}) collective-permute-start(bf16[15,48,128]{2,1,0:T(8,128)(2,1)S(1)} %collective-permute-done.6.refs_0_.refs_2_), channel_id=1, source_target_pairs={{0,32},{1,33},{2,34},{3,35},{4,36},{5,37},{6,38},{7,39},{8,40},{9,... | collective-permute-start | bytes 552968 | tf_op jit(solution)/shard_map/ppermute | solution.py:37
  19.0 8.2 %collective-permute-start.9 = (bf16[15,48,128]{2,1,0:T(8,128)(2,1)S(1)}, bf16[15,48,128]{2,1,0:T(8,128)(2,1)S(1)}, u32[]{:S(2)}, u32[]{:S(2)}) collective-permute-start(bf16[15,48,128]{2,1,0:T(8,128)(2,1)S(1)} %collective-permute-done.7.refs_1_.refs_3_), channel_id=1, source_target_pairs={{0,32},{1,33},{2,34},{3,35},{4,36},{5,37},{6,38},{7,39},{8,40},{9,... | collective-permute-start | bytes 552968 | tf_op jit(solution)/shard_map/ppermute | solution.py:37
  20.3 10.3 %collective-permute-start.2 = (bf16[15,48,128]{2,1,0:T(8,128)(2,1)S(1)}, bf16[15,48,128]{2,1,0:T(8,128)(2,1)S(1)}, u32[]{:S(2)}, u32[]{:S(2)}) collective-permute-start(bf16[15,48,128]{2,1,0:T(8,128)(2,1)S(1)} %collective-permute-done.1.refs_8_.refs_10_), channel_id=1, source_target_pairs={{0,16},{1,17},{2,18},{3,19},{4,20},{5,21},{6,22},{7,23},{8,24},{9,... | collective-permute-start | bytes 552968 | tf_op jit(solution)/shard_map/ppermute | solution.py:37
  22.6 8.1 %collective-permute-start.5 = (bf16[15,48,128]{2,1,0:T(8,128)(2,1)S(1)}, bf16[15,48,128]{2,1,0:T(8,128)(2,1)S(1)}, u32[]{:S(2)}, u32[]{:S(2)}) collective-permute-start(bf16[15,48,128]{2,1,0:T(8,128)(2,1)S(1)} %collective-permute-done.4.refs_9_.refs_11_), channel_id=1, source_target_pairs={{0,16},{1,17},{2,18},{3,19},{4,20},{5,21},{6,22},{7,23},{8,24},{9,... | collective-permute-start | bytes 552968 | tf_op jit(solution)/shard_map/ppermute | solution.py:37
  30.6 6.8 %copy-start.2 = (f32[768]{0:T(1024)S(1)}, f32[768]{0:T(1024)}, u32[]{:S(2)}) copy-start(f32[768]{0:T(1024)} %vir_energy.1) | copy-start | bytes 9220
  33.2 5.4 %collective-permute-start.14 = (bf16[4,2,48,384]{3,2,1,0:T(8,128)(2,1)S(1)}, bf16[4,2,48,384]{3,2,1,0:T(8,128)(2,1)S(1)}, u32[]{:S(2)}, u32[]{:S(2)}) collective-permute-start(bf16[4,2,48,384]{3,2,1,0:T(8,128)(2,1)S(1)} %get-tuple-element.32), channel_id=1, source_target_pairs={{0,1},{1,0},{2,3},{3,2},{4,5},{5,4},{6,7},{7,6},{8,9},{9,8},{10,11... | collective-permute-start | bytes 884744 | tf_op jit(solution)/shard_map/ppermute | solution.py:37
  38.4 4.6 %collective-permute-start.10 = (bf16[4,2,48,384]{3,2,1,0:T(8,128)(2,1)S(1)}, bf16[4,2,48,384]{3,2,1,0:T(8,128)(2,1)S(1)}, u32[]{:S(2)}, u32[]{:S(2)}) collective-permute-start(bf16[4,2,48,384]{3,2,1,0:T(8,128)(2,1)S(1)} %get-tuple-element.26), channel_id=1, source_target_pairs={{0,1},{1,0},{2,3},{3,2},{4,5},{5,4},{6,7},{7,6},{8,9},{9,8},{10,11... | collective-permute-start | bytes 884744 | tf_op jit(solution)/shard_map/ppermute | solution.py:37
  38.7 7.2 %collective-permute-start.15 = (bf16[2,48,384]{2,1,0:T(8,128)(2,1)S(1)}, bf16[2,48,384]{2,1,0:T(8,128)(2,1)S(1)}, u32[]{:S(2)}, u32[]{:S(2)}) collective-permute-start(bf16[2,48,384]{2,1,0:T(8,128)(2,1)S(1)} %get-tuple-element.34), channel_id=1, source_target_pairs={{0,4},{1,5},{2,6},{3,7},{4,0},{5,1},{6,2},{7,3},{8,12},{9,13},{10,... | collective-permute-start | bytes 221192 | tf_op jit(solution)/shard_map/ppermute | solution.py:37
  41.5 4.3 %collective-permute-start.16 = (bf16[2,48,384]{2,1,0:T(8,128)(2,1)S(1)}, bf16[2,48,384]{2,1,0:T(8,128)(2,1)S(1)}, u32[]{:S(2)}, u32[]{:S(2)}) collective-permute-start(bf16[2,48,384]{2,1,0:T(8,128)(2,1)S(1)} %get-tuple-element.35), channel_id=1, source_target_pairs={{0,6},{1,7},{2,0},{3,1},{4,2},{5,3},{6,4},{7,5},{8,14},{9,15},{10,... | collective-permute-start | bytes 221192 | tf_op jit(solution)/shard_map/ppermute | solution.py:37
  42.4 4.4 %collective-permute-start.17 = (bf16[2,48,384]{2,1,0:T(8,128)(2,1)S(1)}, bf16[2,48,384]{2,1,0:T(8,128)(2,1)S(1)}, u32[]{:S(2)}, u32[]{:S(2)}) collective-permute-start(bf16[2,48,384]{2,1,0:T(8,128)(2,1)S(1)} %get-tuple-element.36), channel_id=1, source_target_pairs={{0,2},{1,3},{2,4},{3,5},{4,6},{5,7},{6,0},{7,1},{8,10},{9,11},{10,... | collective-permute-start | bytes 221192 | tf_op jit(solution)/shard_map/ppermute | solution.py:37
  43.1 6.8 %collective-permute-start.11 = (bf16[2,48,384]{2,1,0:T(8,128)(2,1)S(1)}, bf16[2,48,384]{2,1,0:T(8,128)(2,1)S(1)}, u32[]{:S(2)}, u32[]{:S(2)}) collective-permute-start(bf16[2,48,384]{2,1,0:T(8,128)(2,1)S(1)} %get-tuple-element.28), channel_id=1, source_target_pairs={{0,4},{1,5},{2,6},{3,7},{4,0},{5,1},{6,2},{7,3},{8,12},{9,13},{10,... | collective-permute-start | bytes 221192 | tf_op jit(solution)/shard_map/ppermute | solution.py:37
  43.8 6.1 %collective-permute-start.12 = (bf16[2,48,384]{2,1,0:T(8,128)(2,1)S(1)}, bf16[2,48,384]{2,1,0:T(8,128)(2,1)S(1)}, u32[]{:S(2)}, u32[]{:S(2)}) collective-permute-start(bf16[2,48,384]{2,1,0:T(8,128)(2,1)S(1)} %get-tuple-element.29), channel_id=1, source_target_pairs={{0,6},{1,7},{2,0},{3,1},{4,2},{5,3},{6,4},{7,5},{8,14},{9,15},{10,... | collective-permute-start | bytes 221192 | tf_op jit(solution)/shard_map/ppermute | solution.py:37
  45.8 4.8 %collective-permute-start.13 = (bf16[2,48,384]{2,1,0:T(8,128)(2,1)S(1)}, bf16[2,48,384]{2,1,0:T(8,128)(2,1)S(1)}, u32[]{:S(2)}, u32[]{:S(2)}) collective-permute-start(bf16[2,48,384]{2,1,0:T(8,128)(2,1)S(1)} %get-tuple-element.30), channel_id=1, source_target_pairs={{0,2},{1,3},{2,4},{3,5},{4,6},{5,7},{6,0},{7,1},{8,10},{9,11},{10,... | collective-permute-start | bytes 221192 | tf_op jit(solution)/shard_map/ppermute | solution.py:37
  46.8 4.8 %collective-permute-start.18 = (bf16[2,48,384]{2,1,0:T(8,128)(2,1)S(1)}, bf16[2,48,384]{2,1,0:T(8,128)(2,1)S(1)}, u32[]{:S(2)}, u32[]{:S(2)}) collective-permute-start(bf16[2,48,384]{2,1,0:T(8,128)(2,1)S(1)} %add_x.1), channel_id=1, source_target_pairs={{0,8},{1,9},{2,10},{3,11},{4,12},{5,13},{6,14},{7,15},{8,0},{9,1},... | collective-permute-start | bytes 221192 | tf_op jit(solution)/shard_map/ppermute | solution.py:37
  51.8 7.0 %collective-permute-start.19 = (f32[2,48,256]{2,1,0:T(8,128)S(1)}, f32[2,48,256]{2,1,0:T(8,128)S(1)}, u32[]{:S(2)}, u32[]{:S(2)}) collective-permute-start(f32[2,48,256]{2,1,0:T(8,128)S(1)} %get-tuple-element.37), channel_id=1, source_target_pairs={{0,192},{1,81},{2,194},{3,83},{4,196},{5,85},{6,198},{7,87},{8,200... | collective-permute-start | bytes 294920 | tf_op jit(solution)/shard_map/ppermute | solution.py:46
  51.9 9.3 %collective-permute-start.21 = (f32[2,48,128]{2,1,0:T(8,128)S(1)}, f32[2,48,128]{2,1,0:T(8,128)S(1)}, u32[]{:S(2)}, u32[]{:S(2)}) collective-permute-start(f32[2,48,128]{2,1,0:T(8,128)S(1)} %get-tuple-element.38), channel_id=1, source_target_pairs={{0,224},{1,33},{2,226},{3,35},{4,228},{5,37},{6,230},{7,39},{8,232... | collective-permute-start | bytes 147464 | tf_op jit(solution)/shard_map/ppermute | solution.py:46
  58.8 3.8 %collective-permute-start.20 = (f32[48,256]{1,0:T(8,128)S(1)}, f32[48,256]{1,0:T(8,128)S(1)}, u32[]{:S(2)}, u32[]{:S(2)}) collective-permute-start(f32[48,256]{1,0:T(8,128)S(1)} %slice_bitcast_fusion), channel_id=1, source_target_pairs={{0,1},{1,0},{2,3},{3,2},{4,5},{5,4},{6,7},{7,6},{8,9},{9,8},{10,11... | collective-permute-start | bytes 147464 | tf_op jit(solution)/shard_map/ppermute | solution.py:37
  61.2 1.3 %collective-permute-start.22 = (f32[48,128]{1,0:T(8,128)S(1)}, f32[48,128]{1,0:T(8,128)S(1)}, u32[]{:S(2)}, u32[]{:S(2)}) collective-permute-start(f32[48,128]{1,0:T(8,128)S(1)} %slice_bitcast_fusion.1), channel_id=1, source_target_pairs={{0,1},{1,0},{2,3},{3,2},{4,5},{5,4},{6,7},{7,6},{8,9},{9,8},{10,11... | collective-permute-start | bytes 73736 | tf_op jit(solution)/shard_map/ppermute | solution.py:37
  (3 other events, 8.6 us)

commit v6 on v5

--- a/solution.py
+++ b/solution.py
@@ -339,7 +339,7 @@
     )(*parts)
 
 
-def place_kernel(plain, plain_other, mirror, mirror_other, stays, stays_other, divisor, residual, update):
+def place_kernel(mirror, mirror_other, plain, plain_other, stays, stays_other, divisor, residual, update):
     row = lax.axis_index("row")
     z, y_lo = lax.div(row, 2), lax.rem(row, 2)
     here = core_here() == 0
@@ -442,7 +442,7 @@
     mirror = to_rows(mirror, ((-1, 0), (1, 0)))
     plain_other = shift(plain[1], dc=1)
     mirror_other = shift(mirror[1], dc=1)
-    return place(plain, plain_other, mirror, mirror_other, stays, stays_other, divisor)
+    return place(mirror, mirror_other, plain, plain_other, stays, stays_other, divisor)
 
 
 def solution(mesh):

time: 63.9 us -> 63.9 us (level)
  no operation moved by 1% of the time
where the time goes in v6:
time: 63.9 us; the launch traced here: 63.7 us
  starting transfers between devices  35.7 us (56%)
  waiting for transfers between devices  16.4 us (26%)
  Pallas kernels  9.04 us (14%)
  local copies, waits for them, and re-layouts  1.82 us (3%)
  between operations  0.76 us (1%)
    ppermute x21, starting transfers between devices, shift(): return lax.ppermute(array, ('row', 'col'), pairs)  34.8 us
    ppermute x21, waiting for transfers between devices, shift(): return lax.ppermute(array, ('row', 'col'), pairs)  10.3 us
    ppermute x2, waiting for transfers between devices, to_rows(): return lax.ppermute(array, ('row', 'col'), pairs)  6.05 us
    pallas_call x1, Pallas kernels, first_star(): pl.pallas_call(first_kernel, out_shape=jax.ShapeDtypeStruct((GROUPS, 2 *...  3.36 us
    pallas_call x1, Pallas kernels, second_star(): pl.pallas_call(second_kernel, out_shape=halves() + (jax.ShapeDtypeStruct(...  2.61 us
    unnamed x8, local copies, waits for them, and re-layouts  1.82 us
  transfers between devices with their start and end apart: 23, of which 12 were waited for; matrix products, arithmetic and copies ran while one was open for 0% of the time, Pallas kernels for 8%

profile of v6, /device:TPU:1, one launch (start us, length us, event | category | flops | bytes accessed | tf_op | source)
XLA Modules:
  0.0 63.7 jit_solution(6343714277615032500)
XLA Ops:
  0.6 1.0 %copy-done = bf16[48,12,320]{2,0,1:T(8,128)(2,1)S(1)} copy-done((bf16[48,12,320]{2,0,1:T(8,128)(2,1)S(1)}, bf16[48,12,320]{2,0,1:T(8,128)(2,1)}, u32[]{:S(2)}) %copy-start) | copy-done | bytes 368664
  1.7 6.5 %collective-permute-start = (bf16[15,48,128]{2,1,0:T(8,128)(2,1)S(1)}, bf16[15,48,128]{2,1,0:T(8,128)(2,1)S(1)}, u32[]{:S(2)}, u32[]{:S(2)}) collective-permute-start(bf16[15,48,128]{2,1,0:T(8,128)(2,1)S(1)} %get-tuple-element.22.refs_2_.refs_4_), channel_id=1, source_target_pairs={{0,224},{1,225},{2,226},{3,227},{4,228},{5,229},{6,230},{7,231},{8... | collective-permute-start | bytes 552968 | tf_op jit(solution)/shard_map/ppermute | solution.py:37
  9.7 1.8 %collective-permute-done.refs_4_.refs_6_ = bf16[15,48,128]{2,1,0:T(8,128)(2,1)S(1)} collective-permute-done((bf16[15,48,128]{2,1,0:T(8,128)(2,1)S(1)}, bf16[15,48,128]{2,1,0:T(8,128)(2,1)S(1)}, u32[]{:S(2)}, u32[]{:S(2)}) %collective-permute-start) | collective-permute-done | bytes 184352 | tf_op jit(solution)/shard_map/ppermute | solution.py:37
  11.5 3.4 %collective-permute-start.1 = (bf16[15,48,128]{2,1,0:T(8,128)(2,1)S(1)}, bf16[15,48,128]{2,1,0:T(8,128)(2,1)S(1)}, u32[]{:S(2)}, u32[]{:S(2)}) collective-permute-start(bf16[15,48,128]{2,1,0:T(8,128)(2,1)S(1)} %collective-permute-done.refs_4_.refs_6_), channel_id=1, source_target_pairs={{0,224},{1,225},{2,226},{3,227},{4,228},{5,229},{6,230},{7,231},{8... | collective-permute-start | bytes 552968 | tf_op jit(solution)/shard_map/ppermute | solution.py:37
  15.5 3.4 %collective-permute-start.4 = (bf16[15,48,128]{2,1,0:T(8,128)(2,1)S(1)}, bf16[15,48,128]{2,1,0:T(8,128)(2,1)S(1)}, u32[]{:S(2)}, u32[]{:S(2)}) collective-permute-start(bf16[15,48,128]{2,1,0:T(8,128)(2,1)S(1)} %collective-permute-done.3.refs_5_.refs_7_), channel_id=1, source_target_pairs={{0,224},{1,225},{2,226},{3,227},{4,228},{5,229},{6,230},{7,231},{8... | collective-permute-start | bytes 552968 | tf_op jit(solution)/shard_map/ppermute | solution.py:37
  20.3 1.4 %collective-permute-start.2 = (bf16[15,48,128]{2,1,0:T(8,128)(2,1)S(1)}, bf16[15,48,128]{2,1,0:T(8,128)(2,1)S(1)}, u32[]{:S(2)}, u32[]{:S(2)}) collective-permute-start(bf16[15,48,128]{2,1,0:T(8,128)(2,1)S(1)} %collective-permute-done.1.refs_8_.refs_10_), channel_id=1, source_target_pairs={{0,16},{1,17},{2,18},{3,19},{4,20},{5,21},{6,22},{7,23},{8,24},{9,... | collective-permute-start | bytes 552968 | tf_op jit(solution)/shard_map/ppermute | solution.py:37
  22.6 1.3 %collective-permute-start.5 = (bf16[15,48,128]{2,1,0:T(8,128)(2,1)S(1)}, bf16[15,48,128]{2,1,0:T(8,128)(2,1)S(1)}, u32[]{:S(2)}, u32[]{:S(2)}) collective-permute-start(bf16[15,48,128]{2,1,0:T(8,128)(2,1)S(1)} %collective-permute-done.4.refs_9_.refs_11_), channel_id=1, source_target_pairs={{0,16},{1,17},{2,18},{3,19},{4,20},{5,21},{6,22},{7,23},{8,24},{9,... | collective-permute-start | bytes 552968 | tf_op jit(solution)/shard_map/ppermute | solution.py:37
  24.5 2.7 %collective-permute-done.9.refs_7_.refs_9_ = bf16[15,48,128]{2,1,0:T(8,128)(2,1)S(1)} collective-permute-done((bf16[15,48,128]{2,1,0:T(8,128)(2,1)S(1)}, bf16[15,48,128]{2,1,0:T(8,128)(2,1)S(1)}, u32[]{:S(2)}, u32[]{:S(2)}) %collective-permute-start.9) | collective-permute-done | bytes 184352 | tf_op jit(solution)/shard_map/ppermute | solution.py:37
  27.2 3.4 %first_star.1.refs_13_.raw = f32[6,256,256]{2,1,0:T(8,128)S(1)} custom-call(bf16[15,48,128]{2,1,0:T(8,128)(2,1)S(1)} %collective-permute-done.6.refs_0_.refs_2_, bf16[15,48,128]{2,1,0:T(8,128)(2,1)S(1)} %collective-permute-done.7.refs_1_.refs_3_, bf16[15,48,128]{2,1,0:T(8,128)(2,1)S(1)} %get-tuple-element.22.refs_2_.refs_4_, ...), custom_call_target="tpu_custom_call" | custom-call | flops 10000000000 | bytes 4000000 | tf_op jit(solution)/shard_map/first_star/pallas_call | solution.py:230
  30.6 2.6 %second_star.1 = (f32[4,2,48,384]{3,2,1,0:T(8,128)S(1)}, bf16[4,2,48,384]{3,2,1,0:T(8,128)(2,1)S(1)}, bf16[6,1152,256]{2,1,0:T(8,128)(2,1)S(1)}) custom-call(bf16[15,48,128]{2,1,0:T(8,128)(2,1)S(1)} %collective-permute-done.2.refs_0_, bf16[15,48,128]{2,1,0:T(8,128)(2,1)S(1)} %collective-permute-done.5.refs_1_, ...), custom_call_target="tpu_custom_call" | custom-call | tf_op jit(solution)/shard_map/second_star/pallas_call | solution.py:248
  33.2 4.2 %collective-permute-start.14 = (bf16[4,2,48,384]{3,2,1,0:T(8,128)(2,1)S(1)}, bf16[4,2,48,384]{3,2,1,0:T(8,128)(2,1)S(1)}, u32[]{:S(2)}, u32[]{:S(2)}) collective-permute-start(bf16[4,2,48,384]{3,2,1,0:T(8,128)(2,1)S(1)} %get-tuple-element.32), channel_id=1, source_target_pairs={{0,1},{1,0},{2,3},{3,2},{4,5},{5,4},{6,7},{7,6},{8,9},{9,8},{10,11... | collective-permute-start | bytes 884744 | tf_op jit(solution)/shard_map/ppermute | solution.py:37
  37.4 1.0 %last_star.1 = (f32[4,2,48,384]{3,2,1,0:T(8,128)S(1)}, bf16[4,2,48,384]{3,2,1,0:T(8,128)(2,1)S(1)}, f32[48,768]{1,0:T(8,128)S(1)}) custom-call(bf16[6,1152,256]{2,1,0:T(8,128)(2,1)S(1)} %get-tuple-element.24.products, bf16[256,1152]{1,0:T(8,128)(2,1)S(1)} %weights.1.refs_10_.refs_12_, f32[6,256,256]{2,1,0:T(8,128)S(1)} %first_star.1.refs_13_.raw, ...), custom_call_target="tpu_custom_call" | custom-call | tf_op jit(solution)/shard_map/last_star/pallas_call | solution.py:260
  38.7 2.8 %collective-permute-start.15 = (bf16[2,48,384]{2,1,0:T(8,128)(2,1)S(1)}, bf16[2,48,384]{2,1,0:T(8,128)(2,1)S(1)}, u32[]{:S(2)}, u32[]{:S(2)}) collective-permute-start(bf16[2,48,384]{2,1,0:T(8,128)(2,1)S(1)} %get-tuple-element.34), channel_id=1, source_target_pairs={{0,4},{1,5},{2,6},{3,7},{4,0},{5,1},{6,2},{7,3},{8,12},{9,13},{10,... | collective-permute-start | bytes 221192 | tf_op jit(solution)/shard_map/ppermute | solution.py:37
  41.5 0.9 %collective-permute-start.16 = (bf16[2,48,384]{2,1,0:T(8,128)(2,1)S(1)}, bf16[2,48,384]{2,1,0:T(8,128)(2,1)S(1)}, u32[]{:S(2)}, u32[]{:S(2)}) collective-permute-start(bf16[2,48,384]{2,1,0:T(8,128)(2,1)S(1)} %get-tuple-element.35), channel_id=1, source_target_pairs={{0,6},{1,7},{2,0},{3,1},{4,2},{5,3},{6,4},{7,5},{8,14},{9,15},{10,... | collective-permute-start | bytes 221192 | tf_op jit(solution)/shard_map/ppermute | solution.py:37
  43.8 2.1 %collective-permute-start.12 = (bf16[2,48,384]{2,1,0:T(8,128)(2,1)S(1)}, bf16[2,48,384]{2,1,0:T(8,128)(2,1)S(1)}, u32[]{:S(2)}, u32[]{:S(2)}) collective-permute-start(bf16[2,48,384]{2,1,0:T(8,128)(2,1)S(1)} %get-tuple-element.29), channel_id=1, source_target_pairs={{0,6},{1,7},{2,0},{3,1},{4,2},{5,3},{6,4},{7,5},{8,14},{9,15},{10,... | collective-permute-start | bytes 221192 | tf_op jit(solution)/shard_map/ppermute | solution.py:37
  45.9 0.9 %collective-permute-done.17.one = bf16[2,48,384]{2,1,0:T(8,128)(2,1)S(1)} collective-permute-done((bf16[2,48,384]{2,1,0:T(8,128)(2,1)S(1)}, bf16[2,48,384]{2,1,0:T(8,128)(2,1)S(1)}, u32[]{:S(2)}, u32[]{:S(2)}) %collective-permute-start.17) | collective-permute-done | bytes 73760 | tf_op jit(solution)/shard_map/ppermute | solution.py:37
  46.8 3.0 %collective-permute-start.18 = (bf16[2,48,384]{2,1,0:T(8,128)(2,1)S(1)}, bf16[2,48,384]{2,1,0:T(8,128)(2,1)S(1)}, u32[]{:S(2)}, u32[]{:S(2)}) collective-permute-start(bf16[2,48,384]{2,1,0:T(8,128)(2,1)S(1)} %add_x.1), channel_id=1, source_target_pairs={{0,8},{1,9},{2,10},{3,11},{4,12},{5,13},{6,14},{7,15},{8,0},{9,1},... | collective-permute-start | bytes 221192 | tf_op jit(solution)/shard_map/ppermute | solution.py:37
  49.8 0.9 %collective-permute-done.13.one = bf16[2,48,384]{2,1,0:T(8,128)(2,1)S(1)} collective-permute-done((bf16[2,48,384]{2,1,0:T(8,128)(2,1)S(1)}, bf16[2,48,384]{2,1,0:T(8,128)(2,1)S(1)}, u32[]{:S(2)}, u32[]{:S(2)}) %collective-permute-start.13) | collective-permute-done | bytes 73760 | tf_op jit(solution)/shard_map/ppermute | solution.py:37
  50.7 0.9 %collective-permute-done.18.got = bf16[2,48,384]{2,1,0:T(8,128)(2,1)S(1)} collective-permute-done((bf16[2,48,384]{2,1,0:T(8,128)(2,1)S(1)}, bf16[2,48,384]{2,1,0:T(8,128)(2,1)S(1)}, u32[]{:S(2)}, u32[]{:S(2)}) %collective-permute-start.18) | collective-permute-done | bytes 73760 | tf_op jit(solution)/shard_map/ppermute | solution.py:37
  51.9 0.8 %collective-permute-start.19 = (f32[2,48,128]{2,1,0:T(8,128)S(1)}, f32[2,48,128]{2,1,0:T(8,128)S(1)}, u32[]{:S(2)}, u32[]{:S(2)}) collective-permute-start(f32[2,48,128]{2,1,0:T(8,128)S(1)} %get-tuple-element.37), channel_id=1, source_target_pairs={{0,224},{1,33},{2,226},{3,35},{4,228},{5,37},{6,230},{7,39},{8,232... | collective-permute-start | bytes 147464 | tf_op jit(solution)/shard_map/ppermute | solution.py:46
  52.7 6.0 %collective-permute-done.21.plain = f32[2,48,256]{2,1,0:T(8,128)S(1)} collective-permute-done((f32[2,48,256]{2,1,0:T(8,128)S(1)}, f32[2,48,256]{2,1,0:T(8,128)S(1)}, u32[]{:S(2)}, u32[]{:S(2)}) %collective-permute-start.21) | collective-permute-done | bytes 98336 | tf_op jit(solution)/shard_map/ppermute | solution.py:46
  58.8 2.4 %collective-permute-start.22 = (f32[48,256]{1,0:T(8,128)S(1)}, f32[48,256]{1,0:T(8,128)S(1)}, u32[]{:S(2)}, u32[]{:S(2)}) collective-permute-start(f32[48,256]{1,0:T(8,128)S(1)} %slice_bitcast_fusion), channel_id=1, source_target_pairs={{0,1},{1,0},{2,3},{3,2},{4,5},{5,4},{6,7},{7,6},{8,9},{9,8},{10,11... | collective-permute-start | bytes 147464 | tf_op jit(solution)/shard_map/ppermute | solution.py:37
  61.7 0.8 %collective-permute-done.20.mirror_other = f32[48,128]{1,0:T(8,128)S(1)} collective-permute-done((f32[48,128]{1,0:T(8,128)S(1)}, f32[48,128]{1,0:T(8,128)S(1)}, u32[]{:S(2)}, u32[]{:S(2)}) %collective-permute-start.20) | collective-permute-done | bytes 24608 | tf_op jit(solution)/shard_map/ppermute | solution.py:37
  62.6 1.1 %place.1 = (f32[1,48,768]{2,1,0:T(8,128)}, f32[1,48,768]{2,1,0:T(8,128)}) custom-call(f32[2,48,128]{2,1,0:T(8,128)S(1)} %collective-permute-done.19.mirror, f32[48,128]{1,0:T(8,128)S(1)} %collective-permute-done.20.mirror_other, f32[2,48,256]{2,1,0:T(8,128)S(1)} %collective-permute-done.21.plain, f32[48,256]{1,0:T(8,128)S(1)} %collective-permute-done.22.plain_other, ...), custom_call_target="tpu_custom_call" | custom-call | tf_op jit(solution)/shard_map/place/pallas_call | solution.py:376
  (42 shorter events, 7.5 us)
Async XLA Ops:
  1.7 9.8 %collective-permute-start = (bf16[15,48,128]{2,1,0:T(8,128)(2,1)S(1)}, bf16[15,48,128]{2,1,0:T(8,128)(2,1)S(1)}, u32[]{:S(2)}, u32[]{:S(2)}) collective-permute-start(bf16[15,48,128]{2,1,0:T(8,128)(2,1)S(1)} %get-tuple-element.22.refs_2_.refs_4_), channel_id=1, source_target_pairs={{0,224},{1,225},{2,226},{3,227},{4,228},{5,229},{6,230},{7,231},{8... | collective-permute-start | bytes 552968 | tf_op jit(solution)/shard_map/ppermute | solution.py:37
  8.2 7.3 %collective-permute-start.3 = (bf16[15,48,128]{2,1,0:T(8,128)(2,1)S(1)}, bf16[15,48,128]{2,1,0:T(8,128)(2,1)S(1)}, u32[]{:S(2)}, u32[]{:S(2)}) collective-permute-start(bf16[15,48,128]{2,1,0:T(8,128)(2,1)S(1)} %get-tuple-element.23.refs_3_.refs_5_), channel_id=1, source_target_pairs={{0,224},{1,225},{2,226},{3,227},{4,228},{5,229},{6,230},{7,231},{8... | collective-permute-start | bytes 552968 | tf_op jit(solution)/shard_map/ppermute | solution.py:37
  9.0 9.9 %collective-permute-start.6 = (bf16[15,48,128]{2,1,0:T(8,128)(2,1)S(1)}, bf16[15,48,128]{2,1,0:T(8,128)(2,1)S(1)}, u32[]{:S(2)}, u32[]{:S(2)}) collective-permute-start(bf16[15,48,128]{2,1,0:T(8,128)(2,1)S(1)} %get-tuple-element.22.refs_2_.refs_4_), channel_id=1, source_target_pairs={{0,32},{1,33},{2,34},{3,35},{4,36},{5,37},{6,38},{7,39},{8,40},{9,... | collective-permute-start | bytes 552968 | tf_op jit(solution)/shard_map/ppermute | solution.py:37
  9.7 9.3 %collective-permute-start.7 = (bf16[15,48,128]{2,1,0:T(8,128)(2,1)S(1)}, bf16[15,48,128]{2,1,0:T(8,128)(2,1)S(1)}, u32[]{:S(2)}, u32[]{:S(2)}) collective-permute-start(bf16[15,48,128]{2,1,0:T(8,128)(2,1)S(1)} %get-tuple-element.23.refs_3_.refs_5_), channel_id=1, source_target_pairs={{0,32},{1,33},{2,34},{3,35},{4,36},{5,37},{6,38},{7,39},{8,40},{9,... | collective-permute-start | bytes 552968 | tf_op jit(solution)/shard_map/ppermute | solution.py:37
  11.5 8.8 %collective-permute-start.1 = (bf16[15,48,128]{2,1,0:T(8,128)(2,1)S(1)}, bf16[15,48,128]{2,1,0:T(8,128)(2,1)S(1)}, u32[]{:S(2)}, u32[]{:S(2)}) collective-permute-start(bf16[15,48,128]{2,1,0:T(8,128)(2,1)S(1)} %collective-permute-done.refs_4_.refs_6_), channel_id=1, source_target_pairs={{0,224},{1,225},{2,226},{3,227},{4,228},{5,229},{6,230},{7,231},{8... | collective-permute-start | bytes 552968 | tf_op jit(solution)/shard_map/ppermute | solution.py:37
  15.5 7.1 %collective-permute-start.4 = (bf16[15,48,128]{2,1,0:T(8,128)(2,1)S(1)}, bf16[15,48,128]{2,1,0:T(8,128)(2,1)S(1)}, u32[]{:S(2)}, u32[]{:S(2)}) collective-permute-start(bf16[15,48,128]{2,1,0:T(8,128)(2,1)S(1)} %collective-permute-done.3.refs_5_.refs_7_), channel_id=1, source_target_pairs={{0,224},{1,225},{2,226},{3,227},{4,228},{5,229},{6,230},{7,231},{8... | collective-permute-start | bytes 552968 | tf_op jit(solution)/shard_map/ppermute | solution.py:37
  18.9 5.6 %collective-permute-start.8 = (bf16[15,48,128]{2,1,0:T(8,128)(2,1)S(1)}, bf16[15,48,128]{2,1,0:T(8,128)(2,1)S(1)}, u32[]{:S(2)}, u32[]{:S(2)}) collective-permute-start(bf16[15,48,128]{2,1,0:T(8,128)(2,1)S(1)} %collective-permute-done.6.refs_0_.refs_2_), channel_id=1, source_target_pairs={{0,32},{1,33},{2,34},{3,35},{4,36},{5,37},{6,38},{7,39},{8,40},{9,... | collective-permute-start | bytes 552968 | tf_op jit(solution)/shard_map/ppermute | solution.py:37
  19.0 8.2 %collective-permute-start.9 = (bf16[15,48,128]{2,1,0:T(8,128)(2,1)S(1)}, bf16[15,48,128]{2,1,0:T(8,128)(2,1)S(1)}, u32[]{:S(2)}, u32[]{:S(2)}) collective-permute-start(bf16[15,48,128]{2,1,0:T(8,128)(2,1)S(1)} %collective-permute-done.7.refs_1_.refs_3_), channel_id=1, source_target_pairs={{0,32},{1,33},{2,34},{3,35},{4,36},{5,37},{6,38},{7,39},{8,40},{9,... | collective-permute-start | bytes 552968 | tf_op jit(solution)/shard_map/ppermute | solution.py:37
  20.3 10.3 %collective-permute-start.2 = (bf16[15,48,128]{2,1,0:T(8,128)(2,1)S(1)}, bf16[15,48,128]{2,1,0:T(8,128)(2,1)S(1)}, u32[]{:S(2)}, u32[]{:S(2)}) collective-permute-start(bf16[15,48,128]{2,1,0:T(8,128)(2,1)S(1)} %collective-permute-done.1.refs_8_.refs_10_), channel_id=1, source_target_pairs={{0,16},{1,17},{2,18},{3,19},{4,20},{5,21},{6,22},{7,23},{8,24},{9,... | collective-permute-start | bytes 552968 | tf_op jit(solution)/shard_map/ppermute | solution.py:37
  22.6 8.1 %collective-permute-start.5 = (bf16[15,48,128]{2,1,0:T(8,128)(2,1)S(1)}, bf16[15,48,128]{2,1,0:T(8,128)(2,1)S(1)}, u32[]{:S(2)}, u32[]{:S(2)}) collective-permute-start(bf16[15,48,128]{2,1,0:T(8,128)(2,1)S(1)} %collective-permute-done.4.refs_9_.refs_11_), channel_id=1, source_target_pairs={{0,16},{1,17},{2,18},{3,19},{4,20},{5,21},{6,22},{7,23},{8,24},{9,... | collective-permute-start | bytes 552968 | tf_op jit(solution)/shard_map/ppermute | solution.py:37
  30.6 6.8 %copy-start.2 = (f32[768]{0:T(1024)S(1)}, f32[768]{0:T(1024)}, u32[]{:S(2)}) copy-start(f32[768]{0:T(1024)} %vir_energy.1) | copy-start | bytes 9220
  33.2 5.4 %collective-permute-start.14 = (bf16[4,2,48,384]{3,2,1,0:T(8,128)(2,1)S(1)}, bf16[4,2,48,384]{3,2,1,0:T(8,128)(2,1)S(1)}, u32[]{:S(2)}, u32[]{:S(2)}) collective-permute-start(bf16[4,2,48,384]{3,2,1,0:T(8,128)(2,1)S(1)} %get-tuple-element.32), channel_id=1, source_target_pairs={{0,1},{1,0},{2,3},{3,2},{4,5},{5,4},{6,7},{7,6},{8,9},{9,8},{10,11... | collective-permute-start | bytes 884744 | tf_op jit(solution)/shard_map/ppermute | solution.py:37
  38.4 4.6 %collective-permute-start.10 = (bf16[4,2,48,384]{3,2,1,0:T(8,128)(2,1)S(1)}, bf16[4,2,48,384]{3,2,1,0:T(8,128)(2,1)S(1)}, u32[]{:S(2)}, u32[]{:S(2)}) collective-permute-start(bf16[4,2,48,384]{3,2,1,0:T(8,128)(2,1)S(1)} %get-tuple-element.26), channel_id=1, source_target_pairs={{0,1},{1,0},{2,3},{3,2},{4,5},{5,4},{6,7},{7,6},{8,9},{9,8},{10,11... | collective-permute-start | bytes 884744 | tf_op jit(solution)/shard_map/ppermute | solution.py:37
  38.7 7.2 %collective-permute-start.15 = (bf16[2,48,384]{2,1,0:T(8,128)(2,1)S(1)}, bf16[2,48,384]{2,1,0:T(8,128)(2,1)S(1)}, u32[]{:S(2)}, u32[]{:S(2)}) collective-permute-start(bf16[2,48,384]{2,1,0:T(8,128)(2,1)S(1)} %get-tuple-element.34), channel_id=1, source_target_pairs={{0,4},{1,5},{2,6},{3,7},{4,0},{5,1},{6,2},{7,3},{8,12},{9,13},{10,... | collective-permute-start | bytes 221192 | tf_op jit(solution)/shard_map/ppermute | solution.py:37
  41.5 4.3 %collective-permute-start.16 = (bf16[2,48,384]{2,1,0:T(8,128)(2,1)S(1)}, bf16[2,48,384]{2,1,0:T(8,128)(2,1)S(1)}, u32[]{:S(2)}, u32[]{:S(2)}) collective-permute-start(bf16[2,48,384]{2,1,0:T(8,128)(2,1)S(1)} %get-tuple-element.35), channel_id=1, source_target_pairs={{0,6},{1,7},{2,0},{3,1},{4,2},{5,3},{6,4},{7,5},{8,14},{9,15},{10,... | collective-permute-start | bytes 221192 | tf_op jit(solution)/shard_map/ppermute | solution.py:37
  42.4 4.4 %collective-permute-start.17 = (bf16[2,48,384]{2,1,0:T(8,128)(2,1)S(1)}, bf16[2,48,384]{2,1,0:T(8,128)(2,1)S(1)}, u32[]{:S(2)}, u32[]{:S(2)}) collective-permute-start(bf16[2,48,384]{2,1,0:T(8,128)(2,1)S(1)} %get-tuple-element.36), channel_id=1, source_target_pairs={{0,2},{1,3},{2,4},{3,5},{4,6},{5,7},{6,0},{7,1},{8,10},{9,11},{10,... | collective-permute-start | bytes 221192 | tf_op jit(solution)/shard_map/ppermute | solution.py:37
  43.1 6.8 %collective-permute-start.11 = (bf16[2,48,384]{2,1,0:T(8,128)(2,1)S(1)}, bf16[2,48,384]{2,1,0:T(8,128)(2,1)S(1)}, u32[]{:S(2)}, u32[]{:S(2)}) collective-permute-start(bf16[2,48,384]{2,1,0:T(8,128)(2,1)S(1)} %get-tuple-element.28), channel_id=1, source_target_pairs={{0,4},{1,5},{2,6},{3,7},{4,0},{5,1},{6,2},{7,3},{8,12},{9,13},{10,... | collective-permute-start | bytes 221192 | tf_op jit(solution)/shard_map/ppermute | solution.py:37
  43.8 6.1 %collective-permute-start.12 = (bf16[2,48,384]{2,1,0:T(8,128)(2,1)S(1)}, bf16[2,48,384]{2,1,0:T(8,128)(2,1)S(1)}, u32[]{:S(2)}, u32[]{:S(2)}) collective-permute-start(bf16[2,48,384]{2,1,0:T(8,128)(2,1)S(1)} %get-tuple-element.29), channel_id=1, source_target_pairs={{0,6},{1,7},{2,0},{3,1},{4,2},{5,3},{6,4},{7,5},{8,14},{9,15},{10,... | collective-permute-start | bytes 221192 | tf_op jit(solution)/shard_map/ppermute | solution.py:37
  45.8 4.8 %collective-permute-start.13 = (bf16[2,48,384]{2,1,0:T(8,128)(2,1)S(1)}, bf16[2,48,384]{2,1,0:T(8,128)(2,1)S(1)}, u32[]{:S(2)}, u32[]{:S(2)}) collective-permute-start(bf16[2,48,384]{2,1,0:T(8,128)(2,1)S(1)} %get-tuple-element.30), channel_id=1, source_target_pairs={{0,2},{1,3},{2,4},{3,5},{4,6},{5,7},{6,0},{7,1},{8,10},{9,11},{10,... | collective-permute-start | bytes 221192 | tf_op jit(solution)/shard_map/ppermute | solution.py:37
  46.8 4.8 %collective-permute-start.18 = (bf16[2,48,384]{2,1,0:T(8,128)(2,1)S(1)}, bf16[2,48,384]{2,1,0:T(8,128)(2,1)S(1)}, u32[]{:S(2)}, u32[]{:S(2)}) collective-permute-start(bf16[2,48,384]{2,1,0:T(8,128)(2,1)S(1)} %add_x.1), channel_id=1, source_target_pairs={{0,8},{1,9},{2,10},{3,11},{4,12},{5,13},{6,14},{7,15},{8,0},{9,1},... | collective-permute-start | bytes 221192 | tf_op jit(solution)/shard_map/ppermute | solution.py:37
  51.8 7.0 %collective-permute-start.21 = (f32[2,48,256]{2,1,0:T(8,128)S(1)}, f32[2,48,256]{2,1,0:T(8,128)S(1)}, u32[]{:S(2)}, u32[]{:S(2)}) collective-permute-start(f32[2,48,256]{2,1,0:T(8,128)S(1)} %get-tuple-element.38), channel_id=1, source_target_pairs={{0,192},{1,81},{2,194},{3,83},{4,196},{5,85},{6,198},{7,87},{8,200... | collective-permute-start | bytes 294920 | tf_op jit(solution)/shard_map/ppermute | solution.py:46
  51.9 9.3 %collective-permute-start.19 = (f32[2,48,128]{2,1,0:T(8,128)S(1)}, f32[2,48,128]{2,1,0:T(8,128)S(1)}, u32[]{:S(2)}, u32[]{:S(2)}) collective-permute-start(f32[2,48,128]{2,1,0:T(8,128)S(1)} %get-tuple-element.37), channel_id=1, source_target_pairs={{0,224},{1,33},{2,226},{3,35},{4,228},{5,37},{6,230},{7,39},{8,232... | collective-permute-start | bytes 147464 | tf_op jit(solution)/shard_map/ppermute | solution.py:46
  58.8 3.8 %collective-permute-start.22 = (f32[48,256]{1,0:T(8,128)S(1)}, f32[48,256]{1,0:T(8,128)S(1)}, u32[]{:S(2)}, u32[]{:S(2)}) collective-permute-start(f32[48,256]{1,0:T(8,128)S(1)} %slice_bitcast_fusion), channel_id=1, source_target_pairs={{0,1},{1,0},{2,3},{3,2},{4,5},{5,4},{6,7},{7,6},{8,9},{9,8},{10,11... | collective-permute-start | bytes 147464 | tf_op jit(solution)/shard_map/ppermute | solution.py:37
  61.2 1.3 %collective-permute-start.20 = (f32[48,128]{1,0:T(8,128)S(1)}, f32[48,128]{1,0:T(8,128)S(1)}, u32[]{:S(2)}, u32[]{:S(2)}) collective-permute-start(f32[48,128]{1,0:T(8,128)S(1)} %slice_bitcast_fusion.1), channel_id=1, source_target_pairs={{0,1},{1,0},{2,3},{3,2},{4,5},{5,4},{6,7},{7,6},{8,9},{9,8},{10,11... | collective-permute-start | bytes 73736 | tf_op jit(solution)/shard_map/ppermute | solution.py:37
  (3 other events, 8.6 us)
